TPU v7x, 32 devices: a whole 2x2x4 slice. The times are simulated.
32 devices in a mesh: seq: 8 (over z, core), req: 4 (over y, x).
Axes of the slice: x: 2, y: 2, z: 4, core: 2. Of those that a mesh axis runs over, the one named last changes fastest.
Arguments:
- token_ids: int32 [32, 4], replicated, may hold values from 0 to 64127
- embed_table: bfloat16 [64128, 2048], P('req', 'seq'), may hold values from -9 to 9
- cache_len: int32 [32], P('req'), may hold values from 1 to 2048, as said below
- range_start: int32 [32], P('req'), may hold values from 0 to 1023, as said below
- positions: int32 [32], P('req'), may hold values from 0 to 131071
- cached_key_rows: bfloat16 [32, 2048, 512], P('req', 'seq'), may hold values from -220 to 220
- cached_value_rows: bfloat16 [32, 2048, 512], P('req', 'seq'), may hold values from -6 to 6
- attn_gain: bfloat16 [2048], P('seq'), may hold values from 0.099609375 to 1.8984375
- mlp_gain: bfloat16 [2048], P('seq'), may hold values from 0.099609375 to 1.8984375
- w_qkv: bfloat16 [2048, 3072], P('seq'), may hold values from -0.125 to 0.125
- w_out: bfloat16 [2048, 2048], P(None, 'seq'), may hold values from -0.125 to 0.125
- w_gate: bfloat16 [2048, 8192], P('seq', 'req'), may hold values from -0.125 to 0.125
- w_up: bfloat16 [2048, 8192], P('seq', 'req'), may hold values from -0.125 to 0.125
- w_down: bfloat16 [8192, 2048], P('req', 'seq'), may hold values from -0.0625 to 0.0625
Outputs:
- layer_out: bfloat16 [32, 4, 2048], P('req', None, 'seq')
- new_keys: bfloat16 [32, 4, 512], P('req')
- new_values: bfloat16 [32, 4, 512], P('req')
Inputs may be any that keep to these rules, and one draw needn't show every extreme that they name: `cache_len`: every request has at least one cached position and some request fills all 2048 positions. A request's range_start is at most (cache_len - 1) // 2 of the same request.
All inputs are finite; a program needn't handle non-finite values.
Results may differ from a plain program's by a relative error of at most 0.02.
Values may be sent and summed in bfloat16 or wider, within the bound.
No kernel may reach another device: no remote copies, remote signals or barrier semaphores. Data moves between devices by JAX's collectives and lax.ppermute only.
A program may use at most 64 MiB of HBM per device.

v0:
```python
import math

import jax
import jax.numpy as jnp
from jax import lax
from jax.sharding import PartitionSpec as P

D = 2048
QUERY_HEADS = 32
KEY_VALUE_HEADS = 8
HEAD_SIZE = 64


EPSILON = 1e-05
ROPE_BASE = 500000.0


def rotary_embedding(vectors, angle_positions):
    half_size = vectors.shape[-1] // 2
    freqs = ROPE_BASE ** (-2.0 * jnp.arange(half_size, dtype=jnp.float32) / vectors.shape[-1])
    angles = angle_positions[:, None] * freqs[None, :]
    cosine = jnp.cos(angles)[:, None, :]
    sine = jnp.sin(angles)[:, None, :]
    first_half = vectors[..., :half_size]
    second_half = vectors[..., half_size:]
    return jnp.concatenate(
        [first_half * cosine - second_half * sine, second_half * cosine + first_half * sine],
        axis=-1,
    )


def norm_sum(values, site_tag):
    if site_tag == "attention":
        return lax.psum(jnp.sum(values * values, axis=-1), "seq")
    return lax.psum(jnp.sum(values * values, axis=-1), "seq")


def apply_norm(values, squares, gain):
    mean_square = (squares / D)[:, None]
    return (values * lax.rsqrt(mean_square + EPSILON) * gain.astype(jnp.float32)).astype(
        jnp.bfloat16
    )


def shards(
    token_ids,
    embed_table,
    cache_len,
    range_start,
    positions,
    cached_key_rows,
    cached_value_rows,
    attn_gain,
    mlp_gain,
    w_qkv,
    w_out,
    w_gate,
    w_up,
    w_down,
):
    requests_per_shard = cache_len.shape[0]
    context_per_shard = cached_key_rows.shape[1]
    key_value_width = cached_key_rows.shape[2]
    steps = token_ids.shape[1]
    vocab_dev = embed_table.shape[0]
    feat_dev = embed_table.shape[1]
    head_groups = QUERY_HEADS // KEY_VALUE_HEADS
    scale = 1.0 / math.sqrt(HEAD_SIZE)
    seq_index = lax.axis_index("seq")
    req_index = lax.axis_index("req")
    flat_ids = token_ids.reshape(-1)
    vocab_start = req_index * vocab_dev
    vocab_rows = jnp.arange(vocab_dev, dtype=jnp.int32)
    onehot = (flat_ids[:, None] - vocab_start == vocab_rows[None, :]).astype(jnp.bfloat16)
    embedded = lax.psum_scatter(
        jnp.dot(onehot, embed_table, preferred_element_type=jnp.float32).astype(jnp.bfloat16),
        "req",
        scatter_dimension=0,
        tiled=True,
    ).astype(jnp.float32)
    embedded = embedded.astype(jnp.bfloat16).reshape(requests_per_shard, steps, feat_dev)
    place = jnp.arange(context_per_shard, dtype=jnp.int32) + seq_index * context_per_shard
    visible = (place[None, :] >= range_start[:, None]) & (place[None, :] < cache_len[:, None])
    visible_wide = visible[:, None, None, :]
    key_head_rows = cached_key_rows.reshape(
        requests_per_shard, context_per_shard, KEY_VALUE_HEADS, HEAD_SIZE
    )
    value_head_rows = cached_value_rows.reshape(
        requests_per_shard, context_per_shard, KEY_VALUE_HEADS, HEAD_SIZE
    )
    w_pair = jnp.concatenate([w_gate, w_up], axis=1)
    unit_dev = w_gate.shape[1]
    key_collection = []
    value_collection = []
    layer_rows = []
    for decode_layer_step in range(steps):
        resid_in = embedded[:, decode_layer_step].astype(jnp.float32)
        normed = apply_norm(resid_in, norm_sum(resid_in, "attention"), attn_gain)
        combined_parts = lax.psum(jnp.dot(normed, w_qkv, preferred_element_type=jnp.float32), "seq")
        angle_positions = (positions + decode_layer_step).astype(jnp.float32)
        query_rows = rotary_embedding(
            combined_parts[:, : QUERY_HEADS * HEAD_SIZE].reshape(
                requests_per_shard, QUERY_HEADS, HEAD_SIZE
            ),
            angle_positions,
        ).astype(jnp.bfloat16)
        newest_key_seed = rotary_embedding(
            combined_parts[
                :, QUERY_HEADS * HEAD_SIZE : QUERY_HEADS * HEAD_SIZE + key_value_width
            ].reshape(requests_per_shard, KEY_VALUE_HEADS, HEAD_SIZE),
            angle_positions,
        )
        key_collection.append(
            newest_key_seed.reshape(requests_per_shard, key_value_width).astype(jnp.bfloat16)
        )
        value_collection.append(
            combined_parts[:, QUERY_HEADS * HEAD_SIZE + key_value_width :].astype(jnp.bfloat16)
        )
        newest_key_rows = jnp.stack(key_collection, axis=1).reshape(
            requests_per_shard, decode_layer_step + 1, KEY_VALUE_HEADS, HEAD_SIZE
        )
        newest_value_rows = jnp.stack(value_collection, axis=1).reshape(
            requests_per_shard, decode_layer_step + 1, KEY_VALUE_HEADS, HEAD_SIZE
        )
        query_head_groups = query_rows.reshape(
            requests_per_shard, KEY_VALUE_HEADS, head_groups, HEAD_SIZE
        )
        scores = (
            jnp.einsum(
                "rhgd,rphd->rhgp",
                query_head_groups,
                key_head_rows,
                preferred_element_type=jnp.float32,
            )
            * scale
        )
        scores = jnp.where(visible_wide, scores, -1e30)
        fresh_scores = (
            jnp.einsum(
                "rhgd,rjhd->rhgj",
                query_head_groups,
                newest_key_rows,
                preferred_element_type=jnp.float32,
            )
            * scale
        )
        local_top = jnp.maximum(jnp.max(scores, axis=-1), jnp.max(fresh_scores, axis=-1))
        top = lax.pmax(local_top, "seq")
        expo = jnp.where(visible_wide, jnp.exp(scores - top[..., None]), 0.0)
        fresh_expo = jnp.exp(fresh_scores - top[..., None])
        local_total = jnp.sum(expo, axis=-1)
        fresh_total = jnp.sum(fresh_expo, axis=-1)
        local_summed = jnp.einsum(
            "rhgp,rphd->rhgd",
            expo.astype(jnp.bfloat16),
            value_head_rows,
            preferred_element_type=jnp.float32,
        )
        fresh_summed = jnp.einsum(
            "rhgj,rjhd->rhgd",
            fresh_expo.astype(jnp.bfloat16),
            newest_value_rows,
            preferred_element_type=jnp.float32,
        )
        total_all, summed_all = (
            lax.psum(local_total.astype(jnp.bfloat16), "seq").astype(jnp.float32),
            lax.psum(local_summed.astype(jnp.bfloat16), "seq").astype(jnp.float32),
        )
        attended = (summed_all + fresh_summed) / (total_all + fresh_total)[..., None]
        attended = attended.astype(jnp.bfloat16).reshape(
            requests_per_shard, QUERY_HEADS * HEAD_SIZE
        )
        resid = (resid_in + jnp.dot(attended, w_out, preferred_element_type=jnp.float32)).astype(
            jnp.bfloat16
        )
        resid_f = resid.astype(jnp.float32)
        mlp_in = apply_norm(resid_f, norm_sum(resid_f, "feedforward"), mlp_gain)
        unit_terms = jnp.dot(
            lax.all_gather(mlp_in, "req", axis=0, tiled=True),
            w_pair,
            preferred_element_type=jnp.float32,
        )
        units = lax.psum(unit_terms.astype(jnp.bfloat16), "seq").astype(jnp.float32)
        hidden = (jax.nn.silu(units[:, :unit_dev]) * units[:, unit_dev:]).astype(jnp.bfloat16)
        mlp_part = lax.psum_scatter(
            jnp.dot(hidden, w_down, preferred_element_type=jnp.float32).astype(jnp.bfloat16),
            "req",
            scatter_dimension=0,
            tiled=True,
        ).astype(jnp.float32)
        layer_rows.append((resid_f + mlp_part).astype(jnp.bfloat16))
    return (
        jnp.stack(layer_rows, axis=1),
        jnp.stack(key_collection, axis=1),
        jnp.stack(value_collection, axis=1),
    )


def solution(mesh):
    in_specs = (
        P(),
        P("req", "seq"),
        P("req"),
        P("req"),
        P("req"),
        P("req", "seq", None),
        P("req", "seq", None),
        P("seq"),
        P("seq"),
        P("seq", None),
        P(None, "seq"),
        P("seq", "req"),
        P("seq", "req"),
        P("req", "seq"),
    )
    out_specs = (P("req", None, "seq"), P("req", None, None), P("req", None, None))
    return jax.shard_map(shards, mesh=mesh, in_specs=in_specs, out_specs=out_specs, check_vma=False)
```

profile of v0, /device:TPU:0, one launch (start us, length us, event | category | flops | bytes accessed | tf_op | source)
XLA Modules:
  0.0 407.0 jit_solution(14527858061738793326)
XLA Ops:
  7.2 0.8 broadcast_subtract_fusion
  8.2 5.3 %fusion.11 = bf16[128,256]{1,0:T(8,128)(2,1)} fusion(bf16[16032,256]{1,0:T(8,128)(2,1)} %param.15, s32[128]{0:T(128)S(1)} %sub.100), kind=kOutput, calls=%fused_computation.25 | convolution fusion | flops 1052758016 | bytes 8274432 | tf_op jit(solution)/shard_map/dot_general | solution.py:76
  13.7 1.0 constant_dynamic-update-slice_fusion.1
  15.3 1.1 constant_dynamic-update-slice_fusion
  16.5 3.9 copy.113
  20.5 3.9 copy.114
  25.7 14.5 %reduce-scatter.2.cloned.1.call-done = bf16[32,256]{1,0:T(8,128)(2,1)} async-done(((bf16[128,256]{1,0:T(8,128)(2,1)}), bf16[32,256]{1,0:T(8,128)(2,1)}) %reduce-scatter.2.cloned.1.call-update) | async-done | bytes 16400 | tf_op jit(solution)/shard_map/reduce_scatter | solution.py:75
  40.1 0.7 reshape.559
  41.2 15.9 %all-reduce.5 = (f32[8]{0:T(128)S(1)}, f32[8]{0:T(128)S(1)}, f32[8]{0:T(128)S(1)}, f32[8]{0:T(128)S(1)}) all-reduce(f32[8]{0:T(128)S(1)} %get-tuple-element.117, f32[8]{0:T(128)S(1)} %get-tuple-element.120, f32[8]{0:T(128)S(1)} %get-tuple-element.119, f32[8]{0:T(128)S(1)} %get-tuple-element.118), channel_id=1, replica_groups=mesh['seq'=8,'req'=4] {'seq'}, use_global_device_ids=true, to_apply=%region_2.0 | all-reduce | flops 32 | bytes 256 | tf_op jit(solution)/shard_map/psum | solution.py:34
  57.1 1.0 fusion.136
  58.1 1.0 fusion.134
  59.1 1.0 fusion.132
  60.1 1.0 fusion.138
  61.3 53.2 %all-reduce.16.cloned.1.call-done = (f32[8,3072]{1,0:T(8,128)}, f32[8,3072]{1,0:T(8,128)}, f32[8,3072]{1,0:T(8,128)}, f32[8,3072]{1,0:T(8,128)}) async-done(((f32[8,3072]{1,0:T(8,128)}, f32[8,3072]{1,0:T(8,128)}, f32[8,3072]{1,0:T(8,128)}, f32[8,3072]{1,0:T(8,128)}), (f32[8,3072]{1,0:T(8,128)}, f32[8,3072]{1,0:T(8,128)}, f32[8,3072]{1,0:T(8,128)}, f32[8,3072]{1,0:T(8,128)})) %all-reduce.16.cloned.1.call-update) | async-done | bytes 393232 | tf_op jit(solution)/shard_map/psum | solution.py:99
  114.5 0.7 slice.267
  115.2 1.3 slice_bitcast_fusion
  116.5 1.3 slice_bitcast_fusion.3
  117.8 0.7 slice.264
  118.5 1.3 slice_bitcast_fusion.2
  119.8 1.3 slice.265
  121.2 1.3 slice_bitcast_fusion.1
  122.5 0.7 slice.266
  123.2 0.7 slice.168
  123.9 0.8 slice.165
  124.7 0.7 slice.198
  125.5 0.8 slice.195
  126.3 0.7 slice.188
  127.0 0.8 slice.185
  127.9 0.7 slice.178
  128.6 0.8 slice.175
  132.9 2.3 fusion.166
  138.9 27.5 %all-reduce.7 = (f32[8,8,4]{2,1,0:T(8,128)S(1)}, f32[8,8,4]{2,1,0:T(8,128)S(1)}, f32[8,8,4]{2,1,0:T(8,128)S(1)}, f32[8,8,4]{2,1,0:T(8,128)S(1)}) all-reduce(f32[8,8,4]{2,1,0:T(8,128)S(1)} %max.23, f32[8,8,4]{2,1,0:T(8,128)S(1)} %multiply_maximum_fusion, f32[8,8,4]{2,1,0:T(8,128)S(1)} %max.21, ...), channel_id=1, replica_groups=mesh['seq'=8,'req'=4] {'seq'}, use_global_device_ids=true, to_apply=%region_46.47 | all-reduce | flops 1024 | bytes 8192 | tf_op jit(solution)/shard_map/pmax | solution.py:148
  166.4 3.1 convolution_convert_fusion.4
  169.5 1.3 convolution_convert_fusion.5
  170.8 1.3 convolution_convert_fusion.6
  172.1 1.4 fusion.25
  173.5 1.3 convolution_convert_fusion.7
  175.1 0.7 stack.102
  176.2 54.4 %all-reduce.18.cloned.1.call-done = (bf16[8,8,4,64]{3,2,1,0:T(4,128)(2,1)}, bf16[8,8,4]{2,1,0:T(8,128)(2,1)}, bf16[8,8,4,64]{3,2,1,0:T(4,128)(2,1)}, bf16[8,8,4]...) async-done(((bf16[8,8,4,64]{3,2,1,0:T(4,128)(2,1)}, ...) | async-done | bytes 133136 | tf_op jit(solution)/shard_map/psum | solution.py:167
  230.7 0.7 convert_add_fusion.2
  231.4 1.1 fusion.12
  232.7 0.7 convert_add_fusion.1
  233.4 1.2 fusion.10
  237.2 13.6 %all-reduce.4 = (f32[8]{0:T(128)S(1)}, f32[8]{0:T(128)S(1)}, f32[8]{0:T(128)S(1)}, f32[8]{0:T(128)S(1)}) all-reduce(f32[8]{0:T(128)S(1)} %get-tuple-element.109, f32[8]{0:T(128)S(1)} %get-tuple-element.111, f32[8]{0:T(128)S(1)} %get-tuple-element.113, f32[8]{0:T(128)S(1)} %get-tuple-element.115), channel_id=1, replica_groups=mesh['seq'=8,'req'=4] {'seq'}, use_global_device_ids=true, to_apply=%region_52.53 | all-reduce | flops 32 | bytes 256 | tf_op jit(solution)/shard_map/psum | solution.py:35
  250.9 8.1 %all_gather.12 = bf16[32,256]{1,0:T(8,128)(2,1)S(1)} all-gather(bf16[8,256]{1,0:T(8,128)(2,1)S(1)} %get-tuple-element.73), channel_id=1, replica_groups=mesh['seq'=8,'req'=4] {'req'}, dimensions={0}, use_global_device_ids=true | all-gather | bytes 20480 | tf_op jit(solution)/shard_map/all_gather | solution.py:179
  259.0 8.1 %all_gather.13 = bf16[32,256]{1,0:T(8,128)(2,1)S(1)} all-gather(bf16[8,256]{1,0:T(8,128)(2,1)S(1)} %get-tuple-element.74), channel_id=1, replica_groups=mesh['seq'=8,'req'=4] {'req'}, dimensions={0}, use_global_device_ids=true | all-gather | bytes 20480 | tf_op jit(solution)/shard_map/all_gather | solution.py:179
  267.1 7.2 %all_gather.14 = bf16[32,256]{1,0:T(8,128)(2,1)S(1)} all-gather(bf16[8,256]{1,0:T(8,128)(2,1)S(1)} %get-tuple-element.75), channel_id=1, replica_groups=mesh['seq'=8,'req'=4] {'req'}, dimensions={0}, use_global_device_ids=true | all-gather | bytes 20480 | tf_op jit(solution)/shard_map/all_gather | solution.py:179
  274.3 8.1 %all_gather.15 = bf16[32,256]{1,0:T(8,128)(2,1)S(1)} all-gather(bf16[8,256]{1,0:T(8,128)(2,1)S(1)} %get-tuple-element.76), channel_id=1, replica_groups=mesh['seq'=8,'req'=4] {'req'}, dimensions={0}, use_global_device_ids=true | all-gather | bytes 20480 | tf_op jit(solution)/shard_map/all_gather | solution.py:179
  282.4 2.8 convolution_convert_fusion
  285.2 2.8 convolution_convert_fusion.1
  287.9 2.8 convolution_convert_fusion.2
  290.7 2.8 convolution_convert_fusion.3
  295.0 55.2 %all-reduce.20.cloned.1.call-done = (bf16[32,4096]{1,0:T(8,128)(2,1)}, bf16[32,4096]{1,0:T(8,128)(2,1)}, bf16[32,4096]{1,0:T(8,128)(2,1)}, bf16[32,4096]{1,0:T(8,128)(2,1)}) async-done(((bf16[32,4096]{1,0:T(8,128)(2,1)}, bf16[32,4096]{1,0:T(8,128)(2,1)}, bf16[32,4096]{1,0:T(8,128)(2,1)}, bf16[32,4096]{1,0:T(8,128)(2,1)}), (bf16[32,4096]{1,0:T(8,128)(2,1)}, bf16[32,4096]{1,0:T(8,128)(2,1)}, ...) | async-done | bytes 1048592 | tf_op jit(solution)/shard_map/psum | solution.py:183
  350.2 1.0 convert_element_type.431
  351.2 1.0 convert_element_type.411
  352.2 0.9 convolution_convert_fusion.8
  353.1 0.9 convolution_convert_fusion.9
  354.0 0.9 convolution_convert_fusion.10
  355.0 0.9 convolution_convert_fusion.11
  355.9 0.7 pad_maximum_fusion.6
  356.6 40.5 %all-reduce.22.cloned.1.call-done = (bf16[32,256]{1,0:T(8,128)(2,1)}, bf16[32,256]{1,0:T(8,128)(2,1)}, bf16[32,256]{1,0:T(8,128)(2,1)}, bf16[32,256]{1,0:T(8,128)(2,1)}) async-done(((bf16[32,256]{1,0:T(8,128)(2,1)}, bf16[32,256]{1,0:T(8,128)(2,1)}, bf16[32,256]{1,0:T(8,128)(2,1)}, bf16[32,256]{1,0:T(8,128)(2,1)}), (bf16[32,256]{1,0:T(8,128)(2,1)}, bf16[32,256]{1,0:T(8,128)(2,1)}, bf16[32,256]{1,0:T(8,128)(2,1)}, ...) | async-done | bytes 65552
  397.1 0.7 fusion.128
  398.5 0.7 fusion.131
  399.1 0.7 fusion.130
  (172 shorter events, 15.1 us)
Async XLA Ops:
  7.2 50.0 %copy-start = (bf16[256,3072]{1,0:T(8,128)(2,1)S(1)}, bf16[256,3072]{1,0:T(8,128)(2,1)}, u32[]{:S(2)}) copy-start(bf16[256,3072]{1,0:T(8,128)(2,1)} %param.23) | copy-start | bytes 4718596
  7.2 33.0 %reduce-scatter.2.cloned.1.call-start = ((), (), s32[]{:S(2)}) async-start(), calls=%async_computation.1 | async-start | bytes 81920 | tf_op jit(solution)/shard_map/reduce_scatter | solution.py:75
  8.2 5.5 %copy-start.27 = (s32[8]{0:T(128)S(1)}, s32[8]{0:T(128)}, u32[]{:S(2)}) copy-start(s32[8]{0:T(128)} %param.18) | copy-start | bytes 100
  8.2 5.5 %copy-start.4 = (bf16[256,2048]{1,0:T(8,128)(2,1)S(1)}, bf16[256,2048]{1,0:T(8,128)(2,1)}, u32[]{:S(2)}) copy-start(bf16[256,2048]{1,0:T(8,128)(2,1)} %param.25) | copy-start | bytes 3145732
  13.6 100.9 %all-reduce.16.cloned.1.call-start = ((), (), s32[]{:S(2)}) async-start(), calls=%async_computation.2 | async-start | bytes 786432 | tf_op jit(solution)/shard_map/psum | solution.py:99
  13.7 1.6 copy-start.5
  13.7 2.8 copy-start.32
  13.7 2.8 copy-start.33
  20.5 3.9 copy-start.34
  59.1 2.1 copy-start.28
  59.1 2.1 copy-start.29
  61.1 169.6 %all-reduce.18.cloned.1.call-start = ((), (), s32[]{:S(2)}) async-start(), calls=%async_computation.3 | async-start | bytes 655360 | tf_op jit(solution)/shard_map/psum | solution.py:167
  130.3 6.5 %copy-start.11 = (bf16[8,1,8,32]{3,1,2,0:T(2,128)(2,1)}, bf16[8,1,8,32]{3,1,2,0:T(2,128)(2,1)S(1)}, u32[]{:S(2)}) copy-start(bf16[8,1,8,32]{3,1,2,0:T(2,128)(2,1)S(1)} %copy.117) | copy-start | bytes 12292
  130.3 6.5 %copy-start.13 = (bf16[8,1,8,32]{3,1,2,0:T(2,128)(2,1)}, bf16[8,1,8,32]{3,1,2,0:T(2,128)(2,1)S(1)}, u32[]{:S(2)}) copy-start(bf16[8,1,8,32]{3,1,2,0:T(2,128)(2,1)S(1)} %copy.116) | copy-start | bytes 12292
  130.4 6.4 %copy-start.15 = (bf16[8,1,8,32]{3,1,2,0:T(2,128)(2,1)}, bf16[8,1,8,32]{3,1,2,0:T(2,128)(2,1)S(1)}, u32[]{:S(2)}) copy-start(bf16[8,1,8,32]{3,1,2,0:T(2,128)(2,1)S(1)} %copy.124) | copy-start | bytes 12292
  130.5 6.3 %copy-start.17 = (bf16[8,1,8,32]{3,1,2,0:T(2,128)(2,1)}, bf16[8,1,8,32]{3,1,2,0:T(2,128)(2,1)S(1)}, u32[]{:S(2)}) copy-start(bf16[8,1,8,32]{3,1,2,0:T(2,128)(2,1)S(1)} %copy.123) | copy-start | bytes 12292
  132.6 2.7 copy-start.1
  136.4 1.6 copy-start.19
  136.4 1.6 copy-start.20
  137.4 0.8 copy-start.12
  137.4 0.8 copy-start.14
  137.4 0.8 copy-start.16
  137.4 0.8 copy-start.18
  166.4 3.1 copy-start.3
  172.1 2.8 copy-start.10
  175.9 58.8 %copy-start.2 = (bf16[2048,256]{1,0:T(8,128)(2,1)S(1)}, bf16[2048,256]{1,0:T(8,128)(2,1)}, u32[]{:S(2)}) copy-start(bf16[2048,256]{1,0:T(8,128)(2,1)} %param.24) | copy-start | bytes 3145732
  176.1 174.1 %all-reduce.20.cloned.1.call-start = ((), (), s32[]{:S(2)}) async-start(), calls=%async_computation.4 | async-start | bytes 2097152 | tf_op jit(solution)/shard_map/psum | solution.py:183
  232.5 2.9 copy-start.26
  232.5 3.0 copy-start.9
  234.7 0.8 copy-start.31
  235.1 1.3 copy-start.25
  235.1 1.4 copy-start.8
  290.7 2.9 copy-start.21
  290.7 2.9 copy-start.22
  290.7 2.9 copy-start.23
  290.7 2.9 copy-start.24
  293.6 58.6 %copy-start.30 = (bf16[2048,256]{1,0:T(8,128)(2,1)S(1)}, bf16[2048,256]{1,0:T(8,128)(2,1)}, u32[]{:S(2)}) copy-start(bf16[2048,256]{1,0:T(8,128)(2,1)} %param.27) | copy-start | bytes 3145732
  293.6 103.5 %all-reduce.22.cloned.1.call-start = ((), (), s32[]{:S(2)}) async-start(), calls=%async_computation.5 | async-start | bytes 131072
  352.2 1.8 copy-start.7
  353.1 1.8 copy-start.6
Sparse Core Ops, SparseCore 0:
  13.7 26.3 reduce-scatter.1
  61.2 53.1 all-reduce.15
  176.2 54.4 all-reduce.17
  293.7 56.4 all-reduce.19
  356.0 41.0 all-reduce.21
where the time goes:
time: 409 us; the launch traced here: 407 us
  waiting for transfers between devices  218 us (53%)
  blocking collectives  88.5 us (22%)
  matrix products  41.1 us (10%)
  local copies, waits for them, and re-layouts  32.6 us (8%)
  between operations  15.2 us (4%)
  other arithmetic  11.6 us (3%)
    psum x1, waiting for transfers between devices, shards(): units = lax.psum(unit_terms.astype(jnp.bfloat16), 'seq').astype(jnp.float32)  55.2 us
    psum x1, waiting for transfers between devices, shards(): lax.psum(local_summed.astype(jnp.bfloat16), 'seq').astype(jnp.float32)  54.4 us
    psum x1, waiting for transfers between devices, shards(): lax.psum(jnp.dot(normed, w_qkv, preferred_element_type=jnp.float32), 'seq')  53.2 us
    unnamed x6, waiting for transfers between devices  40.6 us
    all_gather x4, blocking collectives, shards(): lax.all_gather(mlp_in, 'req', axis=0, tiled=True)  31.5 us
    psum x2, blocking collectives, norm_sum(): return lax.psum(jnp.sum(values * values, axis=-1), 'seq')  29.5 us
    pmax x1, blocking collectives, shards(): top = lax.pmax(local_top, 'seq')  27.5 us
    reduce_scatter x1, waiting for transfers between devices, shards(): lax.psum_scatter(jnp.dot(onehot, embed_table, preferred_element_type=jnp....  14.5 us
  transfers between devices with their start and end apart: 5, of which 5 were waited for; matrix products, arithmetic and copies ran while one was open for 3% of the time, Pallas kernels for 0%

commit v1 on v0

v1 whole, which is shorter than its diff:
```python
import functools
import math

import jax
import jax.numpy as jnp
import numpy as np
from jax import lax
from jax.experimental import pallas as pl
from jax.experimental.pallas import tpu as pltpu
from jax.sharding import PartitionSpec as P

D = 2048
QUERY_HEADS = 32
KEY_VALUE_HEADS = 8
HEAD_SIZE = 64
GROUP = QUERY_HEADS // KEY_VALUE_HEADS
EPSILON = 1e-05
ROPE_BASE = 500000.0

HEADS = QUERY_HEADS // 2
KV_HEADS = KEY_VALUE_HEADS // 2
QW = HEADS * HEAD_SIZE
KW = KV_HEADS * HEAD_SIZE
HALF = QW + 2 * KW
LANES = 128
LOW = -1e30

BF16 = jnp.bfloat16
F32 = jnp.float32
SMEM = pl.BlockSpec(memory_space=pltpu.SMEM)
VMEM = pl.BlockSpec(memory_space=pltpu.VMEM)
ANY = pl.BlockSpec(memory_space=pl.ANY)


def mm(a, b):
    return lax.dot_general(a, b, (((1,), (0,)), ((), ())), preferred_element_type=F32)


def mm_t(a, b):
    return lax.dot_general(a, b, (((1,), (1,)), ((), ())), preferred_element_type=F32)


def lane_iota(shape):
    return lax.broadcasted_iota(jnp.int32, shape, len(shape) - 1)


def split(value):
    high = value.astype(BF16).astype(F32)
    low = (value - high).astype(BF16).astype(F32)
    return high, low


def tail_of(value):
    high, low = split(value)
    lane = lane_iota((value.shape[0], LANES))
    return jnp.where(lane == 0, high, jnp.where(lane == 1, low, 0.0))


def tail_sum(*tails):
    total = tails[0].astype(F32)
    for tail in tails[1:]:
        total = total + tail.astype(F32)
    return jnp.sum(total, axis=-1, keepdims=True)


def exchange(array, axis, size, mask):
    return lax.ppermute(array, axis, [(i, i ^ mask) for i in range(size)])


def call(kernel, outs, ins, specs, scratch=(), limit=24, cost=None, name=None):
    return pl.pallas_call(
        kernel,
        out_shape=outs,
        in_specs=specs,
        out_specs=jax.tree.map(lambda _: VMEM, outs),
        scratch_shapes=list(scratch),
        compiler_params=pltpu.CompilerParams(vmem_limit_bytes=limit << 20),
        cost_estimate=cost,
        name=name,
    )(*ins)


def shape(dims, dtype):
    return jax.ShapeDtypeStruct(tuple(dims), dtype)


def lookup_kernel(rows, place, ids_s, ids_v, table, out, blocks, sem):
    req_count, count = out.shape[0], out.shape[1]
    vocab_dev = table.shape[0]
    me = place[2]
    base = me * vocab_dev

    def block_copy(k, j):
        local = ids_s[(me ^ k) * count + j] - base
        inside = (local >= 0) & (local < vocab_dev)
        first = jnp.minimum(lax.div(jnp.clip(local, 0, vocab_dev - 1), rows) * rows, vocab_dev - rows)
        copy = pltpu.make_async_copy(
            table.at[pl.ds(pl.multiple_of(first, 8), rows)], blocks.at[k, j], sem
        )
        return inside, copy

    for k in range(req_count):
        @pl.loop(0, count)
        def _(j):
            inside, copy = block_copy(k, j)
            pl.when(inside)(copy.start)

    for k in range(req_count):
        @pl.loop(0, count)
        def _(j):
            inside, copy = block_copy(k, j)
            pl.when(inside)(copy.wait)

    for k in range(req_count):
        local = ids_v[me ^ k] - base
        inside = (local >= 0) & (local < vocab_dev)
        first = jnp.minimum(lax.div(jnp.clip(local, 0, vocab_dev - 1), rows) * rows, vocab_dev - rows)
        row = jnp.where(inside, local - first, -1)[:, :, None]
        at = lax.broadcasted_iota(jnp.int32, (count, rows, 1), 1)
        taken = jnp.where(at == row, blocks[k].astype(F32), 0.0)
        out[k] = jnp.sum(taken, axis=1).astype(BF16)


def project_kernel(parts, place, gain, weight, *refs):
    blocks, (x_out, keep, give) = refs[:parts], refs[parts:]
    x = blocks[0][...].astype(F32)
    for block in blocks[1:]:
        x = x + block[...].astype(F32)
    x_out[...] = x.astype(BF16)
    scaled = (x * gain[...].astype(F32)).astype(BF16)
    tail = tail_of(jnp.sum(x * x, axis=-1, keepdims=True)).astype(BF16)
    first = place[0] == 0
    q_end, k_end = 2 * QW, 2 * QW + 2 * KW
    at = 0
    for start, width in ((0, QW), (q_end, KW), (k_end, KW)):
        one = mm(scaled, weight[:, start : start + width])
        two = mm(scaled, weight[:, start + width : start + 2 * width])
        keep[:, at : at + width] = jnp.where(first, one, two).astype(BF16)
        give[:, at : at + width] = jnp.where(first, two, one).astype(BF16)
        at += width
    keep[:, HALF:] = tail
    give[:, HALF:] = tail


def add_kernel(a, b, out):
    out[:, :HALF] = (a[:, :HALF].astype(F32) + b[:, :HALF].astype(F32)).astype(BF16)
    out[:, HALF:] = tail_of(tail_sum(a[:, HALF:], b[:, HALF:])).astype(BF16)


def rotate(v, cosine, sine):
    width = v.shape[-1]
    lane = lane_iota(v.shape)
    half = HEAD_SIZE // 2
    ahead = pltpu.roll(v, width - half, 1)
    behind = pltpu.roll(v, half, 1)
    other = jnp.where(lane % HEAD_SIZE < half, ahead, behind)
    reps = width // LANES
    cosine = jnp.concatenate([cosine] * reps, axis=1)
    sine = jnp.concatenate([sine] * reps, axis=1)
    return v * cosine + other * sine


def attend_kernel(
    steps, place, starts, lens, a, b, cosine, sine, fold, keys, keys2, values, values2,
    packed, new_k, new_v, out_rows, stats,
):
    count = a.shape[0]
    requests = count // steps
    rows = steps * HEADS
    context = keys.shape[1]
    core, z, me = place[0], place[1], place[3]
    total = a[:, :HALF].astype(F32) + b[:, :HALF].astype(F32)
    squares = tail_sum(a[:, HALF:], b[:, HALF:])
    total = total * lax.rsqrt(squares / D + EPSILON)
    q = rotate(total[:, :QW], cosine[...], sine[...]).astype(BF16)
    k = rotate(total[:, QW : QW + KW], cosine[...], sine[...]).astype(BF16)
    v = total[:, QW + KW :].astype(BF16)
    new_k[...] = k
    new_v[...] = v

    head = lax.broadcasted_iota(jnp.int32, (count, HEADS, QW), 1)
    lane = lax.broadcasted_iota(jnp.int32, (count, HEADS, QW), 2)
    own_head = lane // HEAD_SIZE == head
    wide = jnp.where(own_head, q.astype(F32)[:, None, :], 0.0).astype(BF16)
    q_rows = mm(wide.reshape(count * HEADS, QW), fold[...]).astype(BF16)

    scale = 1.0 / math.sqrt(HEAD_SIZE)
    fresh_all = mm_t(q_rows, k) * scale
    columns = pl.ds(pl.multiple_of(core * KW, KW), KW)
    spot = lax.broadcasted_iota(jnp.int32, (1, context), 1)
    row_head = lax.broadcasted_iota(jnp.int32, (rows, KW), 0) % HEADS
    own_kv = lane_iota((rows, KW)) // HEAD_SIZE == row_head // GROUP
    row_step = lax.broadcasted_iota(jnp.int32, (rows, count), 0) // HEADS
    fresh_at = lane_iota((rows, count))
    stat_lane = lane_iota((rows, LANES))
    stat_head = lax.broadcasted_iota(jnp.int32, (rows, LANES), 0) % HEADS
    for r in range(requests):
        qr = q_rows[r * rows : (r + 1) * rows]
        lo, hi = starts[r], lens[r]
        place_a = spot + me * context
        place_b = spot + (me ^ 1) * context
        seen_a = (place_a >= lo) & (place_a < hi)
        seen_b = (place_b >= lo) & (place_b < hi)
        seen_f = (fresh_at >= r * steps) & (fresh_at <= r * steps + row_step) & (z == 0)
        sa = jnp.where(seen_a, mm_t(qr, keys[r, :, columns]) * scale, LOW)
        sb = jnp.where(seen_b, mm_t(qr, keys2[r, :, columns]) * scale, LOW)
        sf = jnp.where(seen_f, fresh_all[r * rows : (r + 1) * rows], LOW)
        top = jnp.maximum(
            jnp.maximum(jnp.max(sa, axis=-1, keepdims=True), jnp.max(sb, axis=-1, keepdims=True)),
            jnp.max(sf, axis=-1, keepdims=True),
        )
        top_high, top_low = split(top)
        top = top_high + top_low
        pa = jnp.where(seen_a, jnp.exp(sa - top), 0.0)
        pb = jnp.where(seen_b, jnp.exp(sb - top), 0.0)
        pf = jnp.where(seen_f, jnp.exp(sf - top), 0.0)
        weight = (
            jnp.sum(pa, axis=-1, keepdims=True)
            + jnp.sum(pb, axis=-1, keepdims=True)
            + jnp.sum(pf, axis=-1, keepdims=True)
        )
        o = (
            mm(pa.astype(BF16), values[r, :, columns])
            + mm(pb.astype(BF16), values2[r, :, columns])
            + mm(pf.astype(BF16), v)
        )
        out_rows[r * rows : (r + 1) * rows, :] = jnp.where(own_kv, o, 0.0).astype(BF16)
        w_high, w_low = split(weight)
        stat = jnp.where(stat_lane == stat_head, top_high, 0.0)
        stat = jnp.where(stat_lane == stat_head + HEADS, top_low, stat)
        stat = jnp.where(stat_lane == stat_head + 2 * HEADS, w_high, stat)
        stat = jnp.where(stat_lane == stat_head + 3 * HEADS, w_low, stat)
        stats[r * rows : (r + 1) * rows, :] = stat
    spread = mm_t(out_rows[...], fold[...]).reshape(count, HEADS, QW)
    packed[:, :QW] = jnp.sum(jnp.where(own_head, spread, 0.0), axis=1).astype(BF16)
    packed[:, QW:] = jnp.sum(stats[...].reshape(count, HEADS, LANES), axis=1).astype(BF16)


def read_stats(block):
    block = block.astype(F32)
    both = block + pltpu.roll(block, LANES - HEADS, 1)
    return both, pltpu.roll(both, LANES - 2 * HEADS, 1)


def widen(column_block, spread):
    lane = lane_iota(column_block.shape)
    high, low = split(column_block)
    pair = jnp.where(lane < HEADS, high, jnp.where(lane < 2 * HEADS, pltpu.roll(low, HEADS, 1), 0.0))
    return mm(pair.astype(BF16), spread[...])


def merge(a, b, spread):
    top_a, sum_a = read_stats(a[:, QW:])
    top_b, sum_b = read_stats(b[:, QW:])
    top = jnp.maximum(top_a, top_b)
    fa, fb = jnp.exp(top_a - top), jnp.exp(top_b - top)
    total = sum_a * fa + sum_b * fb
    return top, total, fa, fb


def merge_kernel(a, b, spread, out):
    top, total, fa, fb = merge(a, b, spread)
    wide = widen(fa, spread) * a[:, :QW].astype(F32) + widen(fb, spread) * b[:, :QW].astype(F32)
    out[:, :QW] = wide.astype(BF16)
    lane = lane_iota(top.shape)
    top_high, top_low = split(top)
    w_high, w_low = split(total)
    stat = jnp.where(lane < HEADS, top_high, 0.0)
    stat = jnp.where((lane >= HEADS) & (lane < 2 * HEADS), pltpu.roll(top_low, HEADS, 1), stat)
    stat = jnp.where((lane >= 2 * HEADS) & (lane < 3 * HEADS), pltpu.roll(w_high, 2 * HEADS, 1), stat)
    stat = jnp.where((lane >= 3 * HEADS) & (lane < 4 * HEADS), pltpu.roll(w_low, 3 * HEADS, 1), stat)
    out[:, QW:] = stat.astype(BF16)


def output_kernel(place, a, b, spread, w_own, w_two, out):
    top, total, fa, fb = merge(a, b, spread)
    lane = lane_iota(top.shape)
    total = jnp.where(lane < HEADS, total, 1.0)
    fa, fb = fa / total, fb / total
    wide = widen(fa, spread) * a[:, :QW].astype(F32) + widen(fb, spread) * b[:, :QW].astype(F32)
    attended = wide.astype(BF16)
    core = place[0]
    rows = pl.ds(pl.multiple_of(core * QW, QW), QW)
    own = mm(attended, w_own[rows, :])
    two = mm(attended, w_two[rows, :])
    first = core == 0
    width = own.shape[1]
    out[:, :width] = jnp.where(first, own, two)
    out[:, width:] = jnp.where(first, two, own)


def gate_kernel(parts, place, gains, g_own, g_two, u_own, u_two, *refs):
    blocks, (out, rows_ref) = refs[:parts], refs[parts:]
    count = blocks[0].shape[0]
    for i, block in enumerate(blocks):
        rows_ref[i * count : (i + 1) * count, :] = block[...]
    core, z = place[0], place[1]
    chunks, size = out.shape[0], out.shape[1]
    taken = [
        rows_ref[pl.ds(pl.multiple_of((z ^ j) * size, size), size), :].astype(F32)
        for j in range(chunks)
    ]
    x = jnp.concatenate(taken, axis=0)
    squares = jnp.sum(x * x, axis=-1, keepdims=True)
    scaled = (x * gains[...].astype(F32)).astype(BF16)
    feat = scaled.shape[1] // 2
    first = core == 0
    mine = jnp.where(first, scaled[:, :feat], scaled[:, feat:])
    theirs = jnp.where(first, scaled[:, feat:], scaled[:, :feat])
    hid = g_own.shape[1] // 2
    columns = pl.ds(pl.multiple_of(core * hid, hid), hid)
    gate = mm(mine, g_own[:, columns]) + mm(theirs, g_two[:, columns])
    up = mm(mine, u_own[:, columns]) + mm(theirs, u_two[:, columns])
    tail = tail_of(squares)
    for j in range(chunks):
        at = slice(j * size, (j + 1) * size)
        out[j, :, :hid] = gate[at].astype(BF16)
        out[j, :, hid : 2 * hid] = up[at].astype(BF16)
        out[j, :, 2 * hid :] = tail[at].astype(BF16)


def hidden_kernel(parts, *refs):
    blocks, out = refs[:parts], refs[parts]
    hid = out.shape[1]
    total = blocks[0][:, : 2 * hid].astype(F32)
    for block in blocks[1:]:
        total = total + block[:, : 2 * hid].astype(F32)
    squares = tail_sum(*[block[:, 2 * hid :] for block in blocks])
    inverse = lax.rsqrt(squares / D + EPSILON)
    gate, up = total[:, :hid] * inverse, total[:, hid:] * inverse
    out[...] = (gate / (1.0 + jnp.exp(-gate)) * up).astype(BF16)


def down_kernel(parts, place, w_down, *refs):
    mine, theirs, (out, rows_ref) = refs[:parts], refs[parts : 2 * parts], refs[2 * parts :]
    core, z = place[0], place[1]
    size, hid = mine[0].shape
    near = jnp.concatenate([ref[...] for ref in mine], axis=0)
    far = jnp.concatenate([ref[...] for ref in theirs], axis=0)
    total = mm(near, w_down[pl.ds(pl.multiple_of(core * hid, hid), hid), :]) + mm(
        far, w_down[pl.ds(pl.multiple_of((1 - core) * hid, hid), hid), :]
    )
    for j in range(parts):
        rows_ref[pl.ds(pl.multiple_of((z ^ j) * size, size), size), :] = total[
            j * size : (j + 1) * size
        ]
    count = out.shape[1]
    for k in range(out.shape[0]):
        out[k] = rows_ref[k * count : (k + 1) * count, :].astype(BF16)


def shards(
    seq_size,
    req_size,
    token_ids,
    embed_table,
    cache_len,
    range_start,
    positions,
    cached_key_rows,
    cached_value_rows,
    attn_gain,
    mlp_gain,
    w_qkv,
    w_out,
    w_gate,
    w_up,
    w_down,
):
    requests, steps = cache_len.shape[0], token_ids.shape[1]
    count = requests * steps
    feat = embed_table.shape[1]
    seq_index, req_index = lax.axis_index("seq"), lax.axis_index("req")
    core, z = seq_index % 2, seq_index // 2
    depth = seq_size // 2
    place = jnp.stack([core, z, req_index, seq_index]).astype(jnp.int32)
    swap = lambda array: exchange(array, "seq", seq_size, 1)
    over_z = lambda array, mask: exchange(array, "seq", seq_size, 2 * mask)
    over_req = lambda array, mask: exchange(array, "req", req_size, mask)

    ids = token_ids.reshape(-1)
    rows = 16
    found = call(
        functools.partial(lookup_kernel, rows),
        shape((req_size, count, feat), BF16),
        (place, ids, ids.reshape(req_size, count, 1), embed_table),
        [SMEM, SMEM, VMEM, ANY],
        [pltpu.VMEM((req_size, count, rows, feat), BF16), pltpu.SemaphoreType.DMA],
        name="lookup",
    )
    blocks = [found[0]] + [over_req(found[k], k) for k in range(1, req_size)]

    keys2, values2 = swap(cached_key_rows), swap(cached_value_rows)
    gate2, up2, out2 = swap(w_gate), swap(w_up), swap(w_out)
    gain_two = swap(mlp_gain.reshape(1, feat))
    gain_own = mlp_gain.reshape(1, feat)
    pair = lambda own, two: jnp.where(
        core == 0, jnp.concatenate([own, two], axis=1), jnp.concatenate([two, own], axis=1)
    )

    half = HEAD_SIZE // 2
    freqs = ROPE_BASE ** (-2.0 * jnp.arange(half, dtype=F32) / HEAD_SIZE)
    when = (positions[:, None] + jnp.arange(steps, dtype=jnp.int32)[None, :]).astype(F32)
    angles = when.reshape(count, 1) * freqs[None, :]
    cosine, sine = jnp.cos(angles), jnp.sin(angles)
    cosine = jnp.concatenate([cosine] * 4, axis=1)
    sine = jnp.concatenate([-sine, sine] * 2, axis=1)

    wide = HALF + LANES
    x, keep, give = call(
        functools.partial(project_kernel, req_size),
        (shape((count, feat), BF16), shape((count, wide), BF16), shape((count, wide), BF16)),
        (place, attn_gain.reshape(1, feat), w_qkv, *blocks),
        [SMEM] + [VMEM] * (2 + req_size),
        name="project",
    )
    x_two = swap(x)
    mine, other = keep, swap(give)
    mask = 1
    while mask < depth:
        mine = call(add_kernel, shape((count, wide), BF16), (mine, other), [VMEM] * 2, name="add")
        other = over_z(mine, mask)
        mask *= 2

    head_lane, kv_lane = np.arange(QW)[:, None], np.arange(KW)[None, :]
    fold = jnp.asarray(
        (head_lane % HEAD_SIZE == kv_lane % HEAD_SIZE)
        & (head_lane // (GROUP * HEAD_SIZE) == kv_lane // HEAD_SIZE),
        BF16,
    )
    spread = jnp.asarray(
        (np.arange(LANES)[:, None] % HEADS == np.arange(QW)[None, :] // HEAD_SIZE)
        & (np.arange(LANES)[:, None] < 2 * HEADS),
        BF16,
    )
    packed_width = QW + LANES
    packed, new_k, new_v = call(
        functools.partial(attend_kernel, steps),
        (shape((count, packed_width), BF16), shape((count, KW), BF16), shape((count, KW), BF16)),
        (
            place, range_start, cache_len, mine, other, cosine, sine, fold,
            cached_key_rows, keys2, cached_value_rows, values2,
        ),
        [SMEM] * 3 + [VMEM] * 9,
        [pltpu.VMEM((count * HEADS, KW), BF16), pltpu.VMEM((count * HEADS, LANES), F32)],
        name="attend",
    )
    mine, other, mask = packed, over_z(packed, 1), 2
    while mask < depth:
        mine = call(
            merge_kernel, shape((count, packed_width), BF16), (mine, other, spread), [VMEM] * 3, name="merge"
        )
        other = over_z(mine, mask)
        mask *= 2
    part = call(
        output_kernel,
        shape((count, 2 * feat), F32),
        (place, mine, other, spread, w_out, out2),
        [SMEM] + [VMEM] * 5,
        name="output",
    )
    resid = (pair(x, x_two).astype(F32) + (part + swap(part))).astype(BF16)

    taken = [resid] + [over_req(resid, k) for k in range(1, req_size)]
    gains = pair(gain_own, gain_two)
    size = req_size * count // depth
    hid = w_gate.shape[1] // 2
    terms = call(
        functools.partial(gate_kernel, req_size),
        shape((depth, size, 2 * hid + LANES), BF16),
        (place, gains, w_gate, gate2, w_up, up2, *taken),
        [SMEM] + [VMEM] * (5 + req_size),
        [pltpu.VMEM((req_size * count, 2 * feat), BF16)],
        name="gate",
    )
    sums = [terms[0]] + [over_z(terms[j], j) for j in range(1, depth)]
    hidden = call(
        functools.partial(hidden_kernel, depth),
        shape((size, hid), BF16),
        sums,
        [VMEM] * depth,
        name="hidden",
    )
    near = [hidden] + [over_z(hidden, j) for j in range(1, depth)]
    far = [swap(block) for block in near]
    back = call(
        functools.partial(down_kernel, depth),
        shape((req_size, count, feat), BF16),
        (place, w_down, *near, *far),
        [SMEM] + [VMEM] * (1 + 2 * depth),
        [pltpu.VMEM((req_size * count, feat), F32)],
        name="down",
    )
    total = back[0].astype(F32)
    for k in range(1, req_size):
        total = total + over_req(back[k], k).astype(F32)
    resid_own = lax.dynamic_slice_in_dim(resid, core * feat, feat, axis=1)
    layer_out = (resid_own.astype(F32) + total).astype(BF16)

    new_k2, new_v2 = swap(new_k), swap(new_v)
    return (
        layer_out.reshape(requests, steps, feat),
        pair(new_k, new_k2).reshape(requests, steps, 2 * KW),
        pair(new_v, new_v2).reshape(requests, steps, 2 * KW),
    )


def solution(mesh):
    in_specs = (
        P(),
        P("req", "seq"),
        P("req"),
        P("req"),
        P("req"),
        P("req", "seq", None),
        P("req", "seq", None),
        P("seq"),
        P("seq"),
        P("seq", None),
        P(None, "seq"),
        P("seq", "req"),
        P("seq", "req"),
        P("req", "seq"),
    )
    out_specs = (P("req", None, "seq"), P("req", None, None), P("req", None, None))
    body = functools.partial(shards, mesh.shape["seq"], mesh.shape["req"])
    return jax.shard_map(body, mesh=mesh, in_specs=in_specs, out_specs=out_specs, check_vma=False)
```

time: 409 us -> 102 us (0.25)
  waiting for transfers between devices: 218 us -> 41.6 us
  blocking collectives: 88.5 us -> 0 us
  matrix products: 41.1 us -> 0 us
  starting transfers between devices: 0.21 us -> 31 us
  local copies, waits for them, and re-layouts: 32.6 us -> 7.76 us
  Pallas kernels: 0 us -> 18.7 us
  between operations: 15.2 us -> 0.93 us
  other arithmetic: 11.6 us -> 1.71 us
    psum x3 -> x0, waiting for transfers between devices: 163 us -> none  [the longest x1 55.2 us: shards(): units = lax.psum(unit_terms.astype(jnp.bfloat16), 'seq').astype(jnp.float32)]
    ppermute x0 -> x34, waiting for transfers between devices: none -> 41.6 us  [exchange(): return lax.ppermute(array, axis, [(i, i ^ mask) for i in range(size)])]
    dot_general x32 -> x0, matrix products: 41.1 us -> none  [the longest x4 11.2 us: shards(): jnp.dot(lax.all_gather(mlp_in, 'req', axis=0, tiled=True), w_pair, prefer...]
    unnamed x6 -> x0, waiting for transfers between devices: 40.6 us -> none
    all_gather x4 -> x0, blocking collectives: 31.5 us -> none  [shards(): lax.all_gather(mlp_in, 'req', axis=0, tiled=True)]
    ppermute x0 -> x34, starting transfers between devices: none -> 31 us  [exchange(): return lax.ppermute(array, axis, [(i, i ^ mask) for i in range(size)])]
    psum x2 -> x0, blocking collectives: 29.5 us -> none  [norm_sum(): return lax.psum(jnp.sum(values * values, axis=-1), 'seq')]
    pmax x1 -> x0, blocking collectives: 27.5 us -> none  [shards(): top = lax.pmax(local_top, 'seq')]
  transfers between devices with their start and end apart: 5 -> 34, of which waited for: 5 -> 21; matrix products, arithmetic and copies ran while one was open for 3% -> 3% of each run, Pallas kernels for 0% -> 15%
where the time goes in v1:
time: 102 us
  waiting for transfers between devices  41.6 us (41%)
  starting transfers between devices  31 us (30%)
  Pallas kernels  18.7 us (18%)
  local copies, waits for them, and re-layouts  7.76 us (8%)
  other arithmetic  1.71 us (2%)
    ppermute x34, waiting for transfers between devices, exchange(): return lax.ppermute(array, axis, [(i, i ^ mask) for i in range(size)])  41.6 us
    ppermute x34, starting transfers between devices, exchange(): return lax.ppermute(array, axis, [(i, i ^ mask) for i in range(size)])  31 us
    pallas_call x10, Pallas kernels, call(): pl.pallas_call(kernel, out_shape=outs, in_specs=specs, out_specs=jax.tree...  18.7 us
    unnamed x27, local copies, waits for them, and re-layouts  6.77 us
  transfers between devices with their start and end apart: 34, of which 21 were waited for; matrix products, arithmetic and copies ran while one was open for 3% of the time, Pallas kernels for 15%

profile of v1, /device:TPU:0, one launch (start us, length us, event | category | flops | bytes accessed | tf_op | source)
XLA Modules:
  0.0 101.7 jit_solution(7688137663180963868)
XLA Ops:
  0.6 0.5 collective-permute-start.7
  1.2 0.8 copy.22
  2.1 0.1 reshape.113.ids_s
  2.3 3.3 %copy-done = bf16[16032,256]{1,0:T(8,128)(2,1)S(1)} copy-done((bf16[16032,256]{1,0:T(8,128)(2,1)S(1)}, bf16[16032,256]{1,0:T(8,128)(2,1)}, u32[]{:S(2)}) %copy-start) | copy-done | bytes 8208408
  5.6 5.4 %lookup.1 = bf16[4,32,256]{2,1,0:T(8,128)(2,1)S(1)} custom-call(s32[4]{0:T(128)S(1)} %pad_add_fusion.place, s32[128]{0:T(128)S(1)} %reshape.113.ids_s, s32[4,32,1]{2,1,0:T(8,128)S(1)} %reshape_reshape.4.ids_v, bf16[16032,256]{1,0:T(8,128)(2,1)S(1)} %copy-done), custom_call_target="tpu_custom_call" | custom-call | tf_op jit(solution)/shard_map/lookup/pallas_call | solution.py:71
  11.1 3.1 %collective-permute-start = (bf16[32,256]{1,0:T(8,128)(2,1)S(1)}, bf16[32,256]{1,0:T(8,128)(2,1)S(1)}, u32[]{:S(2)}, u32[]{:S(2)}) collective-permute-start(bf16[32,256]{1,0:T(8,128)(2,1)S(1)} %get-tuple-element.24), channel_id=1, source_target_pairs={{0,1},{1,0},{2,3},{3,2},{4,5},{5,4},{6,7},{7,6},{8,9},{9,8},{10,11... | collective-permute-start | bytes 49160 | tf_op jit(solution)/shard_map/ppermute | solution.py:67
  14.2 1.2 %collective-permute-start.1 = (bf16[32,256]{1,0:T(8,128)(2,1)S(1)}, bf16[32,256]{1,0:T(8,128)(2,1)S(1)}, u32[]{:S(2)}, u32[]{:S(2)}) collective-permute-start(bf16[32,256]{1,0:T(8,128)(2,1)S(1)} %get-tuple-element.23), channel_id=1, source_target_pairs={{0,2},{1,3},{2,0},{3,1},{4,6},{5,7},{6,4},{7,5},{8,10},{9,11},{10,... | collective-permute-start | bytes 49160 | tf_op jit(solution)/shard_map/ppermute | solution.py:67
  15.5 0.3 collective-permute-start.2
  15.8 0.2 collective-permute-done.refs_1_
  15.9 2.0 %collective-permute-done.1.refs_2_ = bf16[32,256]{1,0:T(8,128)(2,1)S(1)} collective-permute-done((bf16[32,256]{1,0:T(8,128)(2,1)S(1)}, bf16[32,256]{1,0:T(8,128)(2,1)S(1)}, u32[]{:S(2)}, u32[]{:S(2)}) %collective-permute-start.1) | collective-permute-done | bytes 16416 | tf_op jit(solution)/shard_map/ppermute | solution.py:67
  18.0 2.1 %collective-permute-done.2.refs_3_ = bf16[32,256]{1,0:T(8,128)(2,1)S(1)} collective-permute-done((bf16[32,256]{1,0:T(8,128)(2,1)S(1)}, bf16[32,256]{1,0:T(8,128)(2,1)S(1)}, u32[]{:S(2)}, u32[]{:S(2)}) %collective-permute-start.2) | collective-permute-done | bytes 16416 | tf_op jit(solution)/shard_map/ppermute | solution.py:67
  20.1 0.9 project.1
  21.1 0.5 collective-permute-start.11
  21.6 0.8 collective-permute-done.4.b
  22.5 1.6 %collective-permute-start.5 = (bf16[32,1664]{1,0:T(8,128)(2,1)S(1)}, bf16[32,1664]{1,0:T(8,128)(2,1)S(1)}, u32[]{:S(2)}, u32[]{:S(2)}) collective-permute-start(bf16[32,1664]{1,0:T(8,128)(2,1)S(1)} %add.92.a), channel_id=1, source_target_pairs={{0,8},{4,12},{8,0},{12,4},{16,24},{20,28},{24,16},{28,20},{1,9},{5... | collective-permute-start | bytes 319496 | tf_op jit(solution)/shard_map/ppermute | solution.py:67
  24.1 3.5 %collective-permute-done.5.b = bf16[32,1664]{1,0:T(8,128)(2,1)S(1)} collective-permute-done((bf16[32,1664]{1,0:T(8,128)(2,1)S(1)}, bf16[32,1664]{1,0:T(8,128)(2,1)S(1)}, u32[]{:S(2)}, u32[]{:S(2)}) %collective-permute-start.5) | collective-permute-done | bytes 106528 | tf_op jit(solution)/shard_map/ppermute | solution.py:67
  27.6 2.6 %collective-permute-start.6 = (bf16[32,1664]{1,0:T(8,128)(2,1)S(1)}, bf16[32,1664]{1,0:T(8,128)(2,1)S(1)}, u32[]{:S(2)}, u32[]{:S(2)}) collective-permute-start(bf16[32,1664]{1,0:T(8,128)(2,1)S(1)} %add.93.a), channel_id=1, source_target_pairs={{0,16},{4,20},{8,24},{12,28},{16,0},{20,4},{24,8},{28,12},{1,17},{... | collective-permute-start | bytes 319496 | tf_op jit(solution)/shard_map/ppermute | solution.py:67
  30.2 4.8 %collective-permute-done.6.b = bf16[32,1664]{1,0:T(8,128)(2,1)S(1)} collective-permute-done((bf16[32,1664]{1,0:T(8,128)(2,1)S(1)}, bf16[32,1664]{1,0:T(8,128)(2,1)S(1)}, u32[]{:S(2)}, u32[]{:S(2)}) %collective-permute-start.6) | collective-permute-done | bytes 106528 | tf_op jit(solution)/shard_map/ppermute | solution.py:67
  35.2 0.1 fusion.4
  35.3 0.1 pad_maximum_fusion
  35.5 1.6 %copy-done.2 = bf16[8,256,512]{2,1,0:T(8,128)(2,1)S(1)} copy-done((bf16[8,256,512]{2,1,0:T(8,128)(2,1)S(1)}, bf16[8,256,512]{2,1,0:T(8,128)(2,1)}, u32[]{:S(2)}) %copy-start.2) | copy-done | bytes 2097176
  37.1 1.0 %copy-done.7 = bf16[1024,256]{1,0:T(8,128)(2,1)S(1)} copy-done((bf16[1024,256]{1,0:T(8,128)(2,1)S(1)}, bf16[1024,256]{1,0:T(8,128)(2,1)}, u32[]{:S(2)}) %copy-start.7) | copy-done | bytes 524312
  38.1 6.4 %attend.1 = (bf16[32,1152]{1,0:T(8,128)(2,1)S(1)}, bf16[32,256]{1,0:T(8,128)(2,1)S(1)}, bf16[32,256]{1,0:T(8,128)(2,1)S(1)}) custom-call(s32[4]{0:T(128)S(1)} %pad_add_fusion.place, s32[8]{0:T(128)S(1)} %copy-done.8, s32[8]{0:T(128)S(1)} %copy-done.9, bf16[32,1664]{1,0:T(8,128)(2,1)S(1)} %add.93.a, bf16[32,1664]{1,0:T(8,128)(2,1)S(1)} %collective-permute-done.6.b, ...), custom_call_target="tpu_custom_call" | custom-call | tf_op jit(solution)/shard_map/attend/pallas_call | solution.py:71
  44.5 0.7 collective-permute-start.9
  45.2 4.0 %collective-permute-done.9.b = bf16[32,1152]{1,0:T(8,128)(2,1)S(1)} collective-permute-done((bf16[32,1152]{1,0:T(8,128)(2,1)S(1)}, bf16[32,1152]{1,0:T(8,128)(2,1)S(1)}, u32[]{:S(2)}, u32[]{:S(2)}) %collective-permute-start.9) | collective-permute-done | bytes 73760 | tf_op jit(solution)/shard_map/ppermute | solution.py:67
  49.3 0.4 merge.1.a
  49.6 2.4 %collective-permute-start.10 = (bf16[32,1152]{1,0:T(8,128)(2,1)S(1)}, bf16[32,1152]{1,0:T(8,128)(2,1)S(1)}, u32[]{:S(2)}, u32[]{:S(2)}) collective-permute-start(bf16[32,1152]{1,0:T(8,128)(2,1)S(1)} %merge.1.a), channel_id=1, source_target_pairs={{0,16},{4,20},{8,24},{12,28},{16,0},{20,4},{24,8},{28,12},{1,17},{... | collective-permute-start | bytes 221192 | tf_op jit(solution)/shard_map/ppermute | solution.py:67
  52.0 4.1 %collective-permute-done.10.b = bf16[32,1152]{1,0:T(8,128)(2,1)S(1)} collective-permute-done((bf16[32,1152]{1,0:T(8,128)(2,1)S(1)}, bf16[32,1152]{1,0:T(8,128)(2,1)S(1)}, u32[]{:S(2)}, u32[]{:S(2)}) %collective-permute-start.10) | collective-permute-done | bytes 73760 | tf_op jit(solution)/shard_map/ppermute | solution.py:67
  56.1 1.9 %output.1 = f32[32,512]{1,0:T(8,128)S(1)} custom-call(s32[4]{0:T(128)S(1)} %pad_add_fusion.place, bf16[32,1152]{1,0:T(8,128)(2,1)S(1)} %merge.1.a, bf16[32,1152]{1,0:T(8,128)(2,1)S(1)} %collective-permute-done.10.b, bf16[128,1024]{1,0:T(8,128)(2,1)S(1)} %copy-done.6, bf16[2048,256]{1,0:T(8,128)(2,1)S(1)} %copy-done.5, ...), custom_call_target="tpu_custom_call" | custom-call | tf_op jit(solution)/shard_map/output/pallas_call | solution.py:71
  58.0 0.5 collective-permute-start.3
  58.6 0.7 collective-permute-done.3
  59.4 0.6 collective-permute-start.16
  59.9 0.7 collective-permute-start.17
  60.6 2.3 %collective-permute-start.18 = (bf16[32,512]{1,0:T(8,128)(2,1)S(1)}, bf16[32,512]{1,0:T(8,128)(2,1)S(1)}, u32[]{:S(2)}, u32[]{:S(2)}) collective-permute-start(bf16[32,512]{1,0:T(8,128)(2,1)S(1)} %add_convert_fusion.refs_0_), channel_id=1, source_target_pairs={{0,3},{1,2},{2,1},{3,0},{4,7},{5,6},{6,5},{7,4},{8,11},{9,10},{10,... | collective-permute-start | bytes 98312 | tf_op jit(solution)/shard_map/ppermute | solution.py:67
  63.0 0.4 collective-permute-done.16.refs_1_
  63.4 0.5 collective-permute-done.17.refs_2_
  63.9 1.6 %collective-permute-done.18.refs_3_ = bf16[32,512]{1,0:T(8,128)(2,1)S(1)} collective-permute-done((bf16[32,512]{1,0:T(8,128)(2,1)S(1)}, bf16[32,512]{1,0:T(8,128)(2,1)S(1)}, u32[]{:S(2)}, u32[]{:S(2)}) %collective-permute-start.18) | collective-permute-done | bytes 32800 | tf_op jit(solution)/shard_map/ppermute | solution.py:67
  65.4 2.7 %gate.1 = bf16[4,32,2176]{2,1,0:T(8,128)(2,1)S(1)} custom-call(s32[4]{0:T(128)S(1)} %pad_add_fusion.place, bf16[1,512]{1,0:T(2,128)(2,1)S(1)} %broadcast_select_fusion.gains, bf16[256,2048]{1,0:T(8,128)(2,1)} %g_own.1, bf16[256,2048]{1,0:T(8,128)(2,1)} %collective-permute-done.14.g_two, bf16[256,2048]{1,0:T(8,128)(2,1)} %u_own.1, ...), custom_call_target="tpu_custom_call" | custom-call | tf_op jit(solution)/shard_map/gate/pallas_call | solution.py:71
  68.2 0.6 collective-permute-start.19
  68.8 3.4 %collective-permute-start.20 = (bf16[32,2176]{1,0:T(8,128)(2,1)S(1)}, bf16[32,2176]{1,0:T(8,128)(2,1)S(1)}, u32[]{:S(2)}, u32[]{:S(2)}) collective-permute-start(bf16[32,2176]{1,0:T(8,128)(2,1)S(1)} %get-tuple-element.16), channel_id=1, source_target_pairs={{0,16},{4,20},{8,24},{12,28},{16,0},{20,4},{24,8},{28,12},{1,17},{... | collective-permute-start | bytes 417800 | tf_op jit(solution)/shard_map/ppermute | solution.py:67
  72.1 0.5 collective-permute-start.21
  72.6 1.9 %collective-permute-done.19.refs_1_ = bf16[32,2176]{1,0:T(8,128)(2,1)S(1)} collective-permute-done((bf16[32,2176]{1,0:T(8,128)(2,1)S(1)}, bf16[32,2176]{1,0:T(8,128)(2,1)S(1)}, u32[]{:S(2)}, u32[]{:S(2)}) %collective-permute-start.19) | collective-permute-done | bytes 139296 | tf_op jit(solution)/shard_map/ppermute | solution.py:67
  74.5 7.3 %collective-permute-done.20.refs_2_ = bf16[32,2176]{1,0:T(8,128)(2,1)S(1)} collective-permute-done((bf16[32,2176]{1,0:T(8,128)(2,1)S(1)}, bf16[32,2176]{1,0:T(8,128)(2,1)S(1)}, u32[]{:S(2)}, u32[]{:S(2)}) %collective-permute-start.20) | collective-permute-done | bytes 139296 | tf_op jit(solution)/shard_map/ppermute | solution.py:67
  81.8 0.1 hidden.1.refs_0_
  81.9 2.1 %collective-permute-start.22 = (bf16[32,1024]{1,0:T(8,128)(2,1)S(1)}, bf16[32,1024]{1,0:T(8,128)(2,1)S(1)}, u32[]{:S(2)}, u32[]{:S(2)}) collective-permute-start(bf16[32,1024]{1,0:T(8,128)(2,1)S(1)} %hidden.1.refs_0_), channel_id=1, source_target_pairs={{0,8},{4,12},{8,0},{12,4},{16,24},{20,28},{24,16},{28,20},{1,9},{5... | collective-permute-start | bytes 196616 | tf_op jit(solution)/shard_map/ppermute | solution.py:67
  84.1 1.1 %collective-permute-start.23 = (bf16[32,1024]{1,0:T(8,128)(2,1)S(1)}, bf16[32,1024]{1,0:T(8,128)(2,1)S(1)}, u32[]{:S(2)}, u32[]{:S(2)}) collective-permute-start(bf16[32,1024]{1,0:T(8,128)(2,1)S(1)} %hidden.1.refs_0_), channel_id=1, source_target_pairs={{0,16},{4,20},{8,24},{12,28},{16,0},{20,4},{24,8},{28,12},{1,17},{... | collective-permute-start | bytes 196616 | tf_op jit(solution)/shard_map/ppermute | solution.py:67
  85.2 1.4 %collective-permute-start.24 = (bf16[32,1024]{1,0:T(8,128)(2,1)S(1)}, bf16[32,1024]{1,0:T(8,128)(2,1)S(1)}, u32[]{:S(2)}, u32[]{:S(2)}) collective-permute-start(bf16[32,1024]{1,0:T(8,128)(2,1)S(1)} %hidden.1.refs_0_), channel_id=1, source_target_pairs={{0,24},{4,28},{8,16},{12,20},{16,8},{20,12},{24,0},{28,4},{1,25},{... | collective-permute-start | bytes 196616 | tf_op jit(solution)/shard_map/ppermute | solution.py:67
  86.5 0.5 collective-permute-start.32
  87.1 0.6 collective-permute-done.33
  87.7 0.2 collective-permute-done.32
  87.9 0.4 collective-permute-start.25
  88.3 0.2 collective-permute-start.26
  88.5 1.4 %collective-permute-done.23.refs_2_ = bf16[32,1024]{1,0:T(8,128)(2,1)S(1)} collective-permute-done((bf16[32,1024]{1,0:T(8,128)(2,1)S(1)}, bf16[32,1024]{1,0:T(8,128)(2,1)S(1)}, u32[]{:S(2)}, u32[]{:S(2)}) %collective-permute-start.23) | collective-permute-done | bytes 65568 | tf_op jit(solution)/shard_map/ppermute | solution.py:67
  89.9 1.4 %collective-permute-done.24.refs_3_ = bf16[32,1024]{1,0:T(8,128)(2,1)S(1)} collective-permute-done((bf16[32,1024]{1,0:T(8,128)(2,1)S(1)}, bf16[32,1024]{1,0:T(8,128)(2,1)S(1)}, u32[]{:S(2)}, u32[]{:S(2)}) %collective-permute-start.24) | collective-permute-done | bytes 65568 | tf_op jit(solution)/shard_map/ppermute | solution.py:67
  91.3 0.6 maximum_select_fusion.2
  92.0 0.6 collective-permute-done.28.refs_7_
  92.6 0.9 down.1
  93.5 1.7 %collective-permute-start.29 = (bf16[32,256]{1,0:T(8,128)(2,1)S(1)}, bf16[32,256]{1,0:T(8,128)(2,1)S(1)}, u32[]{:S(2)}, u32[]{:S(2)}) collective-permute-start(bf16[32,256]{1,0:T(8,128)(2,1)S(1)} %get-tuple-element.19), channel_id=1, source_target_pairs={{0,1},{1,0},{2,3},{3,2},{4,5},{5,4},{6,7},{7,6},{8,9},{9,8},{10,11... | collective-permute-start | bytes 49160 | tf_op jit(solution)/shard_map/ppermute | solution.py:67
  95.2 1.2 %collective-permute-start.30 = (bf16[32,256]{1,0:T(8,128)(2,1)S(1)}, bf16[32,256]{1,0:T(8,128)(2,1)S(1)}, u32[]{:S(2)}, u32[]{:S(2)}) collective-permute-start(bf16[32,256]{1,0:T(8,128)(2,1)S(1)} %get-tuple-element.21), channel_id=1, source_target_pairs={{0,2},{1,3},{2,0},{3,1},{4,6},{5,7},{6,4},{7,5},{8,10},{9,11},{10,... | collective-permute-start | bytes 49160 | tf_op jit(solution)/shard_map/ppermute | solution.py:67
  96.4 0.6 collective-permute-start.31
  97.0 0.6 maximum_select_fusion.1
  97.7 1.3 %collective-permute-done.30 = bf16[32,256]{1,0:T(8,128)(2,1)S(1)} collective-permute-done((bf16[32,256]{1,0:T(8,128)(2,1)S(1)}, bf16[32,256]{1,0:T(8,128)(2,1)S(1)}, u32[]{:S(2)}, u32[]{:S(2)}) %collective-permute-start.30) | collective-permute-done | bytes 16416 | tf_op jit(solution)/shard_map/ppermute | solution.py:67
  98.9 2.1 %collective-permute-done.31 = bf16[32,256]{1,0:T(8,128)(2,1)S(1)} collective-permute-done((bf16[32,256]{1,0:T(8,128)(2,1)S(1)}, bf16[32,256]{1,0:T(8,128)(2,1)S(1)}, u32[]{:S(2)}, u32[]{:S(2)}) %collective-permute-start.31) | collective-permute-done | bytes 16416 | tf_op jit(solution)/shard_map/ppermute | solution.py:67
  101.1 0.6 reshape.114
  (64 shorter events, 1.0 us)
Async XLA Ops:
  0.6 34.8 %collective-permute-start.7 = (bf16[8,256,512]{2,1,0:T(8,128)(2,1)}, bf16[8,256,512]{2,1,0:T(8,128)(2,1)}, u32[]{:S(2)}, u32[]{:S(2)}) collective-permute-start(bf16[8,256,512]{2,1,0:T(8,128)(2,1)} %keys.1), channel_id=1, source_target_pairs={{0,4},{4,0},{8,12},{12,8},{16,20},{20,16},{24,28},{28,24},{1,5},{5... | collective-permute-start | bytes 6291464 | tf_op jit(solution)/shard_map/ppermute | solution.py:67
  1.1 34.3 %collective-permute-start.8 = (bf16[8,256,512]{2,1,0:T(8,128)(2,1)}, bf16[8,256,512]{2,1,0:T(8,128)(2,1)}, u32[]{:S(2)}, u32[]{:S(2)}) collective-permute-start(bf16[8,256,512]{2,1,0:T(8,128)(2,1)} %values.1), channel_id=1, source_target_pairs={{0,4},{4,0},{8,12},{12,8},{16,20},{20,16},{24,28},{28,24},{1,5},{5... | collective-permute-start | bytes 6291464 | tf_op jit(solution)/shard_map/ppermute | solution.py:67
  2.3 3.3 %copy-start = (bf16[16032,256]{1,0:T(8,128)(2,1)S(1)}, bf16[16032,256]{1,0:T(8,128)(2,1)}, u32[]{:S(2)}) copy-start(bf16[16032,256]{1,0:T(8,128)(2,1)} %table.1) | copy-start | bytes 24625156
  5.6 10.1 %copy-start.11 = (bf16[256]{0:T(256)(128)(2,1)S(1)}, bf16[256]{0:T(256)(128)(2,1)}, u32[]{:S(2)}) copy-start(bf16[256]{0:T(256)(128)(2,1)} %param.23) | copy-start | bytes 1540
  5.6 14.5 %copy-start.3 = (bf16[256,3072]{1,0:T(8,128)(2,1)S(1)}, bf16[256,3072]{1,0:T(8,128)(2,1)}, u32[]{:S(2)}) copy-start(bf16[256,3072]{1,0:T(8,128)(2,1)} %weight.1) | copy-start | bytes 4718596
  5.6 15.4 %copy-start.5 = (bf16[2048,256]{1,0:T(8,128)(2,1)S(1)}, bf16[2048,256]{1,0:T(8,128)(2,1)}, u32[]{:S(2)}) copy-start(bf16[2048,256]{1,0:T(8,128)(2,1)} %w_own.1) | copy-start | bytes 3145732
  11.0 24.0 %copy-start.10 = (s32[8]{0:T(128)S(1)}, s32[8]{0:T(128)}, u32[]{:S(2)}) copy-start(s32[8]{0:T(128)} %param.20) | copy-start | bytes 100
  11.0 24.4 %copy-start.1 = (bf16[8,256,512]{2,1,0:T(8,128)(2,1)S(1)}, bf16[8,256,512]{2,1,0:T(8,128)(2,1)}, u32[]{:S(2)}) copy-start(bf16[8,256,512]{2,1,0:T(8,128)(2,1)} %keys.1) | copy-start | bytes 6291460
  11.0 24.4 %copy-start.8 = (s32[8]{0:T(128)S(1)}, s32[8]{0:T(128)}, u32[]{:S(2)}) copy-start(s32[8]{0:T(128)} %starts.1) | copy-start | bytes 100
  11.1 24.4 %copy-start.9 = (s32[8]{0:T(128)S(1)}, s32[8]{0:T(128)}, u32[]{:S(2)}) copy-start(s32[8]{0:T(128)} %lens.1) | copy-start | bytes 100
  11.1 4.9 %collective-permute-start = (bf16[32,256]{1,0:T(8,128)(2,1)S(1)}, bf16[32,256]{1,0:T(8,128)(2,1)S(1)}, u32[]{:S(2)}, u32[]{:S(2)}) collective-permute-start(bf16[32,256]{1,0:T(8,128)(2,1)S(1)} %get-tuple-element.24), channel_id=1, source_target_pairs={{0,1},{1,0},{2,3},{3,2},{4,5},{5,4},{6,7},{7,6},{8,9},{9,8},{10,11... | collective-permute-start | bytes 49160 | tf_op jit(solution)/shard_map/ppermute | solution.py:67
  14.2 3.7 %collective-permute-start.1 = (bf16[32,256]{1,0:T(8,128)(2,1)S(1)}, bf16[32,256]{1,0:T(8,128)(2,1)S(1)}, u32[]{:S(2)}, u32[]{:S(2)}) collective-permute-start(bf16[32,256]{1,0:T(8,128)(2,1)S(1)} %get-tuple-element.23), channel_id=1, source_target_pairs={{0,2},{1,3},{2,0},{3,1},{4,6},{5,7},{6,4},{7,5},{8,10},{9,11},{10,... | collective-permute-start | bytes 49160 | tf_op jit(solution)/shard_map/ppermute | solution.py:67
  15.5 4.6 %collective-permute-start.2 = (bf16[32,256]{1,0:T(8,128)(2,1)S(1)}, bf16[32,256]{1,0:T(8,128)(2,1)S(1)}, u32[]{:S(2)}, u32[]{:S(2)}) collective-permute-start(bf16[32,256]{1,0:T(8,128)(2,1)S(1)} %get-tuple-element.22), channel_id=1, source_target_pairs={{0,3},{1,2},{2,1},{3,0},{4,7},{5,6},{6,5},{7,4},{8,11},{9,10},{10,... | collective-permute-start | bytes 49160 | tf_op jit(solution)/shard_map/ppermute | solution.py:67
  21.0 1.4 %collective-permute-start.4 = (bf16[32,1664]{1,0:T(8,128)(2,1)S(1)}, bf16[32,1664]{1,0:T(8,128)(2,1)S(1)}, u32[]{:S(2)}, u32[]{:S(2)}) collective-permute-start(bf16[32,1664]{1,0:T(8,128)(2,1)S(1)} %get-tuple-element.11), channel_id=1, source_target_pairs={{0,4},{4,0},{8,12},{12,8},{16,20},{20,16},{24,28},{28,24},{1,5},{5... | collective-permute-start | bytes 319496 | tf_op jit(solution)/shard_map/ppermute | solution.py:67
  21.1 30.9 %collective-permute-start.11 = (bf16[2048,256]{1,0:T(8,128)(2,1)S(1)}, bf16[2048,256]{1,0:T(8,128)(2,1)}, u32[]{:S(2)}, u32[]{:S(2)}) collective-permute-start(bf16[2048,256]{1,0:T(8,128)(2,1)S(1)} %copy-done.5), channel_id=1, source_target_pairs={{0,4},{4,0},{8,12},{12,8},{16,20},{20,16},{24,28},{28,24},{1,5},{5... | collective-permute-start | bytes 3145736 | tf_op jit(solution)/shard_map/ppermute | solution.py:67
  22.5 5.1 %collective-permute-start.5 = (bf16[32,1664]{1,0:T(8,128)(2,1)S(1)}, bf16[32,1664]{1,0:T(8,128)(2,1)S(1)}, u32[]{:S(2)}, u32[]{:S(2)}) collective-permute-start(bf16[32,1664]{1,0:T(8,128)(2,1)S(1)} %add.92.a), channel_id=1, source_target_pairs={{0,8},{4,12},{8,0},{12,4},{16,24},{20,28},{24,16},{28,20},{1,9},{5... | collective-permute-start | bytes 319496 | tf_op jit(solution)/shard_map/ppermute | solution.py:67
  27.6 7.4 %collective-permute-start.6 = (bf16[32,1664]{1,0:T(8,128)(2,1)S(1)}, bf16[32,1664]{1,0:T(8,128)(2,1)S(1)}, u32[]{:S(2)}, u32[]{:S(2)}) collective-permute-start(bf16[32,1664]{1,0:T(8,128)(2,1)S(1)} %add.93.a), channel_id=1, source_target_pairs={{0,16},{4,20},{8,24},{12,28},{16,0},{20,4},{24,8},{28,12},{1,17},{... | collective-permute-start | bytes 319496 | tf_op jit(solution)/shard_map/ppermute | solution.py:67
  30.2 32.7 %collective-permute-start.14 = (bf16[256,2048]{1,0:T(8,128)(2,1)}, bf16[256,2048]{1,0:T(8,128)(2,1)}, u32[]{:S(2)}, u32[]{:S(2)}) collective-permute-start(bf16[256,2048]{1,0:T(8,128)(2,1)} %g_own.1), channel_id=1, source_target_pairs={{0,4},{4,0},{8,12},{12,8},{16,20},{20,16},{24,28},{28,24},{1,5},{5... | collective-permute-start | bytes 3145736 | tf_op jit(solution)/shard_map/ppermute | solution.py:67
  35.0 28.0 %collective-permute-start.15 = (bf16[256,2048]{1,0:T(8,128)(2,1)}, bf16[256,2048]{1,0:T(8,128)(2,1)}, u32[]{:S(2)}, u32[]{:S(2)}) collective-permute-start(bf16[256,2048]{1,0:T(8,128)(2,1)} %u_own.1), channel_id=1, source_target_pairs={{0,4},{4,0},{8,12},{12,8},{16,20},{20,16},{24,28},{28,24},{1,5},{5... | collective-permute-start | bytes 3145736 | tf_op jit(solution)/shard_map/ppermute | solution.py:67
  35.5 1.6 %copy-start.2 = (bf16[8,256,512]{2,1,0:T(8,128)(2,1)S(1)}, bf16[8,256,512]{2,1,0:T(8,128)(2,1)}, u32[]{:S(2)}) copy-start(bf16[8,256,512]{2,1,0:T(8,128)(2,1)} %values.1) | copy-start | bytes 6291460
  37.1 1.0 %copy-start.7 = (bf16[1024,256]{1,0:T(8,128)(2,1)S(1)}, bf16[1024,256]{1,0:T(8,128)(2,1)}, u32[]{:S(2)}) copy-start(bf16[1024,256]{1,0:T(8,128)(2,1)} %constant.49.clone.fold) | copy-start | bytes 1572868
  38.1 11.1 %copy-start.6 = (bf16[128,1024]{1,0:T(8,128)(2,1)S(1)}, bf16[128,1024]{1,0:T(8,128)(2,1)}, u32[]{:S(2)}) copy-start(bf16[128,1024]{1,0:T(8,128)(2,1)} %constant.50.clone.spread) | copy-start | bytes 786436
  44.5 14.0 %copy-start.12 = (bf16[256]{0:T(256)(128)(2,1)S(1)}, bf16[256]{0:T(256)(128)(2,1)}, u32[]{:S(2)}) copy-start(bf16[256]{0:T(256)(128)(2,1)} %param.24) | copy-start | bytes 1540
  44.5 4.7 %collective-permute-start.9 = (bf16[32,1152]{1,0:T(8,128)(2,1)S(1)}, bf16[32,1152]{1,0:T(8,128)(2,1)S(1)}, u32[]{:S(2)}, u32[]{:S(2)}) collective-permute-start(bf16[32,1152]{1,0:T(8,128)(2,1)S(1)} %get-tuple-element.12.a), channel_id=1, source_target_pairs={{0,8},{4,12},{8,0},{12,4},{16,24},{20,28},{24,16},{28,20},{1,9},{5... | collective-permute-start | bytes 221192 | tf_op jit(solution)/shard_map/ppermute | solution.py:67
  49.6 6.5 %collective-permute-start.10 = (bf16[32,1152]{1,0:T(8,128)(2,1)S(1)}, bf16[32,1152]{1,0:T(8,128)(2,1)S(1)}, u32[]{:S(2)}, u32[]{:S(2)}) collective-permute-start(bf16[32,1152]{1,0:T(8,128)(2,1)S(1)} %merge.1.a), channel_id=1, source_target_pairs={{0,16},{4,20},{8,24},{12,28},{16,0},{20,4},{24,8},{28,12},{1,17},{... | collective-permute-start | bytes 221192 | tf_op jit(solution)/shard_map/ppermute | solution.py:67
  58.0 1.4 %collective-permute-start.12 = (f32[32,512]{1,0:T(8,128)S(1)}, f32[32,512]{1,0:T(8,128)S(1)}, u32[]{:S(2)}, u32[]{:S(2)}) collective-permute-start(f32[32,512]{1,0:T(8,128)S(1)} %output.1), channel_id=1, source_target_pairs={{0,4},{4,0},{8,12},{12,8},{16,20},{20,16},{24,28},{28,24},{1,5},{5... | collective-permute-start | bytes 196616 | tf_op jit(solution)/shard_map/ppermute | solution.py:67
  58.0 1.3 %collective-permute-start.3 = (bf16[32,256]{1,0:T(8,128)(2,1)S(1)}, bf16[32,256]{1,0:T(8,128)(2,1)S(1)}, u32[]{:S(2)}, u32[]{:S(2)}) collective-permute-start(bf16[32,256]{1,0:T(8,128)(2,1)S(1)} %get-tuple-element.9), channel_id=1, source_target_pairs={{0,4},{4,0},{8,12},{12,8},{16,20},{20,16},{24,28},{28,24},{1,5},{5... | collective-permute-start | bytes 49160 | tf_op jit(solution)/shard_map/ppermute | solution.py:67
  58.5 2.1 %collective-permute-start.13 = (bf16[1,256]{1,0:T(2,128)(2,1)S(1)}, bf16[1,256]{1,0:T(2,128)(2,1)S(1)}, u32[]{:S(2)}, u32[]{:S(2)}) collective-permute-start(bf16[1,256]{1,0:T(2,128)(2,1)S(1)} %concatenate.64), channel_id=1, source_target_pairs={{0,4},{4,0},{8,12},{12,8},{16,20},{20,16},{24,28},{28,24},{1,5},{5... | collective-permute-start | bytes 1544 | tf_op jit(solution)/shard_map/ppermute | solution.py:67
  59.4 4.0 %collective-permute-start.16 = (bf16[32,512]{1,0:T(8,128)(2,1)S(1)}, bf16[32,512]{1,0:T(8,128)(2,1)S(1)}, u32[]{:S(2)}, u32[]{:S(2)}) collective-permute-start(bf16[32,512]{1,0:T(8,128)(2,1)S(1)} %add_convert_fusion.refs_0_), channel_id=1, source_target_pairs={{0,1},{1,0},{2,3},{3,2},{4,5},{5,4},{6,7},{7,6},{8,9},{9,8},{10,11... | collective-permute-start | bytes 98312 | tf_op jit(solution)/shard_map/ppermute | solution.py:67
  59.9 3.9 %collective-permute-start.17 = (bf16[32,512]{1,0:T(8,128)(2,1)S(1)}, bf16[32,512]{1,0:T(8,128)(2,1)S(1)}, u32[]{:S(2)}, u32[]{:S(2)}) collective-permute-start(bf16[32,512]{1,0:T(8,128)(2,1)S(1)} %add_convert_fusion.refs_0_), channel_id=1, source_target_pairs={{0,2},{1,3},{2,0},{3,1},{4,6},{5,7},{6,4},{7,5},{8,10},{9,11},{10,... | collective-permute-start | bytes 98312 | tf_op jit(solution)/shard_map/ppermute | solution.py:67
  60.6 4.8 %collective-permute-start.18 = (bf16[32,512]{1,0:T(8,128)(2,1)S(1)}, bf16[32,512]{1,0:T(8,128)(2,1)S(1)}, u32[]{:S(2)}, u32[]{:S(2)}) collective-permute-start(bf16[32,512]{1,0:T(8,128)(2,1)S(1)} %add_convert_fusion.refs_0_), channel_id=1, source_target_pairs={{0,3},{1,2},{2,1},{3,0},{4,7},{5,6},{6,5},{7,4},{8,11},{9,10},{10,... | collective-permute-start | bytes 98312 | tf_op jit(solution)/shard_map/ppermute | solution.py:67
  68.1 24.5 %copy-start.4 = (bf16[2048,256]{1,0:T(8,128)(2,1)S(1)}, bf16[2048,256]{1,0:T(8,128)(2,1)}, u32[]{:S(2)}) copy-start(bf16[2048,256]{1,0:T(8,128)(2,1)} %w_down.1) | copy-start | bytes 3145732
  68.2 6.4 %collective-permute-start.19 = (bf16[32,2176]{1,0:T(8,128)(2,1)S(1)}, bf16[32,2176]{1,0:T(8,128)(2,1)S(1)}, u32[]{:S(2)}, u32[]{:S(2)}) collective-permute-start(bf16[32,2176]{1,0:T(8,128)(2,1)S(1)} %get-tuple-element.17), channel_id=1, source_target_pairs={{0,8},{4,12},{8,0},{12,4},{16,24},{20,28},{24,16},{28,20},{1,9},{5... | collective-permute-start | bytes 417800 | tf_op jit(solution)/shard_map/ppermute | solution.py:67
  68.8 13.0 %collective-permute-start.20 = (bf16[32,2176]{1,0:T(8,128)(2,1)S(1)}, bf16[32,2176]{1,0:T(8,128)(2,1)S(1)}, u32[]{:S(2)}, u32[]{:S(2)}) collective-permute-start(bf16[32,2176]{1,0:T(8,128)(2,1)S(1)} %get-tuple-element.16), channel_id=1, source_target_pairs={{0,16},{4,20},{8,24},{12,28},{16,0},{20,4},{24,8},{28,12},{1,17},{... | collective-permute-start | bytes 417800 | tf_op jit(solution)/shard_map/ppermute | solution.py:67
  72.1 9.7 %collective-permute-start.21 = (bf16[32,2176]{1,0:T(8,128)(2,1)S(1)}, bf16[32,2176]{1,0:T(8,128)(2,1)S(1)}, u32[]{:S(2)}, u32[]{:S(2)}) collective-permute-start(bf16[32,2176]{1,0:T(8,128)(2,1)S(1)} %get-tuple-element.15), channel_id=1, source_target_pairs={{0,24},{4,28},{8,16},{12,20},{16,8},{20,12},{24,0},{28,4},{1,25},{... | collective-permute-start | bytes 417800 | tf_op jit(solution)/shard_map/ppermute | solution.py:67
  81.9 6.4 %collective-permute-start.22 = (bf16[32,1024]{1,0:T(8,128)(2,1)S(1)}, bf16[32,1024]{1,0:T(8,128)(2,1)S(1)}, u32[]{:S(2)}, u32[]{:S(2)}) collective-permute-start(bf16[32,1024]{1,0:T(8,128)(2,1)S(1)} %hidden.1.refs_0_), channel_id=1, source_target_pairs={{0,8},{4,12},{8,0},{12,4},{16,24},{20,28},{24,16},{28,20},{1,9},{5... | collective-permute-start | bytes 196616 | tf_op jit(solution)/shard_map/ppermute | solution.py:67
  84.1 5.9 %collective-permute-start.23 = (bf16[32,1024]{1,0:T(8,128)(2,1)S(1)}, bf16[32,1024]{1,0:T(8,128)(2,1)S(1)}, u32[]{:S(2)}, u32[]{:S(2)}) collective-permute-start(bf16[32,1024]{1,0:T(8,128)(2,1)S(1)} %hidden.1.refs_0_), channel_id=1, source_target_pairs={{0,16},{4,20},{8,24},{12,28},{16,0},{20,4},{24,8},{28,12},{1,17},{... | collective-permute-start | bytes 196616 | tf_op jit(solution)/shard_map/ppermute | solution.py:67
  85.2 6.2 %collective-permute-start.24 = (bf16[32,1024]{1,0:T(8,128)(2,1)S(1)}, bf16[32,1024]{1,0:T(8,128)(2,1)S(1)}, u32[]{:S(2)}, u32[]{:S(2)}) collective-permute-start(bf16[32,1024]{1,0:T(8,128)(2,1)S(1)} %hidden.1.refs_0_), channel_id=1, source_target_pairs={{0,24},{4,28},{8,16},{12,20},{16,8},{20,12},{24,0},{28,4},{1,25},{... | collective-permute-start | bytes 196616 | tf_op jit(solution)/shard_map/ppermute | solution.py:67
  86.5 1.2 %collective-permute-start.33 = (bf16[32,256]{1,0:T(8,128)(2,1)S(1)}, bf16[32,256]{1,0:T(8,128)(2,1)S(1)}, u32[]{:S(2)}, u32[]{:S(2)}) collective-permute-start(bf16[32,256]{1,0:T(8,128)(2,1)S(1)} %get-tuple-element.14), channel_id=1, source_target_pairs={{0,4},{4,0},{8,12},{12,8},{16,20},{20,16},{24,28},{28,24},{1,5},{5... | collective-permute-start | bytes 49160 | tf_op jit(solution)/shard_map/ppermute | solution.py:67
  86.5 1.3 %collective-permute-start.32 = (bf16[32,256]{1,0:T(8,128)(2,1)S(1)}, bf16[32,256]{1,0:T(8,128)(2,1)S(1)}, u32[]{:S(2)}, u32[]{:S(2)}) collective-permute-start(bf16[32,256]{1,0:T(8,128)(2,1)S(1)} %get-tuple-element.13), channel_id=1, source_target_pairs={{0,4},{4,0},{8,12},{12,8},{16,20},{20,16},{24,28},{28,24},{1,5},{5... | collective-permute-start | bytes 49160 | tf_op jit(solution)/shard_map/ppermute | solution.py:67
  87.9 4.1 %collective-permute-start.25 = (bf16[32,1024]{1,0:T(8,128)(2,1)S(1)}, bf16[32,1024]{1,0:T(8,128)(2,1)S(1)}, u32[]{:S(2)}, u32[]{:S(2)}) collective-permute-start(bf16[32,1024]{1,0:T(8,128)(2,1)S(1)} %hidden.1.refs_0_), channel_id=1, source_target_pairs={{0,4},{4,0},{8,12},{12,8},{16,20},{20,16},{24,28},{28,24},{1,5},{5... | collective-permute-start | bytes 196616 | tf_op jit(solution)/shard_map/ppermute | solution.py:67
  88.3 3.7 %collective-permute-start.26 = (bf16[32,1024]{1,0:T(8,128)(2,1)S(1)}, bf16[32,1024]{1,0:T(8,128)(2,1)S(1)}, u32[]{:S(2)}, u32[]{:S(2)}) collective-permute-start(bf16[32,1024]{1,0:T(8,128)(2,1)S(1)} %collective-permute-done.22.refs_1_), channel_id=1, source_target_pairs={{0,4},{4,0},{8,12},{12,8},{16,20},{20,16},{24,28},{28,24},{1,5},{5... | collective-permute-start | bytes 196616 | tf_op jit(solution)/shard_map/ppermute | solution.py:67
  89.9 2.1 %collective-permute-start.27 = (bf16[32,1024]{1,0:T(8,128)(2,1)S(1)}, bf16[32,1024]{1,0:T(8,128)(2,1)S(1)}, u32[]{:S(2)}, u32[]{:S(2)}) collective-permute-start(bf16[32,1024]{1,0:T(8,128)(2,1)S(1)} %collective-permute-done.23.refs_2_), channel_id=1, source_target_pairs={{0,4},{4,0},{8,12},{12,8},{16,20},{20,16},{24,28},{28,24},{1,5},{5... | collective-permute-start | bytes 196616 | tf_op jit(solution)/shard_map/ppermute | solution.py:67
  91.3 1.3 %collective-permute-start.28 = (bf16[32,1024]{1,0:T(8,128)(2,1)S(1)}, bf16[32,1024]{1,0:T(8,128)(2,1)S(1)}, u32[]{:S(2)}, u32[]{:S(2)}) collective-permute-start(bf16[32,1024]{1,0:T(8,128)(2,1)S(1)} %collective-permute-done.24.refs_3_), channel_id=1, source_target_pairs={{0,4},{4,0},{8,12},{12,8},{16,20},{20,16},{24,28},{28,24},{1,5},{5... | collective-permute-start | bytes 196616 | tf_op jit(solution)/shard_map/ppermute | solution.py:67
  93.5 4.2 %collective-permute-start.29 = (bf16[32,256]{1,0:T(8,128)(2,1)S(1)}, bf16[32,256]{1,0:T(8,128)(2,1)S(1)}, u32[]{:S(2)}, u32[]{:S(2)}) collective-permute-start(bf16[32,256]{1,0:T(8,128)(2,1)S(1)} %get-tuple-element.19), channel_id=1, source_target_pairs={{0,1},{1,0},{2,3},{3,2},{4,5},{5,4},{6,7},{7,6},{8,9},{9,8},{10,11... | collective-permute-start | bytes 49160 | tf_op jit(solution)/shard_map/ppermute | solution.py:67
  95.2 3.7 %collective-permute-start.30 = (bf16[32,256]{1,0:T(8,128)(2,1)S(1)}, bf16[32,256]{1,0:T(8,128)(2,1)S(1)}, u32[]{:S(2)}, u32[]{:S(2)}) collective-permute-start(bf16[32,256]{1,0:T(8,128)(2,1)S(1)} %get-tuple-element.21), channel_id=1, source_target_pairs={{0,2},{1,3},{2,0},{3,1},{4,6},{5,7},{6,4},{7,5},{8,10},{9,11},{10,... | collective-permute-start | bytes 49160 | tf_op jit(solution)/shard_map/ppermute | solution.py:67
  96.4 4.6 %collective-permute-start.31 = (bf16[32,256]{1,0:T(8,128)(2,1)S(1)}, bf16[32,256]{1,0:T(8,128)(2,1)S(1)}, u32[]{:S(2)}, u32[]{:S(2)}) collective-permute-start(bf16[32,256]{1,0:T(8,128)(2,1)S(1)} %get-tuple-element.20), channel_id=1, source_target_pairs={{0,3},{1,2},{2,1},{3,0},{4,7},{5,6},{6,5},{7,4},{8,11},{9,10},{10,... | collective-permute-start | bytes 49160 | tf_op jit(solution)/shard_map/ppermute | solution.py:67

commit v2 on v1

v2 whole, which is shorter than its diff:
```python
import functools
import math

import jax
import jax.numpy as jnp
import numpy as np
from jax import lax
from jax.experimental import pallas as pl
from jax.experimental.pallas import tpu as pltpu
from jax.sharding import PartitionSpec as P

D = 2048
QUERY_HEADS = 32
KEY_VALUE_HEADS = 8
HEAD_SIZE = 64
GROUP = QUERY_HEADS // KEY_VALUE_HEADS
EPSILON = 1e-05
ROPE_BASE = 500000.0

HEADS = QUERY_HEADS // 2
KV_HEADS = KEY_VALUE_HEADS // 2
QW = HEADS * HEAD_SIZE
KW = KV_HEADS * HEAD_SIZE
HALF = QW + 2 * KW
LANES = 128
WIDE = HALF + LANES
LOW = -1e30

BF16 = jnp.bfloat16
F32 = jnp.float32
SMEM = pl.BlockSpec(memory_space=pltpu.SMEM)
VMEM = pl.BlockSpec(memory_space=pltpu.VMEM)
HBM = pl.BlockSpec(memory_space=pltpu.HBM)


def mm(a, b):
    return lax.dot_general(a, b, (((1,), (0,)), ((), ())), preferred_element_type=F32)


def mm_t(a, b):
    return lax.dot_general(a, b, (((1,), (1,)), ((), ())), preferred_element_type=F32)


def lane_iota(shape):
    return lax.broadcasted_iota(jnp.int32, shape, len(shape) - 1)


def split(value):
    high = value.astype(BF16).astype(F32)
    low = (value - high).astype(BF16).astype(F32)
    return high, low


def tail_of(value):
    high, low = split(value)
    lane = lane_iota((value.shape[0], LANES))
    return jnp.where(lane == 0, high, jnp.where(lane == 1, low, 0.0))


def tail_sum(*tails):
    return tree([jnp.sum(tail.astype(F32), axis=-1, keepdims=True) for tail in tails])


def exchange(array, axis, size, mask):
    return lax.ppermute(array, axis, [(i, i ^ mask) for i in range(size)])


WIDE_ORDER, NARROW_ORDER = (3, 1, 2), (2, 1, 3)
LIMIT, LOOKUP_LIMIT, STAGE_LIMIT = 16, 53, 40


def direct(array, size, send, order):
    pick = (lambda k: array[k]) if isinstance(array, list) else (lambda k: array)
    order = [k for k in order if k < size] + [k for k in range(1, size) if k not in order]
    got = {k: send(pick(k), k) for k in order}
    return [pick(0)] + [got[k] for k in range(1, size)]


def call(kernel, outs, ins, specs, scratch=(), limit=LIMIT, cost=None, name=None):
    return pl.pallas_call(
        kernel,
        out_shape=outs,
        in_specs=specs,
        out_specs=jax.tree.map(lambda _: VMEM, outs),
        scratch_shapes=list(scratch),
        compiler_params=pltpu.CompilerParams(vmem_limit_bytes=limit << 20),
        cost_estimate=cost,
        name=name,
    )(*ins)


def work(moved):
    return pl.CostEstimate(flops=0, transcendentals=0, bytes_accessed=moved)


def shape(dims, dtype):
    return jax.ShapeDtypeStruct(tuple(dims), dtype)


def lookup_kernel(rows, place, ids, table, out, blocks, taken, listed, sem):
    req_count, count = out.shape[0], out.shape[1]
    steps = ids.shape[0]
    vocab_dev, feat = table.shape
    me = place[2]
    base = me * vocab_dev
    found = jnp.int32(0)
    for j in range(req_count * count):
        local = ids[j % steps, j // steps] - base
        listed[0, found] = j
        listed[1, found] = local
        found = found + ((local >= 0) & (local < vocab_dev)).astype(jnp.int32)

    def block_of(i):
        local = listed[1, i]
        first = jnp.minimum(local & -rows, vocab_dev - rows)
        return local - first, pltpu.make_async_copy(
            table.at[pl.ds(pl.multiple_of(first, 8), rows)], blocks.at[i], sem
        )

    @pl.loop(0, found)
    def _(i):
        block_of(i)[1].start()

    taken[...] = jnp.zeros(taken.shape, F32)
    at = lax.broadcasted_iota(jnp.int32, (rows, feat), 0)

    @pl.loop(0, found)
    def _(i):
        block_of(i)[1].wait()

    total = req_count * count
    batch = 8

    @pl.loop(0, lax.div(found + batch - 1, batch))
    def _(b):
        for u in range(batch):
            i = b * batch + u
            live = i < found
            j = jnp.where(live, listed[0, i], 0)
            local = jnp.where(live, listed[1, i], 0)
            row = jnp.where(live, local - jnp.minimum(local & -rows, vocab_dev - rows), -1)
            group = lax.div(j, count)
            to = jnp.where(live, (group ^ me) * count + (j - group * count), total)
            picked = jnp.where(at == row, blocks[i].astype(F32), 0.0)
            taken[pl.ds(to, 1), :] = jnp.sum(picked, axis=0, keepdims=True)

    out[...] = taken[:total, :].astype(BF16).reshape(out.shape)


def tables_kernel(when, cosine, sine):
    half = HEAD_SIZE // 2
    lane = lane_iota(cosine.shape)
    freqs = jnp.exp((lane % half).astype(F32) * (-2.0 / HEAD_SIZE * math.log(ROPE_BASE)))
    angles = when[...] * freqs
    cosine[...] = jnp.cos(angles)
    sine[...] = jnp.where(lane % HEAD_SIZE < half, -1.0, 1.0) * jnp.sin(angles)


def run_copies(copies, sems):
    copies = [pltpu.make_async_copy(a, b, sems.at[i]) for i, (a, b) in enumerate(copies)]
    for copy in copies:
        copy.start()
    for copy in copies:
        copy.wait()


def stage_cache_kernel(place, keys, keys2, values, values2, k_out, v_out, sems):
    requests, context = keys.shape[0], keys.shape[1]
    columns = pl.ds(pl.multiple_of(place[0] * KW, KW), KW)
    run_copies(
        [
            (array.at[r, :, columns], out.at[r, pl.ds(i * context, context), :])
            for r in range(requests)
            for out, arrays in ((k_out, (keys, keys2)), (v_out, (values, values2)))
            for i, array in enumerate(arrays)
        ],
        sems,
    )


def stage_gate_kernel(place, g_own, g_two, u_own, u_two, g_out, u_out, sems):
    feat, hid = g_own.shape[0], g_out.shape[1]
    columns = pl.ds(pl.multiple_of(place[0] * hid, LANES), hid)
    pieces = 4
    part = feat // pieces
    run_copies(
        [
            (array.at[pl.ds(p * part, part), columns], out.at[pl.ds(to * feat + p * part, part), :])
            for out, arrays in ((g_out, (g_own, g_two)), (u_out, (u_own, u_two)))
            for array, to in zip(arrays, (place[0], 1 - place[0]))
            for p in range(pieces)
        ],
        sems,
    )


def stage_out_kernel(place, o_own, o_two, k, v, kv_two, o_out, k_out, v_out, sems):
    feat = o_own.shape[1]
    pieces = 4
    part = QW // pieces
    copies = [
        pltpu.make_async_copy(
            array.at[pl.ds(pl.multiple_of(place[0] * QW + p * part, part), part), :],
            o_out.at[pl.ds(p * part, part), pl.ds(pl.multiple_of(to * feat, LANES), feat)],
            sems.at[i * pieces + p],
        )
        for i, (array, to) in enumerate(((o_own, place[0]), (o_two, 1 - place[0])))
        for p in range(pieces)
    ]
    for copy in copies:
        copy.start()
    first = place[0] == 0
    for out, own, two in ((k_out, k, kv_two[:, :KW]), (v_out, v, kv_two[:, KW:])):
        own = own[...]
        pair = jnp.concatenate([jnp.where(first, own, two), jnp.where(first, two, own)], axis=1)
        out[...] = pair.reshape(out.shape)
    for copy in copies:
        copy.wait()


def project_kernel(parts, place, gain, next_gain, weight, *refs):
    blocks, (x_out, keep, give) = refs[:parts], refs[parts:]
    x = blocks[0][...].astype(F32)
    for block in blocks[1:]:
        x = x + block[...].astype(F32)
    x_out[...] = x.astype(BF16)
    scaled = (x * gain[...].astype(F32)).astype(BF16)
    tail = tail_of(jnp.sum(x * x, axis=-1, keepdims=True)).astype(BF16)
    first = place[0] == 0
    q_end, k_end = 2 * QW, 2 * QW + 2 * KW
    at = 0
    for start, width in ((0, QW), (q_end, KW), (k_end, KW)):
        one = mm(scaled, weight[:, start : start + width])
        two = mm(scaled, weight[:, start + width : start + 2 * width])
        keep[:, at : at + width] = jnp.where(first, one, two).astype(BF16)
        give[:, at : at + width] = jnp.where(first, two, one).astype(BF16)
        at += width
    keep[:, HALF:] = tail
    give[:, HALF:WIDE] = tail
    feat = x.shape[1]
    give[:, WIDE : WIDE + feat] = x.astype(BF16)
    give[:, WIDE + feat :] = jnp.broadcast_to(next_gain[...], x.shape)


def tree(values):
    while len(values) > 1:
        values = [values[i] + values[i + 1] for i in range(0, len(values), 2)]
    return values[0]


def add_kernel(a, b, out):
    out[:, :HALF] = (a[:, :HALF].astype(F32) + b[:, :HALF].astype(F32)).astype(BF16)
    out[:, HALF:] = tail_of(tail_sum(a[:, HALF:], b[:, HALF:WIDE])).astype(BF16)


def rotate(v, cosine, sine):
    width = v.shape[-1]
    lane = lane_iota(v.shape)
    half = HEAD_SIZE // 2
    ahead = pltpu.roll(v, width - half, 1)
    behind = pltpu.roll(v, half, 1)
    other = jnp.where(lane % HEAD_SIZE < half, ahead, behind)
    reps = width // LANES
    cosine = jnp.concatenate([cosine] * reps, axis=1)
    sine = jnp.concatenate([sine] * reps, axis=1)
    return v * cosine + other * sine


def attend_kernel(
    steps, parts, place, starts, lens, cosine, sine, fold, keys, values, *refs
):
    sums, (packed, new_k, new_v, out_rows, stats) = refs[:parts], refs[parts:]
    count = packed.shape[0]
    requests = count // steps
    rows = steps * HEADS
    context = keys.shape[1] // 2
    z, me = place[1], place[3]
    total = tree([block[:, :HALF].astype(F32) for block in sums])
    squares = tail_sum(*[block[:, HALF:] for block in sums])
    total = total * lax.rsqrt(squares / D + EPSILON)
    q = rotate(total[:, :QW], cosine[...], sine[...]).astype(BF16)
    k = rotate(total[:, QW : QW + KW], cosine[...], sine[...]).astype(BF16)
    v = total[:, QW + KW :].astype(BF16)
    new_k[...] = k
    new_v[...] = v

    head = lax.broadcasted_iota(jnp.int32, (count, HEADS, QW), 1)
    lane = lax.broadcasted_iota(jnp.int32, (count, HEADS, QW), 2)
    own_head = lane // HEAD_SIZE == head
    wide = jnp.where(own_head, q.astype(F32)[:, None, :], 0.0).astype(BF16)
    q_rows = mm(wide.reshape(count * HEADS, QW), fold[...]).astype(BF16)

    scale = 1.0 / math.sqrt(HEAD_SIZE)
    fresh_all = mm_t(q_rows, k) * scale
    spot = lax.broadcasted_iota(jnp.int32, (1, 2 * context), 1)
    spot = jnp.where(spot < context, spot + me * context, spot - context + (me ^ 1) * context)
    row_head = lax.broadcasted_iota(jnp.int32, (rows, KW), 0) % HEADS
    own_kv = lane_iota((rows, KW)) // HEAD_SIZE == row_head // GROUP
    row_step = lax.broadcasted_iota(jnp.int32, (rows, count), 0) // HEADS
    fresh_at = lane_iota((rows, count))
    stat_lane = lane_iota((rows, LANES))
    stat_head = lax.broadcasted_iota(jnp.int32, (rows, LANES), 0) % HEADS
    for r in range(requests):
        qr = q_rows[r * rows : (r + 1) * rows]
        lo, hi = starts[r], lens[r]
        seen = (spot >= lo) & (spot < hi)
        seen_f = (fresh_at >= r * steps) & (fresh_at <= r * steps + row_step) & (z == 0)
        sc = jnp.where(seen, mm_t(qr, keys[r]) * scale, LOW)
        sf = jnp.where(seen_f, fresh_all[r * rows : (r + 1) * rows], LOW)
        top = jnp.maximum(jnp.max(sc, axis=-1, keepdims=True), jnp.max(sf, axis=-1, keepdims=True))
        top_high, top_low = split(top)
        top = top_high + top_low
        pc = jnp.where(seen, jnp.exp(sc - top), 0.0)
        pf = jnp.where(seen_f, jnp.exp(sf - top), 0.0)
        weight = jnp.sum(pc, axis=-1, keepdims=True) + jnp.sum(pf, axis=-1, keepdims=True)
        o = mm(pc.astype(BF16), values[r]) + mm(pf.astype(BF16), v)
        out_rows[r * rows : (r + 1) * rows, :] = jnp.where(own_kv, o, 0.0).astype(BF16)
        w_high, w_low = split(weight)
        stat = jnp.where(stat_lane == stat_head, top_high, 0.0)
        stat = jnp.where(stat_lane == stat_head + HEADS, top_low, stat)
        stat = jnp.where(stat_lane == stat_head + 2 * HEADS, w_high, stat)
        stat = jnp.where(stat_lane == stat_head + 3 * HEADS, w_low, stat)
        stats[r * rows : (r + 1) * rows, :] = stat
    spread = mm_t(out_rows[...], fold[...]).reshape(count, HEADS, QW)
    packed[:, :QW] = jnp.sum(jnp.where(own_head, spread, 0.0), axis=1).astype(BF16)
    packed[:, QW:] = jnp.sum(stats[...].reshape(count, HEADS, LANES), axis=1).astype(BF16)


def read_stats(block):
    block = block.astype(F32)
    both = block + pltpu.roll(block, LANES - HEADS, 1)
    return both, pltpu.roll(both, LANES - 2 * HEADS, 1)


def widen(column_block, spread):
    lane = lane_iota(column_block.shape)
    high, low = split(column_block)
    pair = jnp.where(lane < HEADS, high, jnp.where(lane < 2 * HEADS, pltpu.roll(low, HEADS, 1), 0.0))
    return mm(pair.astype(BF16), spread[...])


def output_kernel(parts, spread, weight, *refs):
    blocks, out = refs[:parts], refs[parts]
    stats = [read_stats(block[:, QW:]) for block in blocks]
    top = functools.reduce(jnp.maximum, [stat[0] for stat in stats])
    factors = [jnp.exp(stat[0] - top) for stat in stats]
    total = sum(stat[1] * factor for stat, factor in zip(stats, factors))
    inverse = 1.0 / jnp.where(lane_iota(top.shape) < HEADS, total, 1.0)
    wide = sum(
        widen(factor * inverse, spread) * block[:, :QW].astype(F32)
        for factor, block in zip(factors, blocks)
    )
    out[...] = mm(wide.astype(BF16), weight[...])


def gate_kernel(parts, place, gains, w_gate, w_up, *refs):
    blocks, (out, rows_ref) = refs[:parts], refs[parts:]
    count = blocks[0].shape[0]
    for i, block in enumerate(blocks):
        rows_ref[i * count : (i + 1) * count, :] = block[...]
    z = place[1]
    chunks, size = out.shape[0], out.shape[1]
    taken = [
        rows_ref[pl.ds(pl.multiple_of((z ^ j) * size, size), size), :].astype(F32)
        for j in range(chunks)
    ]
    x = jnp.concatenate(taken, axis=0)
    squares = jnp.sum(x * x, axis=-1, keepdims=True)
    scaled = (x * gains[...].astype(F32)).astype(BF16)
    hid = w_gate.shape[1]
    gate, up = mm(scaled, w_gate[...]), mm(scaled, w_up[...])
    tail = tail_of(squares)
    for j in range(chunks):
        at = slice(j * size, (j + 1) * size)
        out[j, :, :hid] = gate[at].astype(BF16)
        out[j, :, hid : 2 * hid] = up[at].astype(BF16)
        out[j, :, 2 * hid :] = tail[at].astype(BF16)


def hidden_kernel(parts, *refs):
    blocks, out = refs[:parts], refs[parts]
    hid = out.shape[1]
    total = blocks[0][:, : 2 * hid].astype(F32)
    for block in blocks[1:]:
        total = total + block[:, : 2 * hid].astype(F32)
    squares = tail_sum(*[block[:, 2 * hid :] for block in blocks])
    inverse = lax.rsqrt(squares / D + EPSILON)
    gate, up = total[:, :hid] * inverse, total[:, hid:] * inverse
    out[...] = (gate / (1.0 + jnp.exp(-gate)) * up).astype(BF16)


def down_kernel(parts, place, w_down, *refs):
    mine, theirs, (out, rows_ref) = refs[:parts], refs[parts : 2 * parts], refs[2 * parts :]
    core, z = place[0], place[1]
    size, hid = mine[0].shape
    near = jnp.concatenate([ref[...] for ref in mine], axis=0)
    far = jnp.concatenate([ref[...] for ref in theirs], axis=0)
    total = mm(near, w_down[pl.ds(pl.multiple_of(core * hid, hid), hid), :]) + mm(
        far, w_down[pl.ds(pl.multiple_of((1 - core) * hid, hid), hid), :]
    )
    for j in range(parts):
        rows_ref[pl.ds(pl.multiple_of((z ^ j) * size, size), size), :] = total[
            j * size : (j + 1) * size
        ]
    count = out.shape[1]
    for k in range(out.shape[0]):
        out[k] = rows_ref[k * count : (k + 1) * count, :].astype(BF16)


def shards(
    seq_size,
    req_size,
    token_ids,
    embed_table,
    cache_len,
    range_start,
    positions,
    cached_key_rows,
    cached_value_rows,
    attn_gain,
    mlp_gain,
    w_qkv,
    w_out,
    w_gate,
    w_up,
    w_down,
):
    requests, steps = cache_len.shape[0], token_ids.shape[1]
    count = requests * steps
    feat = embed_table.shape[1]
    seq_index, req_index = lax.axis_index("seq"), lax.axis_index("req")
    core, z = seq_index % 2, seq_index // 2
    depth = seq_size // 2
    place = jnp.stack([core, z, req_index, seq_index]).astype(jnp.int32)
    swap = lambda array: exchange(array, "seq", seq_size, 1)
    over_z = lambda array, mask: exchange(array, "seq", seq_size, 2 * mask)
    over_req = lambda array, mask: exchange(array, "req", req_size, mask)

    rows = 16
    found = call(
        functools.partial(lookup_kernel, rows),
        shape((req_size, count, feat), BF16),
        (place, token_ids.T, embed_table),
        [SMEM, SMEM, HBM],
        [
            pltpu.VMEM((req_size * count, rows, feat), BF16),
            pltpu.VMEM((req_size * count + 8, feat), F32),
            pltpu.SMEM((2, req_size * count + 1), jnp.int32),
            pltpu.SemaphoreType.DMA,
        ],
        limit=LOOKUP_LIMIT,
        name="lookup",
    )
    blocks = [found[0]] + [over_req(found[k], k) for k in range(1, req_size)]

    hid = w_gate.shape[1] // 2
    context = cached_key_rows.shape[1]
    keys2, values2 = swap(cached_key_rows), swap(cached_value_rows)
    *blocks, keys2, values2 = lax.optimization_barrier((*blocks, keys2, values2))
    next_gain = mlp_gain.reshape(1, feat)
    when = (positions[:, None] + jnp.arange(steps, dtype=jnp.int32)[None, :]).astype(F32)
    cosine, sine = call(
        tables_kernel,
        (shape((count, LANES), F32),) * 2,
        (when.reshape(count, 1),),
        [VMEM],
        cost=work(1 << 20),
        name="tables",
    )

    x, keep, give = call(
        functools.partial(project_kernel, req_size),
        (
            shape((count, feat), BF16),
            shape((count, WIDE), BF16),
            shape((count, WIDE + 2 * feat), BF16),
        ),
        (place, attn_gain.reshape(1, feat), next_gain, w_qkv, *blocks),
        [SMEM] + [VMEM] * (3 + req_size),
        name="project",
    )
    got = swap(give)
    mine = call(add_kernel, shape((count, WIDE), BF16), (keep, got), [VMEM] * 2, name="add")
    sums = direct(mine, depth, over_z, WIDE_ORDER)
    _, w_gate, w_up = lax.optimization_barrier((mine, w_gate, w_up))
    gate2, up2 = swap(w_gate), swap(w_up)
    keys, values = call(
        stage_cache_kernel,
        (shape((requests, 2 * context, KW), BF16),) * 2,
        (place, cached_key_rows, keys2, cached_value_rows, values2),
        [SMEM] + [HBM] * 4,
        [pltpu.SemaphoreType.DMA((4 * requests,))],
        cost=work(8 * requests * context * KW * 2),
        limit=STAGE_LIMIT,
        name="stage_cache",
    )
    *sums, keys, values, gate2, up2 = lax.optimization_barrier((*sums, keys, values, gate2, up2))

    head_lane, kv_lane = np.arange(QW)[:, None], np.arange(KW)[None, :]
    fold = jnp.asarray(
        (head_lane % HEAD_SIZE == kv_lane % HEAD_SIZE)
        & (head_lane // (GROUP * HEAD_SIZE) == kv_lane // HEAD_SIZE),
        BF16,
    )
    spread = jnp.asarray(
        (np.arange(LANES)[:, None] % HEADS == np.arange(QW)[None, :] // HEAD_SIZE)
        & (np.arange(LANES)[:, None] < 2 * HEADS),
        BF16,
    )
    packed_width = QW + LANES
    packed, new_k, new_v = call(
        functools.partial(attend_kernel, steps, depth),
        (shape((count, packed_width), BF16), shape((count, KW), BF16), shape((count, KW), BF16)),
        (place, range_start, cache_len, cosine, sine, fold, keys, values, *sums),
        [SMEM] * 3 + [VMEM] * (5 + depth),
        [pltpu.VMEM((count * HEADS, KW), BF16), pltpu.VMEM((count * HEADS, LANES), F32)],
        name="attend",
    )
    partials = direct(packed, depth, over_z, NARROW_ORDER)
    _, w_out, new_k, new_v = lax.optimization_barrier((packed, w_out, new_k, new_v))
    o_pair, all_k, all_v = call(
        stage_out_kernel,
        (shape((QW, 2 * feat), BF16),) + (shape((requests, steps, 2 * KW), BF16),) * 2,
        (place, w_out, swap(w_out), new_k, new_v, swap(jnp.concatenate([new_k, new_v], axis=1))),
        [SMEM] + [HBM] * 2 + [VMEM] * 3,
        [pltpu.SemaphoreType.DMA((8,))],
        cost=work(4 * feat * QW * 2),
        limit=STAGE_LIMIT,
        name="stage_out",
    )
    g_pair, u_pair = call(
        stage_gate_kernel,
        (shape((2 * feat, hid), BF16),) * 2,
        (place, w_gate, gate2, w_up, up2),
        [SMEM] + [HBM] * 4,
        [pltpu.SemaphoreType.DMA((16,))],
        cost=work(8 * feat * hid * 2),
        limit=STAGE_LIMIT,
        name="stage_gate",
    )
    *partials, o_pair, g_pair, u_pair = lax.optimization_barrier((*partials, o_pair, g_pair, u_pair))
    part = call(
        functools.partial(output_kernel, depth),
        shape((count, 2 * feat), F32),
        (spread, o_pair, *partials),
        [VMEM] * (2 + depth),
        name="output",
    )
    pair = lambda own, two: jnp.where(
        core == 0, jnp.concatenate([own, two], axis=1), jnp.concatenate([two, own], axis=1)
    )
    x_pair = pair(x, got[:, WIDE : WIDE + feat])
    gain_pair = pair(next_gain, got[0:1, WIDE + feat :])
    resid = (x_pair.astype(F32) + (part + swap(part))).astype(BF16)

    taken = direct(resid, req_size, over_req, ())
    size = req_size * count // depth
    terms = call(
        functools.partial(gate_kernel, req_size),
        shape((depth, size, 2 * hid + LANES), BF16),
        (place, gain_pair, g_pair, u_pair, *taken),
        [SMEM] + [VMEM] * (3 + req_size),
        [pltpu.VMEM((req_size * count, 2 * feat), BF16)],
        name="gate",
    )
    sums = direct([terms[j] for j in range(depth)], depth, over_z, WIDE_ORDER)
    hidden = call(
        functools.partial(hidden_kernel, depth),
        shape((size, hid), BF16),
        sums,
        [VMEM] * depth,
        name="hidden",
    )
    near = direct(hidden, depth, over_z, NARROW_ORDER)
    far = [swap(block) for block in near]
    back = call(
        functools.partial(down_kernel, depth),
        shape((req_size, count, feat), BF16),
        (place, w_down, *near, *far),
        [SMEM] + [VMEM] * (1 + 2 * depth),
        [pltpu.VMEM((req_size * count, feat), F32)],
        name="down",
    )
    total = sum(
        block.astype(F32)
        for block in direct([back[k] for k in range(req_size)], req_size, over_req, ())
    )
    resid_own = lax.dynamic_slice_in_dim(resid, core * feat, feat, axis=1)
    layer_out = (resid_own.astype(F32) + total).astype(BF16).reshape(requests, steps, feat)
    return layer_out, all_k, all_v


def solution(mesh):
    in_specs = (
        P(),
        P("req", "seq"),
        P("req"),
        P("req"),
        P("req"),
        P("req", "seq", None),
        P("req", "seq", None),
        P("seq"),
        P("seq"),
        P("seq", None),
        P(None, "seq"),
        P("seq", "req"),
        P("seq", "req"),
        P("req", "seq"),
    )
    out_specs = (P("req", None, "seq"), P("req", None, None), P("req", None, None))
    body = functools.partial(shards, mesh.shape["seq"], mesh.shape["req"])
    return jax.shard_map(body, mesh=mesh, in_specs=in_specs, out_specs=out_specs, check_vma=False)
```

time: 102 us -> 84.7 us (0.83)
  waiting for transfers between devices: 41.6 us -> 31.1 us
  local copies, waits for them, and re-layouts: 7.76 us -> 3.09 us
  other arithmetic: 1.71 us -> 0.19 us
    ppermute x34 -> x33, waiting for transfers between devices: 41.6 us -> 31.1 us  [exchange(): return lax.ppermute(array, axis, [(i, i ^ mask) for i in range(size)])]
    unnamed x27 -> x28, local copies, waits for them, and re-layouts: 6.77 us -> 2.33 us
    select_n x3 -> x1, other arithmetic: 1.28 us -> 0.01 us  [shards(): jnp.where(core == 0, jnp.concatenate([own, two], axis=1), jnp.concatenate...]
    ppermute x34 -> x33, starting transfers between devices: 31 us -> 30.4 us  [exchange(): return lax.ppermute(array, axis, [(i, i ^ mask) for i in range(size)])]
    pallas_call x10 -> x12, Pallas kernels: 18.7 us -> 18.6 us  [call(): pl.pallas_call(kernel, out_shape=outs, in_specs=specs, out_specs=jax.tree...]
  transfers between devices with their start and end apart: 34 -> 33, of which waited for: 21 -> 19; matrix products, arithmetic and copies ran while one was open for 3% -> 0% of each run, Pallas kernels for 15% -> 11%
where the time goes in v2:
time: 84.7 us; the launch traced here: 84.3 us
  waiting for transfers between devices  31.1 us (37%)
  starting transfers between devices  30.4 us (36%)
  Pallas kernels  18.6 us (22%)
  local copies, waits for them, and re-layouts  3.09 us (4%)
  between operations  0.94 us (1%)
    ppermute x33, waiting for transfers between devices, exchange(): return lax.ppermute(array, axis, [(i, i ^ mask) for i in range(size)])  31.1 us
    ppermute x33, starting transfers between devices, exchange(): return lax.ppermute(array, axis, [(i, i ^ mask) for i in range(size)])  30.4 us
    pallas_call x12, Pallas kernels, call(): pl.pallas_call(kernel, out_shape=outs, in_specs=specs, out_specs=jax.tree...  18.6 us
    unnamed x28, local copies, waits for them, and re-layouts  2.33 us
  transfers between devices with their start and end apart: 33, of which 19 were waited for; matrix products, arithmetic and copies ran while one was open for 0% of the time, Pallas kernels for 11%

profile of v2, /device:TPU:0, one launch (start us, length us, event | category | flops | bytes accessed | tf_op | source)
XLA Modules:
  0.0 84.3 jit_solution(9411943041055477015)
XLA Ops:
  0.6 0.5 collective-permute-start.3
  1.1 0.1 collective-permute-start.4
  1.2 0.1 pad_add_fusion.place
  1.3 0.7 copy-done.8
  2.0 3.3 %lookup.1 = bf16[4,32,256]{2,1,0:T(8,128)(2,1)S(1)} custom-call(s32[4]{0:T(128)S(1)} %pad_add_fusion.place, s32[4,32]{1,0:T(4,128)S(1)} %bitcast.32, bf16[16032,256]{1,0:T(8,128)(2,1)} %table.1), custom_call_target="tpu_custom_call" | custom-call | tf_op jit(solution)/shard_map/lookup/pallas_call | solution.py:80
  5.3 3.1 %collective-permute-start.2 = (bf16[32,256]{1,0:T(8,128)(2,1)S(1)}, bf16[32,256]{1,0:T(8,128)(2,1)S(1)}, u32[]{:S(2)}, u32[]{:S(2)}) collective-permute-start(bf16[32,256]{1,0:T(8,128)(2,1)S(1)} %get-tuple-element.92), channel_id=1, source_target_pairs={{0,3},{1,2},{2,1},{3,0},{4,7},{5,6},{6,5},{7,4},{8,11},{9,10},{10,... | collective-permute-start | bytes 49160 | tf_op jit(solution)/shard_map/ppermute | solution.py:65
  8.4 0.5 collective-permute-start.1
  8.9 0.1 collective-permute-start
  9.1 1.1 %collective-permute-done.2.refs_3_ = bf16[32,256]{1,0:T(8,128)(2,1)S(1)} collective-permute-done((bf16[32,256]{1,0:T(8,128)(2,1)S(1)}, bf16[32,256]{1,0:T(8,128)(2,1)S(1)}, u32[]{:S(2)}, u32[]{:S(2)}) %collective-permute-start.2) | collective-permute-done | bytes 16416 | tf_op jit(solution)/shard_map/ppermute | solution.py:65
  10.1 2.0 %collective-permute-done.1.refs_2_ = bf16[32,256]{1,0:T(8,128)(2,1)S(1)} collective-permute-done((bf16[32,256]{1,0:T(8,128)(2,1)S(1)}, bf16[32,256]{1,0:T(8,128)(2,1)S(1)}, u32[]{:S(2)}, u32[]{:S(2)}) %collective-permute-start.1) | collective-permute-done | bytes 16416 | tf_op jit(solution)/shard_map/ppermute | solution.py:65
  12.1 0.5 collective-permute-done.refs_1_
  12.7 0.9 %project.1 = (bf16[32,256]{1,0:T(8,128)(2,1)S(1)}, bf16[32,1664]{1,0:T(8,128)(2,1)S(1)}, bf16[32,2176]{1,0:T(8,128)(2,1)S(1)}) custom-call(s32[4]{0:T(128)S(1)} %pad_add_fusion.place, bf16[1,256]{1,0:T(2,128)(2,1)S(1)} %reshape.105.gain, bf16[1,256]{1,0:T(2,128)(2,1)S(1)} %reshape.106.next_gain, bf16[256,3072]{1,0:T(8,128)(2,1)S(1)} %copy-done.2, ...), custom_call_target="tpu_custom_call" | custom-call | tf_op jit(solution)/shard_map/project/pallas_call | solution.py:80
  13.6 0.0 collective-permute-start.5
  13.6 1.3 %collective-permute-done.5.b = bf16[32,2176]{1,0:T(8,128)(2,1)S(1)} collective-permute-done((bf16[32,2176]{1,0:T(8,128)(2,1)S(1)}, bf16[32,2176]{1,0:T(8,128)(2,1)S(1)}, u32[]{:S(2)}, u32[]{:S(2)}) %collective-permute-start.5) | collective-permute-done | bytes 139296 | tf_op jit(solution)/shard_map/ppermute | solution.py:65
  15.0 0.1 add.94.refs_0_
  15.1 0.0 copy-done.3
  15.1 0.2 collective-permute-start.9
  15.3 0.4 collective-permute-start.10
  15.7 3.6 %collective-permute-start.8 = (bf16[32,1664]{1,0:T(8,128)(2,1)S(1)}, bf16[32,1664]{1,0:T(8,128)(2,1)S(1)}, u32[]{:S(2)}, u32[]{:S(2)}) collective-permute-start(bf16[32,1664]{1,0:T(8,128)(2,1)S(1)} %add.94.refs_0_), channel_id=1, source_target_pairs={{0,24},{4,28},{8,16},{12,20},{16,8},{20,12},{24,0},{28,4},{1,25},{... | collective-permute-start | bytes 319496 | tf_op jit(solution)/shard_map/ppermute | solution.py:65
  19.3 0.8 collective-permute-start.6
  20.1 0.1 add_convert_fusion.1
  20.1 0.1 convert_element_type.52.when
  20.2 0.1 tables.1
  20.4 1.6 %copy-done.1 = bf16[8,256,512]{2,1,0:T(8,128)(2,1)S(1)} copy-done((bf16[8,256,512]{2,1,0:T(8,128)(2,1)S(1)}, bf16[8,256,512]{2,1,0:T(8,128)(2,1)}, u32[]{:S(2)}) %copy-start.1) | copy-done | bytes 2097176
  22.0 2.5 %stage_cache.1 = (bf16[8,512,256]{2,1,0:T(8,128)(2,1)S(1)}, bf16[8,512,256]{2,1,0:T(8,128)(2,1)S(1)}) custom-call(s32[4]{0:T(128)S(1)} %pad_add_fusion.place, bf16[8,256,512]{2,1,0:T(8,128)(2,1)S(1)} %copy-done, bf16[8,256,512]{2,1,0:T(8,128)(2,1)} %collective-permute-done.3.keys2, bf16[8,256,512]{2,1,0:T(8,128)(2,1)S(1)} %copy-done.1, ...), custom_call_target="tpu_custom_call" | custom-call | bytes 8388608 | tf_op jit(solution)/shard_map/stage_cache/pallas_call | solution.py:80
  24.5 4.2 %collective-permute-done.7.refs_2_ = bf16[32,1664]{1,0:T(8,128)(2,1)} collective-permute-done((bf16[32,1664]{1,0:T(8,128)(2,1)S(1)}, bf16[32,1664]{1,0:T(8,128)(2,1)}, u32[]{:S(2)}, u32[]{:S(2)}) %collective-permute-start.7) | collective-permute-done | bytes 106528 | tf_op jit(solution)/shard_map/ppermute | solution.py:65
  28.7 5.3 %attend.1 = (bf16[32,1152]{1,0:T(8,128)(2,1)S(1)}, bf16[32,256]{1,0:T(8,128)(2,1)S(1)}, bf16[32,256]{1,0:T(8,128)(2,1)S(1)}) custom-call(s32[4]{0:T(128)S(1)} %pad_add_fusion.place, s32[8]{0:T(128)S(1)} %copy-done.9, s32[8]{0:T(128)S(1)} %copy-done.10, f32[32,128]{1,0:T(8,128)S(1)} %get-tuple-element.50.cosine, f32[32,128]{1,0:T(8,128)S(1)} %get-tuple-element.51.sine, ...), custom_call_target="tpu_custom_call" | custom-call | tf_op jit(solution)/shard_map/attend/pallas_call | solution.py:80
  34.1 0.1 collective-permute-start.14
  34.1 2.5 %collective-permute-start.13 = (bf16[32,1152]{1,0:T(8,128)(2,1)S(1)}, bf16[32,1152]{1,0:T(8,128)(2,1)S(1)}, u32[]{:S(2)}, u32[]{:S(2)}) collective-permute-start(bf16[32,1152]{1,0:T(8,128)(2,1)S(1)} %get-tuple-element.77.refs_0_), channel_id=1, source_target_pairs={{0,24},{4,28},{8,16},{12,20},{16,8},{20,12},{24,0},{28,4},{1,25},{... | collective-permute-start | bytes 221192 | tf_op jit(solution)/shard_map/ppermute | solution.py:65
  36.7 1.9 %collective-permute-start.11 = (bf16[32,1152]{1,0:T(8,128)(2,1)S(1)}, bf16[32,1152]{1,0:T(8,128)(2,1)S(1)}, u32[]{:S(2)}, u32[]{:S(2)}) collective-permute-start(bf16[32,1152]{1,0:T(8,128)(2,1)S(1)} %get-tuple-element.77.refs_0_), channel_id=1, source_target_pairs={{0,8},{4,12},{8,0},{12,4},{16,24},{20,28},{24,16},{28,20},{1,9},{5... | collective-permute-start | bytes 221192 | tf_op jit(solution)/shard_map/ppermute | solution.py:65
  38.6 2.2 %stage_gate.1 = (bf16[512,1024]{1,0:T(8,128)(2,1)S(1)}, bf16[512,1024]{1,0:T(8,128)(2,1)S(1)}) custom-call(s32[4]{0:T(128)S(1)} %pad_add_fusion.place, bf16[256,2048]{1,0:T(8,128)(2,1)S(1)} %copy-done.3, bf16[256,2048]{1,0:T(8,128)(2,1)} %collective-permute-done.9.g_two, bf16[256,2048]{1,0:T(8,128)(2,1)} %u_own, bf16[256,2048]{1,0:T(8,128)(2,1)} %collective-permute-done.10.u_two), custom_call_target="tpu_custom_call" | custom-call | bytes 4194304 | tf_op jit(solution)/shard_map/stage_gate/pallas_call | solution.py:80
  40.8 0.0 copy-start.7
  40.9 1.4 %stage_out.1 = (bf16[1024,512]{1,0:T(8,128)(2,1)S(1)}, bf16[8,4,512]{2,1,0:T(4,128)(2,1)}, bf16[8,4,512]{2,1,0:T(4,128)(2,1)}) custom-call(s32[4]{0:T(128)S(1)} %pad_add_fusion.place, bf16[2048,256]{1,0:T(8,128)(2,1)S(1)} %copy-done.4, bf16[2048,256]{1,0:T(8,128)(2,1)S(1)} %collective-permute-done.14.o_two, bf16[32,256]{1,0:T(8,128)(2,1)S(1)} %get-tuple-element.69.k, ...), custom_call_target="tpu_custom_call" | custom-call | bytes 2097152 | tf_op jit(solution)/shard_map/stage_out/pallas_call | solution.py:80
  42.2 1.5 %collective-permute-done.12.refs_2_ = bf16[32,1152]{1,0:T(8,128)(2,1)S(1)} collective-permute-done((bf16[32,1152]{1,0:T(8,128)(2,1)S(1)}, bf16[32,1152]{1,0:T(8,128)(2,1)S(1)}, u32[]{:S(2)}, u32[]{:S(2)}) %collective-permute-start.12) | collective-permute-done | bytes 73760 | tf_op jit(solution)/shard_map/ppermute | solution.py:65
  43.8 0.7 output.1
  44.5 0.0 collective-permute-start.16
  44.5 1.2 %collective-permute-done.16 = f32[32,512]{1,0:T(8,128)S(1)} collective-permute-done((f32[32,512]{1,0:T(8,128)S(1)}, f32[32,512]{1,0:T(8,128)S(1)}, u32[]{:S(2)}, u32[]{:S(2)}) %collective-permute-start.16) | collective-permute-done | bytes 65568 | tf_op jit(solution)/shard_map/ppermute | solution.py:65
  45.8 1.5 %collective-permute-start.19 = (bf16[32,512]{1,0:T(8,128)(2,1)S(1)}, bf16[32,512]{1,0:T(8,128)(2,1)S(1)}, u32[]{:S(2)}, u32[]{:S(2)}) collective-permute-start(bf16[32,512]{1,0:T(8,128)(2,1)S(1)} %add_convert_fusion.refs_0_), channel_id=1, source_target_pairs={{0,3},{1,2},{2,1},{3,0},{4,7},{5,6},{6,5},{7,4},{8,11},{9,10},{10,... | collective-permute-start | bytes 98312 | tf_op jit(solution)/shard_map/ppermute | solution.py:65
  47.3 1.4 %collective-permute-start.18 = (bf16[32,512]{1,0:T(8,128)(2,1)S(1)}, bf16[32,512]{1,0:T(8,128)(2,1)S(1)}, u32[]{:S(2)}, u32[]{:S(2)}) collective-permute-start(bf16[32,512]{1,0:T(8,128)(2,1)S(1)} %add_convert_fusion.refs_0_), channel_id=1, source_target_pairs={{0,2},{1,3},{2,0},{3,1},{4,6},{5,7},{6,4},{7,5},{8,10},{9,11},{10,... | collective-permute-start | bytes 98312 | tf_op jit(solution)/shard_map/ppermute | solution.py:65
  48.7 0.6 collective-permute-start.17
  49.3 1.3 %collective-permute-done.19.refs_3_ = bf16[32,512]{1,0:T(8,128)(2,1)S(1)} collective-permute-done((bf16[32,512]{1,0:T(8,128)(2,1)S(1)}, bf16[32,512]{1,0:T(8,128)(2,1)S(1)}, u32[]{:S(2)}, u32[]{:S(2)}) %collective-permute-start.19) | collective-permute-done | bytes 32800 | tf_op jit(solution)/shard_map/ppermute | solution.py:65
  50.7 0.6 collective-permute-done.18.refs_2_
  51.2 1.4 %collective-permute-done.17.refs_1_ = bf16[32,512]{1,0:T(8,128)(2,1)S(1)} collective-permute-done((bf16[32,512]{1,0:T(8,128)(2,1)S(1)}, bf16[32,512]{1,0:T(8,128)(2,1)S(1)}, u32[]{:S(2)}, u32[]{:S(2)}) %collective-permute-start.17) | collective-permute-done | bytes 32800 | tf_op jit(solution)/shard_map/ppermute | solution.py:65
  52.6 1.0 %gate.1 = bf16[4,32,2176]{2,1,0:T(8,128)(2,1)S(1)} custom-call(s32[4]{0:T(128)S(1)} %pad_add_fusion.place, bf16[1,512]{1,0:T(2,128)(2,1)S(1)} %broadcast_select_fusion.gains, bf16[512,1024]{1,0:T(8,128)(2,1)S(1)} %get-tuple-element.81.w_gate, bf16[512,1024]{1,0:T(8,128)(2,1)S(1)} %get-tuple-element.82.w_up, bf16[32,512]{1,0:T(8,128)(2,1)S(1)} %add_convert_fusion.refs_0_, ...), custom_call_target="tpu_custom_call" | custom-call | tf_op jit(solution)/shard_map/gate/pallas_call | solution.py:80
  53.7 2.5 %collective-permute-start.22 = (bf16[32,2176]{1,0:T(8,128)(2,1)S(1)}, bf16[32,2176]{1,0:T(8,128)(2,1)S(1)}, u32[]{:S(2)}, u32[]{:S(2)}) collective-permute-start(bf16[32,2176]{1,0:T(8,128)(2,1)S(1)} %get-tuple-element.85), channel_id=1, source_target_pairs={{0,24},{4,28},{8,16},{12,20},{16,8},{20,12},{24,0},{28,4},{1,25},{... | collective-permute-start | bytes 417800 | tf_op jit(solution)/shard_map/ppermute | solution.py:65
  56.2 1.9 %collective-permute-start.20 = (bf16[32,2176]{1,0:T(8,128)(2,1)S(1)}, bf16[32,2176]{1,0:T(8,128)(2,1)S(1)}, u32[]{:S(2)}, u32[]{:S(2)}) collective-permute-start(bf16[32,2176]{1,0:T(8,128)(2,1)S(1)} %get-tuple-element.87), channel_id=1, source_target_pairs={{0,8},{4,12},{8,0},{12,4},{16,24},{20,28},{24,16},{28,20},{1,9},{5... | collective-permute-start | bytes 417800 | tf_op jit(solution)/shard_map/ppermute | solution.py:65
  58.1 4.0 %collective-permute-done.22.refs_3_ = bf16[32,2176]{1,0:T(8,128)(2,1)S(1)} collective-permute-done((bf16[32,2176]{1,0:T(8,128)(2,1)S(1)}, bf16[32,2176]{1,0:T(8,128)(2,1)S(1)}, u32[]{:S(2)}, u32[]{:S(2)}) %collective-permute-start.22) | collective-permute-done | bytes 139296 | tf_op jit(solution)/shard_map/ppermute | solution.py:65
  62.2 5.1 %collective-permute-done.21.refs_2_ = bf16[32,2176]{1,0:T(8,128)(2,1)S(1)} collective-permute-done((bf16[32,2176]{1,0:T(8,128)(2,1)S(1)}, bf16[32,2176]{1,0:T(8,128)(2,1)S(1)}, u32[]{:S(2)}, u32[]{:S(2)}) %collective-permute-start.21) | collective-permute-done | bytes 139296 | tf_op jit(solution)/shard_map/ppermute | solution.py:65
  67.3 0.2 hidden.1.refs_0_
  67.5 2.0 %collective-permute-start.25 = (bf16[32,1024]{1,0:T(8,128)(2,1)S(1)}, bf16[32,1024]{1,0:T(8,128)(2,1)S(1)}, u32[]{:S(2)}, u32[]{:S(2)}) collective-permute-start(bf16[32,1024]{1,0:T(8,128)(2,1)S(1)} %hidden.1.refs_0_), channel_id=1, source_target_pairs={{0,24},{4,28},{8,16},{12,20},{16,8},{20,12},{24,0},{28,4},{1,25},{... | collective-permute-start | bytes 196616 | tf_op jit(solution)/shard_map/ppermute | solution.py:65
  69.5 2.5 %collective-permute-start.23 = (bf16[32,1024]{1,0:T(8,128)(2,1)S(1)}, bf16[32,1024]{1,0:T(8,128)(2,1)S(1)}, u32[]{:S(2)}, u32[]{:S(2)}) collective-permute-start(bf16[32,1024]{1,0:T(8,128)(2,1)S(1)} %hidden.1.refs_0_), channel_id=1, source_target_pairs={{0,8},{4,12},{8,0},{12,4},{16,24},{20,28},{24,16},{28,20},{1,9},{5... | collective-permute-start | bytes 196616 | tf_op jit(solution)/shard_map/ppermute | solution.py:65
  72.0 2.3 %collective-permute-done.25.refs_3_ = bf16[32,1024]{1,0:T(8,128)(2,1)S(1)} collective-permute-done((bf16[32,1024]{1,0:T(8,128)(2,1)S(1)}, bf16[32,1024]{1,0:T(8,128)(2,1)S(1)}, u32[]{:S(2)}, u32[]{:S(2)}) %collective-permute-start.25) | collective-permute-done | bytes 65568 | tf_op jit(solution)/shard_map/ppermute | solution.py:65
  74.3 1.2 %collective-permute-done.24.refs_2_ = bf16[32,1024]{1,0:T(8,128)(2,1)S(1)} collective-permute-done((bf16[32,1024]{1,0:T(8,128)(2,1)S(1)}, bf16[32,1024]{1,0:T(8,128)(2,1)S(1)}, u32[]{:S(2)}, u32[]{:S(2)}) %collective-permute-start.24) | collective-permute-done | bytes 65568 | tf_op jit(solution)/shard_map/ppermute | solution.py:65
  75.5 0.5 collective-permute-start.27
  76.0 0.7 collective-permute-done.28.refs_6_
  76.7 0.2 collective-permute-done.27.refs_5_
  76.9 0.9 %down.1 = bf16[4,32,256]{2,1,0:T(8,128)(2,1)S(1)} custom-call(s32[4]{0:T(128)S(1)} %pad_add_fusion.place, bf16[2048,256]{1,0:T(8,128)(2,1)S(1)} %copy-done.5, bf16[32,1024]{1,0:T(8,128)(2,1)S(1)} %hidden.1.refs_0_, bf16[32,1024]{1,0:T(8,128)(2,1)S(1)} %collective-permute-done.23.refs_1_, bf16[32,1024]{1,0:T(8,128)(2,1)S(1)} %collective-permute-done.24.refs_2_, ...), custom_call_target="tpu_custom_call" | custom-call | tf_op jit(solution)/shard_map/down/pallas_call | solution.py:80
  77.8 0.7 collective-permute-start.30
  78.5 1.5 %collective-permute-start.32 = (bf16[32,256]{1,0:T(8,128)(2,1)S(1)}, bf16[32,256]{1,0:T(8,128)(2,1)S(1)}, u32[]{:S(2)}, u32[]{:S(2)}) collective-permute-start(bf16[32,256]{1,0:T(8,128)(2,1)S(1)} %get-tuple-element.90), channel_id=1, source_target_pairs={{0,3},{1,2},{2,1},{3,0},{4,7},{5,6},{6,5},{7,4},{8,11},{9,10},{10,... | collective-permute-start | bytes 49160 | tf_op jit(solution)/shard_map/ppermute | solution.py:65
  80.0 1.4 %collective-permute-start.31 = (bf16[32,256]{1,0:T(8,128)(2,1)S(1)}, bf16[32,256]{1,0:T(8,128)(2,1)S(1)}, u32[]{:S(2)}, u32[]{:S(2)}) collective-permute-start(bf16[32,256]{1,0:T(8,128)(2,1)S(1)} %get-tuple-element.91), channel_id=1, source_target_pairs={{0,2},{1,3},{2,0},{3,1},{4,6},{5,7},{6,4},{7,5},{8,10},{9,11},{10,... | collective-permute-start | bytes 49160 | tf_op jit(solution)/shard_map/ppermute | solution.py:65
  81.3 0.2 collective-permute-done.30
  81.6 1.5 %collective-permute-done.32 = bf16[32,256]{1,0:T(8,128)(2,1)S(1)} collective-permute-done((bf16[32,256]{1,0:T(8,128)(2,1)S(1)}, bf16[32,256]{1,0:T(8,128)(2,1)S(1)}, u32[]{:S(2)}, u32[]{:S(2)}) %collective-permute-start.32) | collective-permute-done | bytes 16416 | tf_op jit(solution)/shard_map/ppermute | solution.py:65
  83.1 0.6 collective-permute-done.31
  83.7 0.6 reshape.107
  (57 shorter events, 0.2 us)
Async XLA Ops:
  0.6 12.0 %collective-permute-start.3 = (bf16[8,256,512]{2,1,0:T(8,128)(2,1)}, bf16[8,256,512]{2,1,0:T(8,128)(2,1)}, u32[]{:S(2)}, u32[]{:S(2)}) collective-permute-start(bf16[8,256,512]{2,1,0:T(8,128)(2,1)} %keys.1), channel_id=1, source_target_pairs={{0,4},{4,0},{8,12},{12,8},{16,20},{20,16},{24,28},{28,24},{1,5},{5... | collective-permute-start | bytes 6291464 | tf_op jit(solution)/shard_map/ppermute | solution.py:65
  1.1 11.5 %collective-permute-start.4 = (bf16[8,256,512]{2,1,0:T(8,128)(2,1)}, bf16[8,256,512]{2,1,0:T(8,128)(2,1)}, u32[]{:S(2)}, u32[]{:S(2)}) collective-permute-start(bf16[8,256,512]{2,1,0:T(8,128)(2,1)} %values.1), channel_id=1, source_target_pairs={{0,4},{4,0},{8,12},{12,8},{16,20},{20,16},{24,28},{28,24},{1,5},{5... | collective-permute-start | bytes 6291464 | tf_op jit(solution)/shard_map/ppermute | solution.py:65
  1.3 0.7 copy-start.8
  2.0 7.1 %copy-start.12 = (bf16[256]{0:T(256)(128)(2,1)S(1)}, bf16[256]{0:T(256)(128)(2,1)}, u32[]{:S(2)}) copy-start(bf16[256]{0:T(256)(128)(2,1)} %param.24) | copy-start | bytes 1540
  2.0 7.1 %copy-start.13 = (bf16[256]{0:T(256)(128)(2,1)S(1)}, bf16[256]{0:T(256)(128)(2,1)}, u32[]{:S(2)}) copy-start(bf16[256]{0:T(256)(128)(2,1)} %param.23) | copy-start | bytes 1540
  2.0 10.7 %copy-start.2 = (bf16[256,3072]{1,0:T(8,128)(2,1)S(1)}, bf16[256,3072]{1,0:T(8,128)(2,1)}, u32[]{:S(2)}) copy-start(bf16[256,3072]{1,0:T(8,128)(2,1)} %weight.1) | copy-start | bytes 4718596
  2.0 13.1 %copy-start.3 = (bf16[256,2048]{1,0:T(8,128)(2,1)S(1)}, bf16[256,2048]{1,0:T(8,128)(2,1)}, u32[]{:S(2)}) copy-start(bf16[256,2048]{1,0:T(8,128)(2,1)} %g_own) | copy-start | bytes 3145732
  5.3 14.8 %copy-start.11 = (s32[8]{0:T(128)S(1)}, s32[8]{0:T(128)}, u32[]{:S(2)}) copy-start(s32[8]{0:T(128)} %param.20) | copy-start | bytes 100
  5.3 15.1 %copy-start = (bf16[8,256,512]{2,1,0:T(8,128)(2,1)S(1)}, bf16[8,256,512]{2,1,0:T(8,128)(2,1)}, u32[]{:S(2)}) copy-start(bf16[8,256,512]{2,1,0:T(8,128)(2,1)} %keys.1) | copy-start | bytes 6291460
  5.3 4.8 %collective-permute-start.2 = (bf16[32,256]{1,0:T(8,128)(2,1)S(1)}, bf16[32,256]{1,0:T(8,128)(2,1)S(1)}, u32[]{:S(2)}, u32[]{:S(2)}) collective-permute-start(bf16[32,256]{1,0:T(8,128)(2,1)S(1)} %get-tuple-element.92), channel_id=1, source_target_pairs={{0,3},{1,2},{2,1},{3,0},{4,7},{5,6},{6,5},{7,4},{8,11},{9,10},{10,... | collective-permute-start | bytes 49160 | tf_op jit(solution)/shard_map/ppermute | solution.py:65
  8.4 3.7 %collective-permute-start.1 = (bf16[32,256]{1,0:T(8,128)(2,1)S(1)}, bf16[32,256]{1,0:T(8,128)(2,1)S(1)}, u32[]{:S(2)}, u32[]{:S(2)}) collective-permute-start(bf16[32,256]{1,0:T(8,128)(2,1)S(1)} %get-tuple-element.93), channel_id=1, source_target_pairs={{0,2},{1,3},{2,0},{3,1},{4,6},{5,7},{6,4},{7,5},{8,10},{9,11},{10,... | collective-permute-start | bytes 49160 | tf_op jit(solution)/shard_map/ppermute | solution.py:65
  8.9 3.7 %collective-permute-start = (bf16[32,256]{1,0:T(8,128)(2,1)S(1)}, bf16[32,256]{1,0:T(8,128)(2,1)S(1)}, u32[]{:S(2)}, u32[]{:S(2)}) collective-permute-start(bf16[32,256]{1,0:T(8,128)(2,1)S(1)} %get-tuple-element.94), channel_id=1, source_target_pairs={{0,1},{1,0},{2,3},{3,2},{4,5},{5,4},{6,7},{7,6},{8,9},{9,8},{10,11... | collective-permute-start | bytes 49160 | tf_op jit(solution)/shard_map/ppermute | solution.py:65
  13.6 1.4 %collective-permute-start.5 = (bf16[32,2176]{1,0:T(8,128)(2,1)S(1)}, bf16[32,2176]{1,0:T(8,128)(2,1)S(1)}, u32[]{:S(2)}, u32[]{:S(2)}) collective-permute-start(bf16[32,2176]{1,0:T(8,128)(2,1)S(1)} %get-tuple-element.49), channel_id=1, source_target_pairs={{0,4},{4,0},{8,12},{12,8},{16,20},{20,16},{24,28},{28,24},{1,5},{5... | collective-permute-start | bytes 417800 | tf_op jit(solution)/shard_map/ppermute | solution.py:65
  15.1 13.6 %collective-permute-start.9 = (bf16[256,2048]{1,0:T(8,128)(2,1)S(1)}, bf16[256,2048]{1,0:T(8,128)(2,1)}, u32[]{:S(2)}, u32[]{:S(2)}) collective-permute-start(bf16[256,2048]{1,0:T(8,128)(2,1)S(1)} %copy-done.3), channel_id=1, source_target_pairs={{0,4},{4,0},{8,12},{12,8},{16,20},{20,16},{24,28},{28,24},{1,5},{5... | collective-permute-start | bytes 3145736 | tf_op jit(solution)/shard_map/ppermute | solution.py:65
  15.3 13.4 %collective-permute-start.10 = (bf16[256,2048]{1,0:T(8,128)(2,1)}, bf16[256,2048]{1,0:T(8,128)(2,1)}, u32[]{:S(2)}, u32[]{:S(2)}) collective-permute-start(bf16[256,2048]{1,0:T(8,128)(2,1)} %u_own), channel_id=1, source_target_pairs={{0,4},{4,0},{8,12},{12,8},{16,20},{20,16},{24,28},{28,24},{1,5},{5... | collective-permute-start | bytes 3145736 | tf_op jit(solution)/shard_map/ppermute | solution.py:65
  15.7 8.8 %collective-permute-start.8 = (bf16[32,1664]{1,0:T(8,128)(2,1)S(1)}, bf16[32,1664]{1,0:T(8,128)(2,1)S(1)}, u32[]{:S(2)}, u32[]{:S(2)}) collective-permute-start(bf16[32,1664]{1,0:T(8,128)(2,1)S(1)} %add.94.refs_0_), channel_id=1, source_target_pairs={{0,24},{4,28},{8,16},{12,20},{16,8},{20,12},{24,0},{28,4},{1,25},{... | collective-permute-start | bytes 319496 | tf_op jit(solution)/shard_map/ppermute | solution.py:65
  19.3 9.4 %collective-permute-start.7 = (bf16[32,1664]{1,0:T(8,128)(2,1)S(1)}, bf16[32,1664]{1,0:T(8,128)(2,1)}, u32[]{:S(2)}, u32[]{:S(2)}) collective-permute-start(bf16[32,1664]{1,0:T(8,128)(2,1)S(1)} %add.94.refs_0_), channel_id=1, source_target_pairs={{0,16},{4,20},{8,24},{12,28},{16,0},{20,4},{24,8},{28,12},{1,17},{... | collective-permute-start | bytes 319496 | tf_op jit(solution)/shard_map/ppermute | solution.py:65
  19.3 9.4 %collective-permute-start.6 = (bf16[32,1664]{1,0:T(8,128)(2,1)S(1)}, bf16[32,1664]{1,0:T(8,128)(2,1)}, u32[]{:S(2)}, u32[]{:S(2)}) collective-permute-start(bf16[32,1664]{1,0:T(8,128)(2,1)S(1)} %add.94.refs_0_), channel_id=1, source_target_pairs={{0,8},{4,12},{8,0},{12,4},{16,24},{20,28},{24,16},{28,20},{1,9},{5... | collective-permute-start | bytes 319496 | tf_op jit(solution)/shard_map/ppermute | solution.py:65
  20.4 1.6 %copy-start.1 = (bf16[8,256,512]{2,1,0:T(8,128)(2,1)S(1)}, bf16[8,256,512]{2,1,0:T(8,128)(2,1)}, u32[]{:S(2)}) copy-start(bf16[8,256,512]{2,1,0:T(8,128)(2,1)} %values.1) | copy-start | bytes 6291460
  22.0 6.7 %copy-start.6 = (bf16[1024,256]{1,0:T(8,128)(2,1)S(1)}, bf16[1024,256]{1,0:T(8,128)(2,1)}, u32[]{:S(2)}) copy-start(bf16[1024,256]{1,0:T(8,128)(2,1)} %constant.42.clone.fold) | copy-start | bytes 1572868
  22.0 6.7 %copy-start.9 = (s32[8]{0:T(128)S(1)}, s32[8]{0:T(128)}, u32[]{:S(2)}) copy-start(s32[8]{0:T(128)} %starts.1) | copy-start | bytes 100
  22.0 6.7 %copy-start.10 = (s32[8]{0:T(128)S(1)}, s32[8]{0:T(128)}, u32[]{:S(2)}) copy-start(s32[8]{0:T(128)} %lens.1) | copy-start | bytes 100
  28.7 5.4 %copy-start.4 = (bf16[2048,256]{1,0:T(8,128)(2,1)S(1)}, bf16[2048,256]{1,0:T(8,128)(2,1)}, u32[]{:S(2)}) copy-start(bf16[2048,256]{1,0:T(8,128)(2,1)} %o_own) | copy-start | bytes 3145732
  34.1 6.8 %collective-permute-start.14 = (bf16[2048,256]{1,0:T(8,128)(2,1)S(1)}, bf16[2048,256]{1,0:T(8,128)(2,1)S(1)}, u32[]{:S(2)}, u32[]{:S(2)}) collective-permute-start(bf16[2048,256]{1,0:T(8,128)(2,1)S(1)} %copy-done.4), channel_id=1, source_target_pairs={{0,4},{4,0},{8,12},{12,8},{16,20},{20,16},{24,28},{28,24},{1,5},{5... | collective-permute-start | bytes 3145736 | tf_op jit(solution)/shard_map/ppermute | solution.py:65
  34.1 8.1 %collective-permute-start.13 = (bf16[32,1152]{1,0:T(8,128)(2,1)S(1)}, bf16[32,1152]{1,0:T(8,128)(2,1)S(1)}, u32[]{:S(2)}, u32[]{:S(2)}) collective-permute-start(bf16[32,1152]{1,0:T(8,128)(2,1)S(1)} %get-tuple-element.77.refs_0_), channel_id=1, source_target_pairs={{0,24},{4,28},{8,16},{12,20},{16,8},{20,12},{24,0},{28,4},{1,25},{... | collective-permute-start | bytes 221192 | tf_op jit(solution)/shard_map/ppermute | solution.py:65
  36.7 7.1 %collective-permute-start.12 = (bf16[32,1152]{1,0:T(8,128)(2,1)S(1)}, bf16[32,1152]{1,0:T(8,128)(2,1)S(1)}, u32[]{:S(2)}, u32[]{:S(2)}) collective-permute-start(bf16[32,1152]{1,0:T(8,128)(2,1)S(1)} %get-tuple-element.77.refs_0_), channel_id=1, source_target_pairs={{0,16},{4,20},{8,24},{12,28},{16,0},{20,4},{24,8},{28,12},{1,17},{... | collective-permute-start | bytes 221192 | tf_op jit(solution)/shard_map/ppermute | solution.py:65
  36.7 7.1 %collective-permute-start.11 = (bf16[32,1152]{1,0:T(8,128)(2,1)S(1)}, bf16[32,1152]{1,0:T(8,128)(2,1)S(1)}, u32[]{:S(2)}, u32[]{:S(2)}) collective-permute-start(bf16[32,1152]{1,0:T(8,128)(2,1)S(1)} %get-tuple-element.77.refs_0_), channel_id=1, source_target_pairs={{0,8},{4,12},{8,0},{12,4},{16,24},{20,28},{24,16},{28,20},{1,9},{5... | collective-permute-start | bytes 221192 | tf_op jit(solution)/shard_map/ppermute | solution.py:65
  38.6 2.2 %collective-permute-start.15 = (bf16[32,512]{1,0:T(8,128)(2,1)S(1)}, bf16[32,512]{1,0:T(8,128)(2,1)S(1)}, u32[]{:S(2)}, u32[]{:S(2)}) collective-permute-start(bf16[32,512]{1,0:T(8,128)(2,1)S(1)} %pad_maximum_fusion), channel_id=1, source_target_pairs={{0,4},{4,0},{8,12},{12,8},{16,20},{20,16},{24,28},{28,24},{1,5},{5... | collective-permute-start | bytes 98312 | tf_op jit(solution)/shard_map/ppermute | solution.py:65
  40.8 3.0 %copy-start.7 = (bf16[128,1024]{1,0:T(8,128)(2,1)S(1)}, bf16[128,1024]{1,0:T(8,128)(2,1)}, u32[]{:S(2)}) copy-start(bf16[128,1024]{1,0:T(8,128)(2,1)} %constant.43.clone.spread) | copy-start | bytes 786436
  44.5 1.3 %collective-permute-start.16 = (f32[32,512]{1,0:T(8,128)S(1)}, f32[32,512]{1,0:T(8,128)S(1)}, u32[]{:S(2)}, u32[]{:S(2)}) collective-permute-start(f32[32,512]{1,0:T(8,128)S(1)} %output.1), channel_id=1, source_target_pairs={{0,4},{4,0},{8,12},{12,8},{16,20},{20,16},{24,28},{28,24},{1,5},{5... | collective-permute-start | bytes 196616 | tf_op jit(solution)/shard_map/ppermute | solution.py:65
  45.8 4.9 %collective-permute-start.19 = (bf16[32,512]{1,0:T(8,128)(2,1)S(1)}, bf16[32,512]{1,0:T(8,128)(2,1)S(1)}, u32[]{:S(2)}, u32[]{:S(2)}) collective-permute-start(bf16[32,512]{1,0:T(8,128)(2,1)S(1)} %add_convert_fusion.refs_0_), channel_id=1, source_target_pairs={{0,3},{1,2},{2,1},{3,0},{4,7},{5,6},{6,5},{7,4},{8,11},{9,10},{10,... | collective-permute-start | bytes 98312 | tf_op jit(solution)/shard_map/ppermute | solution.py:65
  47.3 3.9 %collective-permute-start.18 = (bf16[32,512]{1,0:T(8,128)(2,1)S(1)}, bf16[32,512]{1,0:T(8,128)(2,1)S(1)}, u32[]{:S(2)}, u32[]{:S(2)}) collective-permute-start(bf16[32,512]{1,0:T(8,128)(2,1)S(1)} %add_convert_fusion.refs_0_), channel_id=1, source_target_pairs={{0,2},{1,3},{2,0},{3,1},{4,6},{5,7},{6,4},{7,5},{8,10},{9,11},{10,... | collective-permute-start | bytes 98312 | tf_op jit(solution)/shard_map/ppermute | solution.py:65
  48.7 3.9 %collective-permute-start.17 = (bf16[32,512]{1,0:T(8,128)(2,1)S(1)}, bf16[32,512]{1,0:T(8,128)(2,1)S(1)}, u32[]{:S(2)}, u32[]{:S(2)}) collective-permute-start(bf16[32,512]{1,0:T(8,128)(2,1)S(1)} %add_convert_fusion.refs_0_), channel_id=1, source_target_pairs={{0,1},{1,0},{2,3},{3,2},{4,5},{5,4},{6,7},{7,6},{8,9},{9,8},{10,11... | collective-permute-start | bytes 98312 | tf_op jit(solution)/shard_map/ppermute | solution.py:65
  49.3 27.6 %copy-start.5 = (bf16[2048,256]{1,0:T(8,128)(2,1)S(1)}, bf16[2048,256]{1,0:T(8,128)(2,1)}, u32[]{:S(2)}) copy-start(bf16[2048,256]{1,0:T(8,128)(2,1)} %w_down.1) | copy-start | bytes 3145732
  53.7 8.5 %collective-permute-start.22 = (bf16[32,2176]{1,0:T(8,128)(2,1)S(1)}, bf16[32,2176]{1,0:T(8,128)(2,1)S(1)}, u32[]{:S(2)}, u32[]{:S(2)}) collective-permute-start(bf16[32,2176]{1,0:T(8,128)(2,1)S(1)} %get-tuple-element.85), channel_id=1, source_target_pairs={{0,24},{4,28},{8,16},{12,20},{16,8},{20,12},{24,0},{28,4},{1,25},{... | collective-permute-start | bytes 417800 | tf_op jit(solution)/shard_map/ppermute | solution.py:65
  56.2 11.1 %collective-permute-start.21 = (bf16[32,2176]{1,0:T(8,128)(2,1)S(1)}, bf16[32,2176]{1,0:T(8,128)(2,1)S(1)}, u32[]{:S(2)}, u32[]{:S(2)}) collective-permute-start(bf16[32,2176]{1,0:T(8,128)(2,1)S(1)} %get-tuple-element.86), channel_id=1, source_target_pairs={{0,16},{4,20},{8,24},{12,28},{16,0},{20,4},{24,8},{28,12},{1,17},{... | collective-permute-start | bytes 417800 | tf_op jit(solution)/shard_map/ppermute | solution.py:65
  56.2 11.1 %collective-permute-start.20 = (bf16[32,2176]{1,0:T(8,128)(2,1)S(1)}, bf16[32,2176]{1,0:T(8,128)(2,1)S(1)}, u32[]{:S(2)}, u32[]{:S(2)}) collective-permute-start(bf16[32,2176]{1,0:T(8,128)(2,1)S(1)} %get-tuple-element.87), channel_id=1, source_target_pairs={{0,8},{4,12},{8,0},{12,4},{16,24},{20,28},{24,16},{28,20},{1,9},{5... | collective-permute-start | bytes 417800 | tf_op jit(solution)/shard_map/ppermute | solution.py:65
  67.5 6.7 %collective-permute-start.25 = (bf16[32,1024]{1,0:T(8,128)(2,1)S(1)}, bf16[32,1024]{1,0:T(8,128)(2,1)S(1)}, u32[]{:S(2)}, u32[]{:S(2)}) collective-permute-start(bf16[32,1024]{1,0:T(8,128)(2,1)S(1)} %hidden.1.refs_0_), channel_id=1, source_target_pairs={{0,24},{4,28},{8,16},{12,20},{16,8},{20,12},{24,0},{28,4},{1,25},{... | collective-permute-start | bytes 196616 | tf_op jit(solution)/shard_map/ppermute | solution.py:65
  69.5 6.0 %collective-permute-start.24 = (bf16[32,1024]{1,0:T(8,128)(2,1)S(1)}, bf16[32,1024]{1,0:T(8,128)(2,1)S(1)}, u32[]{:S(2)}, u32[]{:S(2)}) collective-permute-start(bf16[32,1024]{1,0:T(8,128)(2,1)S(1)} %hidden.1.refs_0_), channel_id=1, source_target_pairs={{0,16},{4,20},{8,24},{12,28},{16,0},{20,4},{24,8},{28,12},{1,17},{... | collective-permute-start | bytes 196616 | tf_op jit(solution)/shard_map/ppermute | solution.py:65
  69.5 6.0 %collective-permute-start.23 = (bf16[32,1024]{1,0:T(8,128)(2,1)S(1)}, bf16[32,1024]{1,0:T(8,128)(2,1)S(1)}, u32[]{:S(2)}, u32[]{:S(2)}) collective-permute-start(bf16[32,1024]{1,0:T(8,128)(2,1)S(1)} %hidden.1.refs_0_), channel_id=1, source_target_pairs={{0,8},{4,12},{8,0},{12,4},{16,24},{20,28},{24,16},{28,20},{1,9},{5... | collective-permute-start | bytes 196616 | tf_op jit(solution)/shard_map/ppermute | solution.py:65
  72.0 4.0 %collective-permute-start.26 = (bf16[32,1024]{1,0:T(8,128)(2,1)S(1)}, bf16[32,1024]{1,0:T(8,128)(2,1)S(1)}, u32[]{:S(2)}, u32[]{:S(2)}) collective-permute-start(bf16[32,1024]{1,0:T(8,128)(2,1)S(1)} %hidden.1.refs_0_), channel_id=1, source_target_pairs={{0,4},{4,0},{8,12},{12,8},{16,20},{20,16},{24,28},{28,24},{1,5},{5... | collective-permute-start | bytes 196616 | tf_op jit(solution)/shard_map/ppermute | solution.py:65
  74.3 1.7 %collective-permute-start.29 = (bf16[32,1024]{1,0:T(8,128)(2,1)S(1)}, bf16[32,1024]{1,0:T(8,128)(2,1)S(1)}, u32[]{:S(2)}, u32[]{:S(2)}) collective-permute-start(bf16[32,1024]{1,0:T(8,128)(2,1)S(1)} %collective-permute-done.25.refs_3_), channel_id=1, source_target_pairs={{0,4},{4,0},{8,12},{12,8},{16,20},{20,16},{24,28},{28,24},{1,5},{5... | collective-permute-start | bytes 196616 | tf_op jit(solution)/shard_map/ppermute | solution.py:65
  75.5 1.3 %collective-permute-start.28 = (bf16[32,1024]{1,0:T(8,128)(2,1)S(1)}, bf16[32,1024]{1,0:T(8,128)(2,1)S(1)}, u32[]{:S(2)}, u32[]{:S(2)}) collective-permute-start(bf16[32,1024]{1,0:T(8,128)(2,1)S(1)} %collective-permute-done.24.refs_2_), channel_id=1, source_target_pairs={{0,4},{4,0},{8,12},{12,8},{16,20},{20,16},{24,28},{28,24},{1,5},{5... | collective-permute-start | bytes 196616 | tf_op jit(solution)/shard_map/ppermute | solution.py:65
  75.5 1.4 %collective-permute-start.27 = (bf16[32,1024]{1,0:T(8,128)(2,1)S(1)}, bf16[32,1024]{1,0:T(8,128)(2,1)S(1)}, u32[]{:S(2)}, u32[]{:S(2)}) collective-permute-start(bf16[32,1024]{1,0:T(8,128)(2,1)S(1)} %collective-permute-done.23.refs_1_), channel_id=1, source_target_pairs={{0,4},{4,0},{8,12},{12,8},{16,20},{20,16},{24,28},{28,24},{1,5},{5... | collective-permute-start | bytes 196616 | tf_op jit(solution)/shard_map/ppermute | solution.py:65
  77.8 3.8 %collective-permute-start.30 = (bf16[32,256]{1,0:T(8,128)(2,1)S(1)}, bf16[32,256]{1,0:T(8,128)(2,1)S(1)}, u32[]{:S(2)}, u32[]{:S(2)}) collective-permute-start(bf16[32,256]{1,0:T(8,128)(2,1)S(1)} %get-tuple-element.89), channel_id=1, source_target_pairs={{0,1},{1,0},{2,3},{3,2},{4,5},{5,4},{6,7},{7,6},{8,9},{9,8},{10,11... | collective-permute-start | bytes 49160 | tf_op jit(solution)/shard_map/ppermute | solution.py:65
  78.5 4.6 %collective-permute-start.32 = (bf16[32,256]{1,0:T(8,128)(2,1)S(1)}, bf16[32,256]{1,0:T(8,128)(2,1)S(1)}, u32[]{:S(2)}, u32[]{:S(2)}) collective-permute-start(bf16[32,256]{1,0:T(8,128)(2,1)S(1)} %get-tuple-element.90), channel_id=1, source_target_pairs={{0,3},{1,2},{2,1},{3,0},{4,7},{5,6},{6,5},{7,4},{8,11},{9,10},{10,... | collective-permute-start | bytes 49160 | tf_op jit(solution)/shard_map/ppermute | solution.py:65
  80.0 3.7 %collective-permute-start.31 = (bf16[32,256]{1,0:T(8,128)(2,1)S(1)}, bf16[32,256]{1,0:T(8,128)(2,1)S(1)}, u32[]{:S(2)}, u32[]{:S(2)}) collective-permute-start(bf16[32,256]{1,0:T(8,128)(2,1)S(1)} %get-tuple-element.91), channel_id=1, source_target_pairs={{0,2},{1,3},{2,0},{3,1},{4,6},{5,7},{6,4},{7,5},{8,10},{9,11},{10,... | collective-permute-start | bytes 49160 | tf_op jit(solution)/shard_map/ppermute | solution.py:65

commit v3 on v2

v3 whole, which is shorter than its diff:
```python
import functools
import math

import jax
import jax.numpy as jnp
import numpy as np
from jax import lax
from jax.experimental import pallas as pl
from jax.experimental.pallas import tpu as pltpu
from jax.sharding import PartitionSpec as P

D = 2048
QUERY_HEADS = 32
KEY_VALUE_HEADS = 8
HEAD_SIZE = 64
GROUP = QUERY_HEADS // KEY_VALUE_HEADS
EPSILON = 1e-05
ROPE_BASE = 500000.0

HEADS = QUERY_HEADS // 2
KV_HEADS = KEY_VALUE_HEADS // 2
QW = HEADS * HEAD_SIZE
KW = KV_HEADS * HEAD_SIZE
HALF = QW + 2 * KW
LANES = 128
TILE = 256
WIDE = HALF + LANES
LOW = -1e30

BF16 = jnp.bfloat16
F32 = jnp.float32
SMEM = pl.BlockSpec(memory_space=pltpu.SMEM)
VMEM = pl.BlockSpec(memory_space=pltpu.VMEM)
HBM = pl.BlockSpec(memory_space=pltpu.HBM)


def mm(a, b):
    return lax.dot_general(a, b, (((1,), (0,)), ((), ())), preferred_element_type=F32)


def mm_t(a, b):
    return lax.dot_general(a, b, (((1,), (1,)), ((), ())), preferred_element_type=F32)


def lane_iota(shape):
    return lax.broadcasted_iota(jnp.int32, shape, len(shape) - 1)


def split(value):
    high = value.astype(BF16).astype(F32)
    low = (value - high).astype(BF16).astype(F32)
    return high, low


def tail_of(value):
    high, low = split(value)
    lane = lane_iota((value.shape[0], LANES))
    return jnp.where(lane == 0, high, jnp.where(lane == 1, low, 0.0))


def tail_sum(*tails):
    return tree([jnp.sum(tail.astype(F32), axis=-1, keepdims=True) for tail in tails])


def exchange(array, axis, size, mask):
    return lax.ppermute(array, axis, [(i, i ^ mask) for i in range(size)])


WIDE_ORDER, NARROW_ORDER, REQ_ORDER = (3, 1, 2), (3, 1, 2), (3, 2, 1)
LIMIT, LOOKUP_LIMIT, STAGE_LIMIT = 12, 53, 48


def direct(array, size, send, order):
    pick = (lambda k: array[k]) if isinstance(array, list) else (lambda k: array)
    order = [k for k in order if k < size] + [k for k in range(1, size) if k not in order]
    got = lax.optimization_barrier(tuple(send(pick(k), k) for k in order))
    return [pick(0)] + [got[order.index(k)] for k in range(1, size)]


def call(kernel, outs, ins, specs, scratch=(), limit=LIMIT, cost=None, name=None):
    return pl.pallas_call(
        kernel,
        out_shape=outs,
        in_specs=specs,
        out_specs=jax.tree.map(lambda _: VMEM, outs),
        scratch_shapes=list(scratch),
        compiler_params=pltpu.CompilerParams(vmem_limit_bytes=limit << 20),
        cost_estimate=cost,
        name=name,
    )(*ins)


def work(moved):
    return pl.CostEstimate(flops=0, transcendentals=0, bytes_accessed=moved)


def time_of(moved):
    return pl.CostEstimate(flops=256 * moved, transcendentals=0, bytes_accessed=0)


def here():
    seq, req = lax.axis_index("seq"), lax.axis_index("req")
    return seq & 1, seq >> 1, req, seq


def shape(dims, dtype):
    return jax.ShapeDtypeStruct(tuple(dims), dtype)


def lookup_kernel(rows, ids, table, out, blocks, taken, listed, sem):
    req_count, count = out.shape[0], out.shape[1]
    steps = ids.shape[0]
    vocab_dev, feat = table.shape
    me = here()[2]
    base = me * vocab_dev
    found = jnp.int32(0)
    for j in range(req_count * count):
        local = ids[j % steps, j // steps] - base
        listed[0, found] = j
        listed[1, found] = local
        found = found + ((local >= 0) & (local < vocab_dev)).astype(jnp.int32)

    def block_of(i):
        local = listed[1, i]
        first = jnp.minimum(local & -rows, vocab_dev - rows)
        return local - first, pltpu.make_async_copy(
            table.at[pl.ds(pl.multiple_of(first, 8), rows)], blocks.at[i], sem
        )

    @pl.loop(0, found)
    def _(i):
        block_of(i)[1].start()

    taken[...] = jnp.zeros(taken.shape, F32)
    at = lax.broadcasted_iota(jnp.int32, (rows, feat), 0)

    @pl.loop(0, found)
    def _(i):
        block_of(i)[1].wait()

    total = req_count * count
    batch = 8

    @pl.loop(0, lax.div(found + batch - 1, batch))
    def _(b):
        for u in range(batch):
            i = b * batch + u
            live = i < found
            j = jnp.where(live, listed[0, i], 0)
            local = jnp.where(live, listed[1, i], 0)
            row = jnp.where(live, local - jnp.minimum(local & -rows, vocab_dev - rows), -1)
            group = lax.div(j, count)
            to = jnp.where(live, (group ^ me) * count + (j - group * count), total)
            picked = jnp.where(at == row, blocks[i].astype(F32), 0.0)
            taken[pl.ds(to, 1), :] = jnp.sum(picked, axis=0, keepdims=True)

    out[...] = taken[:total, :].astype(BF16).reshape(out.shape)


def tables_kernel(starts, lens, when, cosine, sine, bias):
    half = HEAD_SIZE // 2
    lane = lane_iota(cosine.shape)
    freqs = jnp.exp((lane % half).astype(F32) * (-2.0 / HEAD_SIZE * math.log(ROPE_BASE)))
    angles = when[...] * freqs
    cosine[...] = jnp.cos(angles)
    sine[...] = jnp.where(lane % HEAD_SIZE < half, -1.0, 1.0) * jnp.sin(angles)
    me = here()[3]
    context = bias.shape[1] // 2
    spot = lane_iota((1, 2 * context))
    spot = jnp.where(spot < context, spot + me * context, spot - context + (me ^ 1) * context)
    for r in range(bias.shape[0]):
        bias[r : r + 1, :] = jnp.where((spot >= starts[r]) & (spot < lens[r]), 0.0, LOW)


def run_copies(copies, sems):
    copies = [pltpu.make_async_copy(a, b, sems.at[i]) for i, (a, b) in enumerate(copies)]
    for copy in copies:
        copy.start()
    for copy in copies:
        copy.wait()


def stage_cache_kernel(keys, keys2, values, values2, k_out, v_out, sems):
    requests, context = keys.shape[0], keys.shape[1]
    columns = pl.ds(pl.multiple_of(here()[0] * KW, KW), KW)
    run_copies(
        [
            (array.at[r, :, columns], out.at[r, pl.ds(i * context, context), :])
            for r in range(requests)
            for out, arrays in ((k_out, (keys, keys2)), (v_out, (values, values2)))
            for i, array in enumerate(arrays)
        ],
        sems,
    )


def stage_units_kernel(own, two, out, sems):
    feat, hid = own.shape[0], out.shape[1]
    core = here()[0]
    columns = pl.ds(pl.multiple_of(core * hid, LANES), hid)
    pieces = 8
    part = feat // pieces
    run_copies(
        [
            (array.at[pl.ds(p * part, part), columns], out.at[pl.ds(to * feat + p * part, part), :])
            for array, to in ((own, core), (two, 1 - core))
            for p in range(pieces)
        ],
        sems,
    )


def stage_out_kernel(o_own, o_two, out, sems):
    feat = o_own.shape[1]
    core = here()[0]
    pieces = 4
    part = QW // pieces
    run_copies(
        [
            (
                array.at[pl.ds(pl.multiple_of(core * QW + p * part, part), part), :],
                out.at[pl.ds(p * part, part), pl.ds(pl.multiple_of(to * feat, LANES), feat)],
            )
            for array, to in ((o_own, core), (o_two, 1 - core))
            for p in range(pieces)
        ],
        sems,
    )


def join_kernel(k, v, kv_two, k_out, v_out):
    first = here()[0] == 0
    for out, own, two in ((k_out, k, kv_two[:, :KW]), (v_out, v, kv_two[:, KW:])):
        own = own[...]
        pair = jnp.concatenate([jnp.where(first, own, two), jnp.where(first, two, own)], axis=1)
        out[...] = pair.reshape(out.shape)


def project_kernel(parts, gain, next_gain, weight, *refs):
    blocks, (x_out, keep, give) = refs[:parts], refs[parts:]
    x = blocks[0][...].astype(F32)
    for block in blocks[1:]:
        x = x + block[...].astype(F32)
    x_out[...] = x.astype(BF16)
    scaled = (x * gain[...].astype(F32)).astype(BF16)
    tail = tail_of(jnp.sum(x * x, axis=-1, keepdims=True)).astype(BF16)
    first = here()[0] == 0
    q_end, k_end = 2 * QW, 2 * QW + 2 * KW
    at = 0
    for start, width in ((0, QW), (q_end, KW), (k_end, KW)):
        for tile in range(start, start + width, TILE):
            one = mm(scaled, weight[:, tile : tile + TILE]).astype(BF16)
            two = mm(scaled, weight[:, tile + width : tile + width + TILE]).astype(BF16)
            keep[:, at : at + TILE] = jnp.where(first, one, two)
            give[:, at : at + TILE] = jnp.where(first, two, one)
            at += TILE
    keep[:, HALF:] = tail
    give[:, HALF:WIDE] = tail
    feat = x.shape[1]
    give[:, WIDE : WIDE + feat] = x.astype(BF16)
    give[:, WIDE + feat :] = jnp.broadcast_to(next_gain[...], x.shape)


def tree(values):
    while len(values) > 1:
        values = [values[i] + values[i + 1] for i in range(0, len(values), 2)]
    return values[0]


def add_kernel(a, b, out):
    out[:, :HALF] = (a[:, :HALF].astype(F32) + b[:, :HALF].astype(F32)).astype(BF16)
    out[:, HALF:] = tail_of(tail_sum(a[:, HALF:], b[:, HALF:WIDE])).astype(BF16)


def rotate(v, cosine, sine):
    width = v.shape[-1]
    lane = lane_iota(v.shape)
    half = HEAD_SIZE // 2
    ahead = pltpu.roll(v, width - half, 1)
    behind = pltpu.roll(v, half, 1)
    other = jnp.where(lane % HEAD_SIZE < half, ahead, behind)
    reps = width // LANES
    cosine = jnp.concatenate([cosine] * reps, axis=1)
    sine = jnp.concatenate([sine] * reps, axis=1)
    return v * cosine + other * sine


def attend_kernel(steps, parts, cosine, sine, bias, keys, values, *refs):
    sums, (packed, new_k, new_v, q_rows, o_rows, tops, totals) = refs[:parts], refs[parts:]
    count = packed.shape[0]
    requests = count // steps
    rows = steps * HEADS
    z = here()[1]
    total = tree([block[:, :HALF].astype(F32) for block in sums])
    squares = tail_sum(*[block[:, HALF:] for block in sums])
    total = total * lax.rsqrt(squares / D + EPSILON)
    q = rotate(total[:, :QW], cosine[...], sine[...]).astype(BF16)
    k = rotate(total[:, QW : QW + KW], cosine[...], sine[...]).astype(BF16)
    v = total[:, QW + KW :].astype(BF16)
    new_k[...] = k
    new_v[...] = v

    q = q.astype(F32) * (1.0 / math.sqrt(HEAD_SIZE))
    lane = lane_iota((count, LANES))
    per = LANES // HEAD_SIZE
    q_rows[...] = jnp.zeros(q_rows.shape, F32)

    def column(index):
        return slice(index // per * LANES, index // per * LANES + LANES)

    def move(block, at, to):
        return block if at % per == to % per else pltpu.roll(block, HEAD_SIZE, 1)

    for h in range(HEADS):
        kv = h // GROUP
        block = move(q[:, column(h)], h, kv)
        block = jnp.where(lane // HEAD_SIZE == kv % per, block, 0.0)
        q_rows[kv // per, pl.ds(h, count, stride=HEADS), :] = block

    row_step = lax.broadcasted_iota(jnp.int32, (rows, count), 0) // HEADS
    fresh_at = lane_iota((rows, count))
    ats = [slice(r * rows, (r + 1) * rows) for r in range(requests)]
    q_all = [
        jnp.concatenate([q_rows[i, at, :] for i in range(KW // LANES)], axis=1).astype(BF16)
        for at in ats
    ]
    fresh = mm_t(jnp.concatenate(q_all, axis=0), k)
    raw = [mm_t(q_all[r], keys[r]) for r in range(requests)]
    weights = []
    for r, at in enumerate(ats):
        seen_f = (fresh_at >= r * steps) & (fresh_at <= r * steps + row_step) & (z == 0)
        sc = raw[r] + bias[r : r + 1, :]
        sf = jnp.where(seen_f, fresh[at], LOW)
        top = jnp.maximum(jnp.max(sc, axis=-1, keepdims=True), jnp.max(sf, axis=-1, keepdims=True))
        top_high, top_low = split(jnp.maximum(top, LOW / 2))
        top = top_high + top_low
        pc = jnp.exp(sc - top)
        pf = jnp.exp(sf - top)
        weight = jnp.sum(pc, axis=-1, keepdims=True) + jnp.sum(pf, axis=-1, keepdims=True)
        tops[at, :] = jnp.broadcast_to(top, (rows, LANES))
        totals[at, :] = jnp.broadcast_to(weight, (rows, LANES))
        weights.append((pc.astype(BF16), pf.astype(BF16)))
    for r, at in enumerate(ats):
        o = mm(weights[r][0], values[r]) + mm(weights[r][1], v)
        for i in range(KW // LANES):
            o_rows[i, at, :] = o[:, i * LANES : (i + 1) * LANES]

    top = jnp.zeros((count, LANES), F32)
    weight = jnp.zeros((count, LANES), F32)
    for first in range(0, HEADS, per):
        heads = range(first, first + per)
        blocks = [
            move(o_rows[h // GROUP // per, pl.ds(h, count, stride=HEADS), :], h // GROUP, h)
            for h in heads
        ]
        block = blocks[0]
        for i in range(1, per):
            block = jnp.where(lane // HEAD_SIZE == i, blocks[i], block)
        packed[:, column(first)] = block.astype(BF16)
        for h in heads:
            top = jnp.where(lane == h, tops[pl.ds(h, count, stride=HEADS), :], top)
            weight = jnp.where(lane == h, totals[pl.ds(h, count, stride=HEADS), :], weight)
    packed[:, QW:] = sum(
        pltpu.roll(part, i * HEADS, 1) if i else part
        for i, part in enumerate((*split(top), *split(weight)))
    ).astype(BF16)


def read_stats(block):
    block = block.astype(F32)
    both = block + pltpu.roll(block, LANES - HEADS, 1)
    return both, pltpu.roll(both, LANES - 2 * HEADS, 1)


def pack_factors(factor):
    lane = lane_iota(factor.shape)
    high, low = split(factor)
    low = pltpu.roll(low, HEADS, 1)
    return jnp.where(lane < HEADS, high, jnp.where(lane < 2 * HEADS, low, 0.0)).astype(BF16)


def output_kernel(parts, spread, weight, *refs):
    blocks, out = refs[:parts], refs[parts]
    stats = [read_stats(block[:, QW:]) for block in blocks]
    top = functools.reduce(jnp.maximum, [stat[0] for stat in stats])
    factors = [jnp.exp(stat[0] - top) for stat in stats]
    total = sum(stat[1] * factor for stat, factor in zip(stats, factors))
    inverse = 1.0 / jnp.where(lane_iota(top.shape) < HEADS, total, 1.0)
    count = out.shape[0]
    packed = jnp.concatenate([pack_factors(factor * inverse) for factor in factors], axis=0)
    wide = []
    for tile in range(0, QW, TILE):
        at = slice(tile, tile + TILE)
        spreads = mm(packed, spread[:, at])
        wide.append(
            sum(
                spreads[i * count : (i + 1) * count] * block[:, at].astype(F32)
                for i, block in enumerate(blocks)
            ).astype(BF16)
        )
    out[...] = mm(jnp.concatenate(wide, axis=1), weight[...])


def gate_kernel(parts, gains, w_gate, w_up, *refs):
    blocks, (out, rows_ref) = refs[:parts], refs[parts:]
    count = blocks[0].shape[0]
    for i, block in enumerate(blocks):
        rows_ref[i * count : (i + 1) * count, :] = block[...]
    z = here()[1]
    chunks, size = out.shape[0], out.shape[1]
    taken = [
        rows_ref[pl.ds(pl.multiple_of((z ^ j) * size, size), size), :].astype(F32)
        for j in range(chunks)
    ]
    x = jnp.concatenate(taken, axis=0)
    squares = jnp.sum(x * x, axis=-1, keepdims=True)
    scaled = (x * gains[...].astype(F32)).astype(BF16)
    hid = w_gate.shape[1]
    tile = min(TILE, hid)
    for base, weight in ((0, w_gate), (hid, w_up)):
        for start in range(0, hid, tile):
            terms = mm(scaled, weight[:, start : start + tile]).astype(BF16)
            for j in range(chunks):
                out[j, :, base + start : base + start + tile] = terms[j * size : (j + 1) * size]
    tail = tail_of(squares).astype(BF16)
    for j in range(chunks):
        out[j, :, 2 * hid :] = tail[j * size : (j + 1) * size]


def hidden_kernel(parts, *refs):
    blocks, out = refs[:parts], refs[parts]
    hid = out.shape[1]
    total = blocks[0][:, : 2 * hid].astype(F32)
    for block in blocks[1:]:
        total = total + block[:, : 2 * hid].astype(F32)
    squares = tail_sum(*[block[:, 2 * hid :] for block in blocks])
    inverse = lax.rsqrt(squares / D + EPSILON)
    gate, up = total[:, :hid] * inverse, total[:, hid:] * inverse
    out[...] = (gate / (1.0 + jnp.exp(-gate)) * up).astype(BF16)


def down_kernel(parts, w_down, *refs):
    mine, theirs, (out, rows_ref) = refs[:parts], refs[parts : 2 * parts], refs[2 * parts :]
    core, z = here()[:2]
    size, hid = mine[0].shape
    near = jnp.concatenate([ref[...] for ref in mine], axis=0)
    far = jnp.concatenate([ref[...] for ref in theirs], axis=0)
    total = mm(near, w_down[pl.ds(pl.multiple_of(core * hid, hid), hid), :]) + mm(
        far, w_down[pl.ds(pl.multiple_of((1 - core) * hid, hid), hid), :]
    )
    for j in range(parts):
        rows_ref[pl.ds(pl.multiple_of((z ^ j) * size, size), size), :] = total[
            j * size : (j + 1) * size
        ]
    count = out.shape[1]
    for k in range(out.shape[0]):
        out[k] = rows_ref[k * count : (k + 1) * count, :].astype(BF16)


def shards(
    seq_size,
    req_size,
    token_ids,
    embed_table,
    cache_len,
    range_start,
    positions,
    cached_key_rows,
    cached_value_rows,
    attn_gain,
    mlp_gain,
    w_qkv,
    w_out,
    w_gate,
    w_up,
    w_down,
):
    requests, steps = cache_len.shape[0], token_ids.shape[1]
    count = requests * steps
    feat = embed_table.shape[1]
    core = lax.axis_index("seq") % 2
    depth = seq_size // 2
    swap = lambda array: exchange(array, "seq", seq_size, 1)
    over_z = lambda array, mask: exchange(array, "seq", seq_size, 2 * mask)
    over_req = lambda array, mask: exchange(array, "req", req_size, mask)

    rows = 16
    found = call(
        functools.partial(lookup_kernel, rows),
        shape((req_size, count, feat), BF16),
        (token_ids.T, embed_table),
        [SMEM, HBM],
        [
            pltpu.VMEM((req_size * count, rows, feat), BF16),
            pltpu.VMEM((req_size * count + 8, feat), F32),
            pltpu.SMEM((2, req_size * count + 1), jnp.int32),
            pltpu.SemaphoreType.DMA,
        ],
        limit=LOOKUP_LIMIT,
        name="lookup",
    )
    blocks = direct([found[k] for k in range(req_size)], req_size, over_req, REQ_ORDER)
    hid = w_gate.shape[1] // 2
    context = cached_key_rows.shape[1]
    when = (positions[:, None] + jnp.arange(steps, dtype=jnp.int32)[None, :]).astype(F32)
    cosine, sine, bias = call(
        tables_kernel,
        (shape((count, LANES), F32),) * 2 + (shape((requests, 2 * context), F32),),
        (range_start, cache_len, when.reshape(count, 1)),
        [SMEM, SMEM, VMEM],
        cost=work(1 << 20),
        name="tables",
    )
    *blocks, cosine, sine, bias = lax.optimization_barrier((*blocks, cosine, sine, bias))

    keys2, values2 = swap(cached_key_rows), swap(cached_value_rows)
    *blocks, keys2, values2 = lax.optimization_barrier((*blocks, keys2, values2))
    next_gain = mlp_gain.reshape(1, feat)

    x, keep, give = call(
        functools.partial(project_kernel, req_size),
        (
            shape((count, feat), BF16),
            shape((count, WIDE), BF16),
            shape((count, WIDE + 2 * feat), BF16),
        ),
        (attn_gain.reshape(1, feat), next_gain, w_qkv, *blocks),
        [VMEM] * (3 + req_size),
        name="project",
    )
    got = swap(give)
    mine = call(add_kernel, shape((count, WIDE), BF16), (keep, got), [VMEM] * 2, name="add")
    sums = direct(mine, depth, over_z, WIDE_ORDER)
    _, w_gate, w_out = lax.optimization_barrier((mine, w_gate, w_out))
    gate2, out2 = swap(w_gate), swap(w_out)
    keys, values = call(
        stage_cache_kernel,
        (shape((requests, 2 * context, KW), BF16),) * 2,
        (cached_key_rows, keys2, cached_value_rows, values2),
        [HBM] * 4,
        [pltpu.SemaphoreType.DMA((4 * requests,))],
        cost=time_of(8 * requests * context * KW * 2),
        limit=STAGE_LIMIT,
        name="stage_cache",
    )
    *sums, keys, values, gate2, out2 = lax.optimization_barrier((*sums, keys, values, gate2, out2))

    spread = jnp.asarray(
        (np.arange(LANES)[:, None] % HEADS == np.arange(QW)[None, :] // HEAD_SIZE)
        & (np.arange(LANES)[:, None] < 2 * HEADS),
        BF16,
    )
    packed_width = QW + LANES
    packed, new_k, new_v = call(
        functools.partial(attend_kernel, steps, len(sums)),
        (shape((count, packed_width), BF16), shape((count, KW), BF16), shape((count, KW), BF16)),
        (cosine, sine, bias, keys, values, *sums),
        [VMEM] * (5 + len(sums)),
        [pltpu.VMEM((KW // LANES, count * HEADS, LANES), F32)] * 2
        + [pltpu.VMEM((count * HEADS, LANES), F32)] * 2,
        name="attend",
    )
    partials = direct(packed, depth, over_z, NARROW_ORDER)
    o_pair = call(
        stage_out_kernel,
        shape((QW, 2 * feat), BF16),
        (w_out, out2),
        [HBM] * 2,
        [pltpu.SemaphoreType.DMA((8,))],
        cost=work(4 * feat * QW * 2),
        limit=STAGE_LIMIT,
        name="stage_out",
    )
    def stage_units(own, two):
        return call(
            stage_units_kernel,
            shape((2 * feat, hid), BF16),
            (own, two),
            [HBM] * 2,
            [pltpu.SemaphoreType.DMA((16,))],
            cost=work(4 * feat * hid * 2),
            limit=STAGE_LIMIT,
            name="stage_units",
        )

    _, w_up = lax.optimization_barrier((packed, w_up))
    up2 = swap(w_up)
    g_pair = stage_units(w_gate, gate2)
    *partials, o_pair, g_pair, up2 = lax.optimization_barrier((*partials, o_pair, g_pair, up2))
    part = call(
        functools.partial(output_kernel, depth),
        shape((count, 2 * feat), F32),
        (spread, o_pair, *partials),
        [VMEM] * (2 + depth),
        name="output",
    )
    pair = lambda own, two: jnp.where(
        core == 0, jnp.concatenate([own, two], axis=1), jnp.concatenate([two, own], axis=1)
    )
    x_pair = pair(x, got[:, WIDE : WIDE + feat])
    gain_pair = pair(next_gain, got[0:1, WIDE + feat :])
    resid = (x_pair.astype(F32) + (part + swap(part))).astype(BF16)

    _, new_k, new_v = lax.optimization_barrier((part, new_k, new_v))
    kv_two = swap(jnp.concatenate([new_k, new_v], axis=1))
    taken = direct(resid, req_size, over_req, REQ_ORDER)
    u_pair = stage_units(w_up, up2)
    *taken, u_pair = lax.optimization_barrier((*taken, u_pair))
    size = req_size * count // depth
    terms = call(
        functools.partial(gate_kernel, req_size),
        shape((depth, size, 2 * hid + LANES), BF16),
        (gain_pair, g_pair, u_pair, *taken),
        [VMEM] * (3 + req_size),
        [pltpu.VMEM((req_size * count, 2 * feat), BF16)],
        name="gate",
    )
    sums = direct([terms[j] for j in range(depth)], depth, over_z, WIDE_ORDER)
    all_k, all_v = call(
        join_kernel,
        (shape((requests, steps, 2 * KW), BF16),) * 2,
        (new_k, new_v, kv_two),
        [VMEM] * 3,
        cost=work(1 << 20),
        name="join",
    )
    *sums, all_k, all_v = lax.optimization_barrier((*sums, all_k, all_v))
    hidden = call(
        functools.partial(hidden_kernel, depth),
        shape((size, hid), BF16),
        sums,
        [VMEM] * depth,
        name="hidden",
    )
    near = direct(hidden, depth, over_z, NARROW_ORDER)
    far = [swap(block) for block in near]
    back = call(
        functools.partial(down_kernel, depth),
        shape((req_size, count, feat), BF16),
        (w_down, *near, *far),
        [VMEM] * (1 + 2 * depth),
        [pltpu.VMEM((req_size * count, feat), F32)],
        name="down",
    )
    total = sum(
        block.astype(F32)
        for block in direct([back[k] for k in range(req_size)], req_size, over_req, REQ_ORDER)
    )
    resid_own = lax.dynamic_slice_in_dim(resid, core * feat, feat, axis=1)
    layer_out = (resid_own.astype(F32) + total).astype(BF16).reshape(requests, steps, feat)
    return layer_out, all_k, all_v


def solution(mesh):
    in_specs = (
        P(),
        P("req", "seq"),
        P("req"),
        P("req"),
        P("req"),
        P("req", "seq", None),
        P("req", "seq", None),
        P("seq"),
        P("seq"),
        P("seq", None),
        P(None, "seq"),
        P("seq", "req"),
        P("seq", "req"),
        P("req", "seq"),
    )
    out_specs = (P("req", None, "seq"), P("req", None, None), P("req", None, None))
    body = functools.partial(shards, mesh.shape["seq"], mesh.shape["req"])
    return jax.shard_map(body, mesh=mesh, in_specs=in_specs, out_specs=out_specs, check_vma=False)
```

time: 84.7 us -> 79.5 us (0.939)
  Pallas kernels: 18.6 us -> 11.3 us
  waiting for transfers between devices: 31.1 us -> 32.3 us
  starting transfers between devices: 30.4 us -> 31.5 us
    pallas_call x12 -> x14, Pallas kernels: 18.6 us -> 11.3 us  [call(): pl.pallas_call(kernel, out_shape=outs, in_specs=specs, out_specs=jax.tree...]
    ppermute x33, waiting for transfers between devices: 31.1 us -> 32.3 us  [exchange(): return lax.ppermute(array, axis, [(i, i ^ mask) for i in range(size)])]
    ppermute x33, starting transfers between devices: 30.4 us -> 31.5 us  [exchange(): return lax.ppermute(array, axis, [(i, i ^ mask) for i in range(size)])]
  transfers between devices with their start and end apart: 33 -> 33, of which waited for: 19 -> 25; matrix products, arithmetic and copies ran while one was open for 0% -> 0% of each run, Pallas kernels for 11% -> 10%
where the time goes in v3:
time: 79.5 us; the launch traced here: 79.2 us
  waiting for transfers between devices  32.3 us (41%)
  starting transfers between devices  31.5 us (40%)
  Pallas kernels  11.3 us (14%)
  local copies, waits for them, and re-layouts  3.06 us (4%)
  between operations  0.92 us (1%)
    ppermute x33, waiting for transfers between devices, exchange(): return lax.ppermute(array, axis, [(i, i ^ mask) for i in range(size)])  32.3 us
    ppermute x33, starting transfers between devices, exchange(): return lax.ppermute(array, axis, [(i, i ^ mask) for i in range(size)])  31.5 us
    pallas_call x14, Pallas kernels, call(): pl.pallas_call(kernel, out_shape=outs, in_specs=specs, out_specs=jax.tree...  11.3 us
    unnamed x28, local copies, waits for them, and re-layouts  2.3 us
  transfers between devices with their start and end apart: 33, of which 25 were waited for; matrix products, arithmetic and copies ran while one was open for 0% of the time, Pallas kernels for 10%

profile of v3, /device:TPU:0, one launch (start us, length us, event | category | flops | bytes accessed | tf_op | source)
XLA Modules:
  0.0 79.2 jit_solution(6888794256335264470)
XLA Ops:
  0.6 0.5 collective-permute-start.3
  1.2 0.7 copy-done.8
  1.9 2.5 %lookup.1 = bf16[4,32,256]{2,1,0:T(8,128)(2,1)S(1)} custom-call(s32[4,32]{1,0:T(4,128)S(1)} %bitcast.28, bf16[16032,256]{1,0:T(8,128)(2,1)} %table.1), custom_call_target="tpu_custom_call" | custom-call | tf_op jit(solution)/shard_map/lookup/pallas_call | solution.py:81
  4.5 4.1 %collective-permute-start = (bf16[32,256]{1,0:T(8,128)(2,1)S(1)}, bf16[32,256]{1,0:T(8,128)(2,1)S(1)}, u32[]{:S(2)}, u32[]{:S(2)}) collective-permute-start(bf16[32,256]{1,0:T(8,128)(2,1)S(1)} %get-tuple-element.168), channel_id=1, source_target_pairs={{0,3},{1,2},{2,1},{3,0},{4,7},{5,6},{6,5},{7,4},{8,11},{9,10},{10,... | collective-permute-start | bytes 49160 | tf_op jit(solution)/shard_map/ppermute | solution.py:66
  8.6 0.2 collective-permute-start.1
  8.8 0.5 collective-permute-start.2
  9.5 0.7 tables.1
  10.2 0.2 collective-permute-done.refs_3_
  10.3 2.0 %collective-permute-done.1.refs_2_ = bf16[32,256]{1,0:T(8,128)(2,1)S(1)} collective-permute-done((bf16[32,256]{1,0:T(8,128)(2,1)S(1)}, bf16[32,256]{1,0:T(8,128)(2,1)S(1)}, u32[]{:S(2)}, u32[]{:S(2)}) %collective-permute-start.1) | collective-permute-done | bytes 16416 | tf_op jit(solution)/shard_map/ppermute | solution.py:66
  12.4 0.2 collective-permute-done.2.refs_1_
  12.6 0.4 project.1
  13.0 1.3 %collective-permute-done.5.b = bf16[32,2176]{1,0:T(8,128)(2,1)S(1)} collective-permute-done((bf16[32,2176]{1,0:T(8,128)(2,1)S(1)}, bf16[32,2176]{1,0:T(8,128)(2,1)S(1)}, u32[]{:S(2)}, u32[]{:S(2)}) %collective-permute-start.5) | collective-permute-done | bytes 139296 | tf_op jit(solution)/shard_map/ppermute | solution.py:66
  14.5 0.2 collective-permute-start.10
  14.7 0.4 collective-permute-start.9
  15.0 3.6 %collective-permute-start.6 = (bf16[32,1664]{1,0:T(8,128)(2,1)S(1)}, bf16[32,1664]{1,0:T(8,128)(2,1)S(1)}, u32[]{:S(2)}, u32[]{:S(2)}) collective-permute-start(bf16[32,1664]{1,0:T(8,128)(2,1)S(1)} %add.87.refs_0_), channel_id=1, source_target_pairs={{0,24},{4,28},{8,16},{12,20},{16,8},{20,12},{24,0},{28,4},{1,25},{... | collective-permute-start | bytes 319496 | tf_op jit(solution)/shard_map/ppermute | solution.py:66
  18.6 0.8 collective-permute-start.8
  19.4 2.5 %stage_cache.1 = (bf16[8,512,256]{2,1,0:T(8,128)(2,1)S(1)}, bf16[8,512,256]{2,1,0:T(8,128)(2,1)S(1)}) custom-call(bf16[8,256,512]{2,1,0:T(8,128)(2,1)} %keys.1, bf16[8,256,512]{2,1,0:T(8,128)(2,1)} %collective-permute-done.3.keys2, bf16[8,256,512]{2,1,0:T(8,128)(2,1)} %values.1, bf16[8,256,512]{2,1,0:T(8,128)(2,1)} %collective-permute-done.4.values2), custom_call_target="tpu_custom_call" | custom-call | flops 2147483648 | tf_op jit(solution)/shard_map/stage_cache/pallas_call | solution.py:81
  21.9 0.7 collective-permute-done.6.refs_3_
  22.7 2.6 %collective-permute-done.7.refs_1_ = bf16[32,1664]{1,0:T(8,128)(2,1)S(1)} collective-permute-done((bf16[32,1664]{1,0:T(8,128)(2,1)S(1)}, bf16[32,1664]{1,0:T(8,128)(2,1)S(1)}, u32[]{:S(2)}, u32[]{:S(2)}) %collective-permute-start.7) | collective-permute-done | bytes 106528 | tf_op jit(solution)/shard_map/ppermute | solution.py:66
  25.3 2.6 %collective-permute-done.8.refs_2_ = bf16[32,1664]{1,0:T(8,128)(2,1)S(1)} collective-permute-done((bf16[32,1664]{1,0:T(8,128)(2,1)S(1)}, bf16[32,1664]{1,0:T(8,128)(2,1)S(1)}, u32[]{:S(2)}, u32[]{:S(2)}) %collective-permute-start.8) | collective-permute-done | bytes 106528 | tf_op jit(solution)/shard_map/ppermute | solution.py:66
  27.9 1.7 %attend.1 = (bf16[32,1152]{1,0:T(8,128)(2,1)S(1)}, bf16[32,256]{1,0:T(8,128)(2,1)S(1)}, bf16[32,256]{1,0:T(8,128)(2,1)S(1)}) custom-call(f32[32,128]{1,0:T(8,128)S(1)} %get-tuple-element.97.cosine, f32[32,128]{1,0:T(8,128)S(1)} %get-tuple-element.98.sine, f32[8,512]{1,0:T(8,128)S(1)} %get-tuple-element.99.bias, ...), custom_call_target="tpu_custom_call" | custom-call | tf_op jit(solution)/shard_map/attend/pallas_call | solution.py:81
  29.7 2.5 %collective-permute-start.11 = (bf16[32,1152]{1,0:T(8,128)(2,1)S(1)}, bf16[32,1152]{1,0:T(8,128)(2,1)S(1)}, u32[]{:S(2)}, u32[]{:S(2)}) collective-permute-start(bf16[32,1152]{1,0:T(8,128)(2,1)S(1)} %get-tuple-element.124.refs_0_), channel_id=1, source_target_pairs={{0,24},{4,28},{8,16},{12,20},{16,8},{20,12},{24,0},{28,4},{1,25},{... | collective-permute-start | bytes 221192 | tf_op jit(solution)/shard_map/ppermute | solution.py:66
  32.2 1.9 %collective-permute-start.13 = (bf16[32,1152]{1,0:T(8,128)(2,1)S(1)}, bf16[32,1152]{1,0:T(8,128)(2,1)S(1)}, u32[]{:S(2)}, u32[]{:S(2)}) collective-permute-start(bf16[32,1152]{1,0:T(8,128)(2,1)S(1)} %get-tuple-element.124.refs_0_), channel_id=1, source_target_pairs={{0,16},{4,20},{8,24},{12,28},{16,0},{20,4},{24,8},{28,12},{1,17},{... | collective-permute-start | bytes 221192 | tf_op jit(solution)/shard_map/ppermute | solution.py:66
  34.2 0.5 stage_units.2.w_gate
  34.7 0.2 stage_out.1.weight
  34.9 1.8 %collective-permute-done.11.refs_3_ = bf16[32,1152]{1,0:T(8,128)(2,1)S(1)} collective-permute-done((bf16[32,1152]{1,0:T(8,128)(2,1)S(1)}, bf16[32,1152]{1,0:T(8,128)(2,1)S(1)}, u32[]{:S(2)}, u32[]{:S(2)}) %collective-permute-start.11) | collective-permute-done | bytes 73760 | tf_op jit(solution)/shard_map/ppermute | solution.py:66
  36.7 2.7 %collective-permute-done.12.refs_1_ = bf16[32,1152]{1,0:T(8,128)(2,1)S(1)} collective-permute-done((bf16[32,1152]{1,0:T(8,128)(2,1)S(1)}, bf16[32,1152]{1,0:T(8,128)(2,1)S(1)}, u32[]{:S(2)}, u32[]{:S(2)}) %collective-permute-start.12) | collective-permute-done | bytes 73760 | tf_op jit(solution)/shard_map/ppermute | solution.py:66
  39.4 0.6 output.1
  40.0 0.3 copy-done.4
  40.4 1.2 %collective-permute-done.15 = f32[32,512]{1,0:T(8,128)S(1)} collective-permute-done((f32[32,512]{1,0:T(8,128)S(1)}, f32[32,512]{1,0:T(8,128)S(1)}, u32[]{:S(2)}, u32[]{:S(2)}) %collective-permute-start.15) | collective-permute-done | bytes 65568 | tf_op jit(solution)/shard_map/ppermute | solution.py:66
  41.6 1.9 %collective-permute-start.16 = (bf16[32,512]{1,0:T(8,128)(2,1)S(1)}, bf16[32,512]{1,0:T(8,128)(2,1)S(1)}, u32[]{:S(2)}, u32[]{:S(2)}) collective-permute-start(bf16[32,512]{1,0:T(8,128)(2,1)S(1)} %add_convert_fusion.refs_0_), channel_id=1, source_target_pairs={{0,3},{1,2},{2,1},{3,0},{4,7},{5,6},{6,5},{7,4},{8,11},{9,10},{10,... | collective-permute-start | bytes 98312 | tf_op jit(solution)/shard_map/ppermute | solution.py:66
  43.5 0.3 collective-permute-start.17
  43.8 1.4 %collective-permute-start.18 = (bf16[32,512]{1,0:T(8,128)(2,1)S(1)}, bf16[32,512]{1,0:T(8,128)(2,1)S(1)}, u32[]{:S(2)}, u32[]{:S(2)}) collective-permute-start(bf16[32,512]{1,0:T(8,128)(2,1)S(1)} %add_convert_fusion.refs_0_), channel_id=1, source_target_pairs={{0,1},{1,0},{2,3},{3,2},{4,5},{5,4},{6,7},{7,6},{8,9},{9,8},{10,11... | collective-permute-start | bytes 98312 | tf_op jit(solution)/shard_map/ppermute | solution.py:66
  45.2 1.2 %copy-done.5 = bf16[256,2048]{1,0:T(8,128)(2,1)S(1)} copy-done((bf16[256,2048]{1,0:T(8,128)(2,1)S(1)}, bf16[256,2048]{1,0:T(8,128)(2,1)}, u32[]{:S(2)}) %copy-start.5) | copy-done | bytes 1048600
  46.4 0.5 stage_units.3.w_up
  46.9 0.5 collective-permute-done.17.refs_2_
  47.5 0.3 collective-permute-done.18.refs_1_
  47.7 0.5 gate.1
  48.2 1.8 %collective-permute-start.19 = (bf16[32,2176]{1,0:T(8,128)(2,1)S(1)}, bf16[32,2176]{1,0:T(8,128)(2,1)S(1)}, u32[]{:S(2)}, u32[]{:S(2)}) collective-permute-start(bf16[32,2176]{1,0:T(8,128)(2,1)S(1)} %get-tuple-element.161), channel_id=1, source_target_pairs={{0,24},{4,28},{8,16},{12,20},{16,8},{20,12},{24,0},{28,4},{1,25},{... | collective-permute-start | bytes 417800 | tf_op jit(solution)/shard_map/ppermute | solution.py:66
  50.1 0.4 collective-permute-start.20
  50.5 2.2 %collective-permute-start.21 = (bf16[32,2176]{1,0:T(8,128)(2,1)S(1)}, bf16[32,2176]{1,0:T(8,128)(2,1)S(1)}, u32[]{:S(2)}, u32[]{:S(2)}) collective-permute-start(bf16[32,2176]{1,0:T(8,128)(2,1)S(1)} %get-tuple-element.159), channel_id=1, source_target_pairs={{0,16},{4,20},{8,24},{12,28},{16,0},{20,4},{24,8},{28,12},{1,17},{... | collective-permute-start | bytes 417800 | tf_op jit(solution)/shard_map/ppermute | solution.py:66
  52.7 1.2 %collective-permute-done.22.kv_two = bf16[32,512]{1,0:T(8,128)(2,1)S(1)} collective-permute-done((bf16[32,512]{1,0:T(8,128)(2,1)S(1)}, bf16[32,512]{1,0:T(8,128)(2,1)S(1)}, u32[]{:S(2)}, u32[]{:S(2)}) %collective-permute-start.22) | collective-permute-done | bytes 32800 | tf_op jit(solution)/shard_map/ppermute | solution.py:66
  53.9 0.6 join.1
  54.5 2.3 %collective-permute-done.19.refs_3_ = bf16[32,2176]{1,0:T(8,128)(2,1)S(1)} collective-permute-done((bf16[32,2176]{1,0:T(8,128)(2,1)S(1)}, bf16[32,2176]{1,0:T(8,128)(2,1)S(1)}, u32[]{:S(2)}, u32[]{:S(2)}) %collective-permute-start.19) | collective-permute-done | bytes 139296 | tf_op jit(solution)/shard_map/ppermute | solution.py:66
  56.8 1.6 %collective-permute-done.20.refs_1_ = bf16[32,2176]{1,0:T(8,128)(2,1)S(1)} collective-permute-done((bf16[32,2176]{1,0:T(8,128)(2,1)S(1)}, bf16[32,2176]{1,0:T(8,128)(2,1)S(1)}, u32[]{:S(2)}, u32[]{:S(2)}) %collective-permute-start.20) | collective-permute-done | bytes 139296 | tf_op jit(solution)/shard_map/ppermute | solution.py:66
  58.4 3.6 %collective-permute-done.21.refs_2_ = bf16[32,2176]{1,0:T(8,128)(2,1)S(1)} collective-permute-done((bf16[32,2176]{1,0:T(8,128)(2,1)S(1)}, bf16[32,2176]{1,0:T(8,128)(2,1)S(1)}, u32[]{:S(2)}, u32[]{:S(2)}) %collective-permute-start.21) | collective-permute-done | bytes 139296 | tf_op jit(solution)/shard_map/ppermute | solution.py:66
  62.0 0.2 hidden.1.refs_0_
  62.2 2.7 %collective-permute-start.23 = (bf16[32,1024]{1,0:T(8,128)(2,1)S(1)}, bf16[32,1024]{1,0:T(8,128)(2,1)S(1)}, u32[]{:S(2)}, u32[]{:S(2)}) collective-permute-start(bf16[32,1024]{1,0:T(8,128)(2,1)S(1)} %hidden.1.refs_0_), channel_id=1, source_target_pairs={{0,24},{4,28},{8,16},{12,20},{16,8},{20,12},{24,0},{28,4},{1,25},{... | collective-permute-start | bytes 196616 | tf_op jit(solution)/shard_map/ppermute | solution.py:66
  65.0 1.7 %collective-permute-start.25 = (bf16[32,1024]{1,0:T(8,128)(2,1)S(1)}, bf16[32,1024]{1,0:T(8,128)(2,1)S(1)}, u32[]{:S(2)}, u32[]{:S(2)}) collective-permute-start(bf16[32,1024]{1,0:T(8,128)(2,1)S(1)} %hidden.1.refs_0_), channel_id=1, source_target_pairs={{0,16},{4,20},{8,24},{12,28},{16,0},{20,4},{24,8},{28,12},{1,17},{... | collective-permute-start | bytes 196616 | tf_op jit(solution)/shard_map/ppermute | solution.py:66
  66.7 2.2 %collective-permute-done.23.refs_3_ = bf16[32,1024]{1,0:T(8,128)(2,1)S(1)} collective-permute-done((bf16[32,1024]{1,0:T(8,128)(2,1)S(1)}, bf16[32,1024]{1,0:T(8,128)(2,1)S(1)}, u32[]{:S(2)}, u32[]{:S(2)}) %collective-permute-start.23) | collective-permute-done | bytes 65568 | tf_op jit(solution)/shard_map/ppermute | solution.py:66
  68.9 0.5 collective-permute-done.24.refs_1_
  69.4 0.7 collective-permute-done.25.refs_2_
  70.2 0.5 collective-permute-start.28
  70.7 0.7 collective-permute-done.27.refs_5_
  71.4 0.2 collective-permute-done.28.refs_6_
  71.6 0.4 collective-permute-done.29.refs_7_
  71.9 0.3 down.1
  72.3 2.3 %collective-permute-start.30 = (bf16[32,256]{1,0:T(8,128)(2,1)S(1)}, bf16[32,256]{1,0:T(8,128)(2,1)S(1)}, u32[]{:S(2)}, u32[]{:S(2)}) collective-permute-start(bf16[32,256]{1,0:T(8,128)(2,1)S(1)} %get-tuple-element.165), channel_id=1, source_target_pairs={{0,3},{1,2},{2,1},{3,0},{4,7},{5,6},{6,5},{7,4},{8,11},{9,10},{10,... | collective-permute-start | bytes 49160 | tf_op jit(solution)/shard_map/ppermute | solution.py:66
  74.6 0.3 collective-permute-start.31
  74.8 1.0 %collective-permute-start.32 = (bf16[32,256]{1,0:T(8,128)(2,1)S(1)}, bf16[32,256]{1,0:T(8,128)(2,1)S(1)}, u32[]{:S(2)}, u32[]{:S(2)}) collective-permute-start(bf16[32,256]{1,0:T(8,128)(2,1)S(1)} %get-tuple-element.163), channel_id=1, source_target_pairs={{0,1},{1,0},{2,3},{3,2},{4,5},{5,4},{6,7},{7,6},{8,9},{9,8},{10,11... | collective-permute-start | bytes 49160 | tf_op jit(solution)/shard_map/ppermute | solution.py:66
  75.8 1.1 %collective-permute-done.30 = bf16[32,256]{1,0:T(8,128)(2,1)S(1)} collective-permute-done((bf16[32,256]{1,0:T(8,128)(2,1)S(1)}, bf16[32,256]{1,0:T(8,128)(2,1)S(1)}, u32[]{:S(2)}, u32[]{:S(2)}) %collective-permute-start.30) | collective-permute-done | bytes 16416 | tf_op jit(solution)/shard_map/ppermute | solution.py:66
  77.0 1.3 %collective-permute-done.31 = bf16[32,256]{1,0:T(8,128)(2,1)S(1)} collective-permute-done((bf16[32,256]{1,0:T(8,128)(2,1)S(1)}, bf16[32,256]{1,0:T(8,128)(2,1)S(1)}, u32[]{:S(2)}, u32[]{:S(2)}) %collective-permute-start.31) | collective-permute-done | bytes 16416 | tf_op jit(solution)/shard_map/ppermute | solution.py:66
  78.3 0.3 collective-permute-done.32
  78.6 0.6 reshape.107
  (58 shorter events, 0.7 us)
Async XLA Ops:
  0.6 11.9 %collective-permute-start.3 = (bf16[8,256,512]{2,1,0:T(8,128)(2,1)}, bf16[8,256,512]{2,1,0:T(8,128)(2,1)}, u32[]{:S(2)}, u32[]{:S(2)}) collective-permute-start(bf16[8,256,512]{2,1,0:T(8,128)(2,1)} %keys.1), channel_id=1, source_target_pairs={{0,4},{4,0},{8,12},{12,8},{16,20},{20,16},{24,28},{28,24},{1,5},{5... | collective-permute-start | bytes 6291464 | tf_op jit(solution)/shard_map/ppermute | solution.py:66
  1.2 11.4 %collective-permute-start.4 = (bf16[8,256,512]{2,1,0:T(8,128)(2,1)}, bf16[8,256,512]{2,1,0:T(8,128)(2,1)}, u32[]{:S(2)}, u32[]{:S(2)}) collective-permute-start(bf16[8,256,512]{2,1,0:T(8,128)(2,1)} %values.1), channel_id=1, source_target_pairs={{0,4},{4,0},{8,12},{12,8},{16,20},{20,16},{24,28},{28,24},{1,5},{5... | collective-permute-start | bytes 6291464 | tf_op jit(solution)/shard_map/ppermute | solution.py:66
  1.2 0.7 copy-start.8
  1.9 7.4 %copy-start.11 = (s32[8]{0:T(128)S(1)}, s32[8]{0:T(128)}, u32[]{:S(2)}) copy-start(s32[8]{0:T(128)} %param.19) | copy-start | bytes 100
  1.9 7.5 %copy-start.12 = (bf16[256]{0:T(256)(128)(2,1)S(1)}, bf16[256]{0:T(256)(128)(2,1)}, u32[]{:S(2)}) copy-start(bf16[256]{0:T(256)(128)(2,1)} %param.23) | copy-start | bytes 1540
  1.9 7.5 %copy-start.13 = (bf16[256]{0:T(256)(128)(2,1)S(1)}, bf16[256]{0:T(256)(128)(2,1)}, u32[]{:S(2)}) copy-start(bf16[256]{0:T(256)(128)(2,1)} %param.22) | copy-start | bytes 1540
  1.9 7.5 %copy-start.9 = (s32[8]{0:T(128)S(1)}, s32[8]{0:T(128)}, u32[]{:S(2)}) copy-start(s32[8]{0:T(128)} %starts.1) | copy-start | bytes 100
  1.9 7.5 %copy-start.10 = (s32[8]{0:T(128)S(1)}, s32[8]{0:T(128)}, u32[]{:S(2)}) copy-start(s32[8]{0:T(128)} %lens.1) | copy-start | bytes 100
  1.9 10.6 %copy-start = (bf16[256,3072]{1,0:T(8,128)(2,1)S(1)}, bf16[256,3072]{1,0:T(8,128)(2,1)}, u32[]{:S(2)}) copy-start(bf16[256,3072]{1,0:T(8,128)(2,1)} %weight.1) | copy-start | bytes 4718596
  4.5 10.2 %copy-start.1 = (bf16[256,2048]{1,0:T(8,128)(2,1)S(1)}, bf16[256,2048]{1,0:T(8,128)(2,1)}, u32[]{:S(2)}) copy-start(bf16[256,2048]{1,0:T(8,128)(2,1)} %own) | copy-start | bytes 3145732
  4.5 5.8 %collective-permute-start = (bf16[32,256]{1,0:T(8,128)(2,1)S(1)}, bf16[32,256]{1,0:T(8,128)(2,1)S(1)}, u32[]{:S(2)}, u32[]{:S(2)}) collective-permute-start(bf16[32,256]{1,0:T(8,128)(2,1)S(1)} %get-tuple-element.168), channel_id=1, source_target_pairs={{0,3},{1,2},{2,1},{3,0},{4,7},{5,6},{6,5},{7,4},{8,11},{9,10},{10,... | collective-permute-start | bytes 49160 | tf_op jit(solution)/shard_map/ppermute | solution.py:66
  8.6 3.7 %collective-permute-start.1 = (bf16[32,256]{1,0:T(8,128)(2,1)S(1)}, bf16[32,256]{1,0:T(8,128)(2,1)S(1)}, u32[]{:S(2)}, u32[]{:S(2)}) collective-permute-start(bf16[32,256]{1,0:T(8,128)(2,1)S(1)} %get-tuple-element.167), channel_id=1, source_target_pairs={{0,2},{1,3},{2,0},{3,1},{4,6},{5,7},{6,4},{7,5},{8,10},{9,11},{10,... | collective-permute-start | bytes 49160 | tf_op jit(solution)/shard_map/ppermute | solution.py:66
  8.8 3.7 %collective-permute-start.2 = (bf16[32,256]{1,0:T(8,128)(2,1)S(1)}, bf16[32,256]{1,0:T(8,128)(2,1)S(1)}, u32[]{:S(2)}, u32[]{:S(2)}) collective-permute-start(bf16[32,256]{1,0:T(8,128)(2,1)S(1)} %get-tuple-element.166), channel_id=1, source_target_pairs={{0,1},{1,0},{2,3},{3,2},{4,5},{5,4},{6,7},{7,6},{8,9},{9,8},{10,11... | collective-permute-start | bytes 49160 | tf_op jit(solution)/shard_map/ppermute | solution.py:66
  13.0 1.4 %collective-permute-start.5 = (bf16[32,2176]{1,0:T(8,128)(2,1)S(1)}, bf16[32,2176]{1,0:T(8,128)(2,1)S(1)}, u32[]{:S(2)}, u32[]{:S(2)}) collective-permute-start(bf16[32,2176]{1,0:T(8,128)(2,1)S(1)} %get-tuple-element.96), channel_id=1, source_target_pairs={{0,4},{4,0},{8,12},{12,8},{16,20},{20,16},{24,28},{28,24},{1,5},{5... | collective-permute-start | bytes 417800 | tf_op jit(solution)/shard_map/ppermute | solution.py:66
  14.5 13.5 %collective-permute-start.10 = (bf16[2048,256]{1,0:T(8,128)(2,1)}, bf16[2048,256]{1,0:T(8,128)(2,1)S(1)}, u32[]{:S(2)}, u32[]{:S(2)}) collective-permute-start(bf16[2048,256]{1,0:T(8,128)(2,1)} %o_own), channel_id=1, source_target_pairs={{0,4},{4,0},{8,12},{12,8},{16,20},{20,16},{24,28},{28,24},{1,5},{5... | collective-permute-start | bytes 3145736 | tf_op jit(solution)/shard_map/ppermute | solution.py:66
  14.7 13.3 %collective-permute-start.9 = (bf16[256,2048]{1,0:T(8,128)(2,1)S(1)}, bf16[256,2048]{1,0:T(8,128)(2,1)S(1)}, u32[]{:S(2)}, u32[]{:S(2)}) collective-permute-start(bf16[256,2048]{1,0:T(8,128)(2,1)S(1)} %copy-done.1), channel_id=1, source_target_pairs={{0,4},{4,0},{8,12},{12,8},{16,20},{20,16},{24,28},{28,24},{1,5},{5... | collective-permute-start | bytes 3145736 | tf_op jit(solution)/shard_map/ppermute | solution.py:66
  15.0 7.6 %collective-permute-start.6 = (bf16[32,1664]{1,0:T(8,128)(2,1)S(1)}, bf16[32,1664]{1,0:T(8,128)(2,1)S(1)}, u32[]{:S(2)}, u32[]{:S(2)}) collective-permute-start(bf16[32,1664]{1,0:T(8,128)(2,1)S(1)} %add.87.refs_0_), channel_id=1, source_target_pairs={{0,24},{4,28},{8,16},{12,20},{16,8},{20,12},{24,0},{28,4},{1,25},{... | collective-permute-start | bytes 319496 | tf_op jit(solution)/shard_map/ppermute | solution.py:66
  18.6 6.7 %collective-permute-start.7 = (bf16[32,1664]{1,0:T(8,128)(2,1)S(1)}, bf16[32,1664]{1,0:T(8,128)(2,1)S(1)}, u32[]{:S(2)}, u32[]{:S(2)}) collective-permute-start(bf16[32,1664]{1,0:T(8,128)(2,1)S(1)} %add.87.refs_0_), channel_id=1, source_target_pairs={{0,8},{4,12},{8,0},{12,4},{16,24},{20,28},{24,16},{28,20},{1,9},{5... | collective-permute-start | bytes 319496 | tf_op jit(solution)/shard_map/ppermute | solution.py:66
  18.6 9.3 %collective-permute-start.8 = (bf16[32,1664]{1,0:T(8,128)(2,1)S(1)}, bf16[32,1664]{1,0:T(8,128)(2,1)S(1)}, u32[]{:S(2)}, u32[]{:S(2)}) collective-permute-start(bf16[32,1664]{1,0:T(8,128)(2,1)S(1)} %add.87.refs_0_), channel_id=1, source_target_pairs={{0,16},{4,20},{8,24},{12,28},{16,0},{20,4},{24,8},{28,12},{1,17},{... | collective-permute-start | bytes 319496 | tf_op jit(solution)/shard_map/ppermute | solution.py:66
  27.9 1.7 %copy-start.3 = (bf16[256,2048]{1,0:T(8,128)(2,1)S(1)}, bf16[256,2048]{1,0:T(8,128)(2,1)}, u32[]{:S(2)}) copy-start(bf16[256,2048]{1,0:T(8,128)(2,1)} %own.1) | copy-start | bytes 3145732
  29.6 5.1 %copy-start.2 = (bf16[2048,256]{1,0:T(8,128)(2,1)S(1)}, bf16[2048,256]{1,0:T(8,128)(2,1)}, u32[]{:S(2)}) copy-start(bf16[2048,256]{1,0:T(8,128)(2,1)} %o_own) | copy-start | bytes 3145732
  29.6 9.7 %collective-permute-start.14 = (bf16[256,2048]{1,0:T(8,128)(2,1)S(1)}, bf16[256,2048]{1,0:T(8,128)(2,1)S(1)}, u32[]{:S(2)}, u32[]{:S(2)}) collective-permute-start(bf16[256,2048]{1,0:T(8,128)(2,1)S(1)} %copy-done.3), channel_id=1, source_target_pairs={{0,4},{4,0},{8,12},{12,8},{16,20},{20,16},{24,28},{28,24},{1,5},{5... | collective-permute-start | bytes 3145736 | tf_op jit(solution)/shard_map/ppermute | solution.py:66
  29.7 7.0 %collective-permute-start.11 = (bf16[32,1152]{1,0:T(8,128)(2,1)S(1)}, bf16[32,1152]{1,0:T(8,128)(2,1)S(1)}, u32[]{:S(2)}, u32[]{:S(2)}) collective-permute-start(bf16[32,1152]{1,0:T(8,128)(2,1)S(1)} %get-tuple-element.124.refs_0_), channel_id=1, source_target_pairs={{0,24},{4,28},{8,16},{12,20},{16,8},{20,12},{24,0},{28,4},{1,25},{... | collective-permute-start | bytes 221192 | tf_op jit(solution)/shard_map/ppermute | solution.py:66
  32.2 7.1 %collective-permute-start.12 = (bf16[32,1152]{1,0:T(8,128)(2,1)S(1)}, bf16[32,1152]{1,0:T(8,128)(2,1)S(1)}, u32[]{:S(2)}, u32[]{:S(2)}) collective-permute-start(bf16[32,1152]{1,0:T(8,128)(2,1)S(1)} %get-tuple-element.124.refs_0_), channel_id=1, source_target_pairs={{0,8},{4,12},{8,0},{12,4},{16,24},{20,28},{24,16},{28,20},{1,9},{5... | collective-permute-start | bytes 221192 | tf_op jit(solution)/shard_map/ppermute | solution.py:66
  32.2 7.1 %collective-permute-start.13 = (bf16[32,1152]{1,0:T(8,128)(2,1)S(1)}, bf16[32,1152]{1,0:T(8,128)(2,1)S(1)}, u32[]{:S(2)}, u32[]{:S(2)}) collective-permute-start(bf16[32,1152]{1,0:T(8,128)(2,1)S(1)} %get-tuple-element.124.refs_0_), channel_id=1, source_target_pairs={{0,16},{4,20},{8,24},{12,28},{16,0},{20,4},{24,8},{28,12},{1,17},{... | collective-permute-start | bytes 221192 | tf_op jit(solution)/shard_map/ppermute | solution.py:66
  34.7 4.7 %copy-start.7 = (bf16[128,1024]{1,0:T(8,128)(2,1)S(1)}, bf16[128,1024]{1,0:T(8,128)(2,1)}, u32[]{:S(2)}) copy-start(bf16[128,1024]{1,0:T(8,128)(2,1)} %constant.26.clone.spread) | copy-start | bytes 786436
  39.4 1.0 %copy-start.4 = (bf16[256,2048]{1,0:T(8,128)(2,1)}, bf16[256,2048]{1,0:T(8,128)(2,1)S(1)}, u32[]{:S(2)}) copy-start(bf16[256,2048]{1,0:T(8,128)(2,1)S(1)} %collective-permute-done.14.two) | copy-start | bytes 3145732
  40.3 1.3 %collective-permute-start.15 = (f32[32,512]{1,0:T(8,128)S(1)}, f32[32,512]{1,0:T(8,128)S(1)}, u32[]{:S(2)}, u32[]{:S(2)}) collective-permute-start(f32[32,512]{1,0:T(8,128)S(1)} %output.1), channel_id=1, source_target_pairs={{0,4},{4,0},{8,12},{12,8},{16,20},{20,16},{24,28},{28,24},{1,5},{5... | collective-permute-start | bytes 196616 | tf_op jit(solution)/shard_map/ppermute | solution.py:66
  41.6 5.3 %collective-permute-start.16 = (bf16[32,512]{1,0:T(8,128)(2,1)S(1)}, bf16[32,512]{1,0:T(8,128)(2,1)S(1)}, u32[]{:S(2)}, u32[]{:S(2)}) collective-permute-start(bf16[32,512]{1,0:T(8,128)(2,1)S(1)} %add_convert_fusion.refs_0_), channel_id=1, source_target_pairs={{0,3},{1,2},{2,1},{3,0},{4,7},{5,6},{6,5},{7,4},{8,11},{9,10},{10,... | collective-permute-start | bytes 98312 | tf_op jit(solution)/shard_map/ppermute | solution.py:66
  43.5 3.9 %collective-permute-start.17 = (bf16[32,512]{1,0:T(8,128)(2,1)S(1)}, bf16[32,512]{1,0:T(8,128)(2,1)S(1)}, u32[]{:S(2)}, u32[]{:S(2)}) collective-permute-start(bf16[32,512]{1,0:T(8,128)(2,1)S(1)} %add_convert_fusion.refs_0_), channel_id=1, source_target_pairs={{0,2},{1,3},{2,0},{3,1},{4,6},{5,7},{6,4},{7,5},{8,10},{9,11},{10,... | collective-permute-start | bytes 98312 | tf_op jit(solution)/shard_map/ppermute | solution.py:66
  43.8 3.9 %collective-permute-start.18 = (bf16[32,512]{1,0:T(8,128)(2,1)S(1)}, bf16[32,512]{1,0:T(8,128)(2,1)S(1)}, u32[]{:S(2)}, u32[]{:S(2)}) collective-permute-start(bf16[32,512]{1,0:T(8,128)(2,1)S(1)} %add_convert_fusion.refs_0_), channel_id=1, source_target_pairs={{0,1},{1,0},{2,3},{3,2},{4,5},{5,4},{6,7},{7,6},{8,9},{9,8},{10,11... | collective-permute-start | bytes 98312 | tf_op jit(solution)/shard_map/ppermute | solution.py:66
  45.2 1.2 %copy-start.5 = (bf16[256,2048]{1,0:T(8,128)(2,1)S(1)}, bf16[256,2048]{1,0:T(8,128)(2,1)}, u32[]{:S(2)}) copy-start(bf16[256,2048]{1,0:T(8,128)(2,1)} %copy-done.4) | copy-start | bytes 3145732
  46.9 25.0 %copy-start.6 = (bf16[2048,256]{1,0:T(8,128)(2,1)S(1)}, bf16[2048,256]{1,0:T(8,128)(2,1)}, u32[]{:S(2)}) copy-start(bf16[2048,256]{1,0:T(8,128)(2,1)} %w_down.1) | copy-start | bytes 3145732
  48.2 8.6 %collective-permute-start.19 = (bf16[32,2176]{1,0:T(8,128)(2,1)S(1)}, bf16[32,2176]{1,0:T(8,128)(2,1)S(1)}, u32[]{:S(2)}, u32[]{:S(2)}) collective-permute-start(bf16[32,2176]{1,0:T(8,128)(2,1)S(1)} %get-tuple-element.161), channel_id=1, source_target_pairs={{0,24},{4,28},{8,16},{12,20},{16,8},{20,12},{24,0},{28,4},{1,25},{... | collective-permute-start | bytes 417800 | tf_op jit(solution)/shard_map/ppermute | solution.py:66
  50.1 8.3 %collective-permute-start.20 = (bf16[32,2176]{1,0:T(8,128)(2,1)S(1)}, bf16[32,2176]{1,0:T(8,128)(2,1)S(1)}, u32[]{:S(2)}, u32[]{:S(2)}) collective-permute-start(bf16[32,2176]{1,0:T(8,128)(2,1)S(1)} %get-tuple-element.160), channel_id=1, source_target_pairs={{0,8},{4,12},{8,0},{12,4},{16,24},{20,28},{24,16},{28,20},{1,9},{5... | collective-permute-start | bytes 417800 | tf_op jit(solution)/shard_map/ppermute | solution.py:66
  50.5 11.5 %collective-permute-start.21 = (bf16[32,2176]{1,0:T(8,128)(2,1)S(1)}, bf16[32,2176]{1,0:T(8,128)(2,1)S(1)}, u32[]{:S(2)}, u32[]{:S(2)}) collective-permute-start(bf16[32,2176]{1,0:T(8,128)(2,1)S(1)} %get-tuple-element.159), channel_id=1, source_target_pairs={{0,16},{4,20},{8,24},{12,28},{16,0},{20,4},{24,8},{28,12},{1,17},{... | collective-permute-start | bytes 417800 | tf_op jit(solution)/shard_map/ppermute | solution.py:66
  52.7 1.2 %collective-permute-start.22 = (bf16[32,512]{1,0:T(8,128)(2,1)S(1)}, bf16[32,512]{1,0:T(8,128)(2,1)S(1)}, u32[]{:S(2)}, u32[]{:S(2)}) collective-permute-start(bf16[32,512]{1,0:T(8,128)(2,1)S(1)} %pad_maximum_fusion), channel_id=1, source_target_pairs={{0,4},{4,0},{8,12},{12,8},{16,20},{20,16},{24,28},{28,24},{1,5},{5... | collective-permute-start | bytes 98312 | tf_op jit(solution)/shard_map/ppermute | solution.py:66
  62.2 6.7 %collective-permute-start.23 = (bf16[32,1024]{1,0:T(8,128)(2,1)S(1)}, bf16[32,1024]{1,0:T(8,128)(2,1)S(1)}, u32[]{:S(2)}, u32[]{:S(2)}) collective-permute-start(bf16[32,1024]{1,0:T(8,128)(2,1)S(1)} %hidden.1.refs_0_), channel_id=1, source_target_pairs={{0,24},{4,28},{8,16},{12,20},{16,8},{20,12},{24,0},{28,4},{1,25},{... | collective-permute-start | bytes 196616 | tf_op jit(solution)/shard_map/ppermute | solution.py:66
  65.0 4.4 %collective-permute-start.24 = (bf16[32,1024]{1,0:T(8,128)(2,1)S(1)}, bf16[32,1024]{1,0:T(8,128)(2,1)S(1)}, u32[]{:S(2)}, u32[]{:S(2)}) collective-permute-start(bf16[32,1024]{1,0:T(8,128)(2,1)S(1)} %hidden.1.refs_0_), channel_id=1, source_target_pairs={{0,8},{4,12},{8,0},{12,4},{16,24},{20,28},{24,16},{28,20},{1,9},{5... | collective-permute-start | bytes 196616 | tf_op jit(solution)/shard_map/ppermute | solution.py:66
  65.0 5.2 %collective-permute-start.25 = (bf16[32,1024]{1,0:T(8,128)(2,1)S(1)}, bf16[32,1024]{1,0:T(8,128)(2,1)S(1)}, u32[]{:S(2)}, u32[]{:S(2)}) collective-permute-start(bf16[32,1024]{1,0:T(8,128)(2,1)S(1)} %hidden.1.refs_0_), channel_id=1, source_target_pairs={{0,16},{4,20},{8,24},{12,28},{16,0},{20,4},{24,8},{28,12},{1,17},{... | collective-permute-start | bytes 196616 | tf_op jit(solution)/shard_map/ppermute | solution.py:66
  66.7 4.0 %collective-permute-start.26 = (bf16[32,1024]{1,0:T(8,128)(2,1)S(1)}, bf16[32,1024]{1,0:T(8,128)(2,1)S(1)}, u32[]{:S(2)}, u32[]{:S(2)}) collective-permute-start(bf16[32,1024]{1,0:T(8,128)(2,1)S(1)} %hidden.1.refs_0_), channel_id=1, source_target_pairs={{0,4},{4,0},{8,12},{12,8},{16,20},{20,16},{24,28},{28,24},{1,5},{5... | collective-permute-start | bytes 196616 | tf_op jit(solution)/shard_map/ppermute | solution.py:66
  70.2 1.3 %collective-permute-start.27 = (bf16[32,1024]{1,0:T(8,128)(2,1)S(1)}, bf16[32,1024]{1,0:T(8,128)(2,1)S(1)}, u32[]{:S(2)}, u32[]{:S(2)}) collective-permute-start(bf16[32,1024]{1,0:T(8,128)(2,1)S(1)} %collective-permute-done.24.refs_1_), channel_id=1, source_target_pairs={{0,4},{4,0},{8,12},{12,8},{16,20},{20,16},{24,28},{28,24},{1,5},{5... | collective-permute-start | bytes 196616 | tf_op jit(solution)/shard_map/ppermute | solution.py:66
  70.2 1.4 %collective-permute-start.28 = (bf16[32,1024]{1,0:T(8,128)(2,1)S(1)}, bf16[32,1024]{1,0:T(8,128)(2,1)S(1)}, u32[]{:S(2)}, u32[]{:S(2)}) collective-permute-start(bf16[32,1024]{1,0:T(8,128)(2,1)S(1)} %collective-permute-done.25.refs_2_), channel_id=1, source_target_pairs={{0,4},{4,0},{8,12},{12,8},{16,20},{20,16},{24,28},{28,24},{1,5},{5... | collective-permute-start | bytes 196616 | tf_op jit(solution)/shard_map/ppermute | solution.py:66
  70.7 1.3 %collective-permute-start.29 = (bf16[32,1024]{1,0:T(8,128)(2,1)S(1)}, bf16[32,1024]{1,0:T(8,128)(2,1)S(1)}, u32[]{:S(2)}, u32[]{:S(2)}) collective-permute-start(bf16[32,1024]{1,0:T(8,128)(2,1)S(1)} %collective-permute-done.23.refs_3_), channel_id=1, source_target_pairs={{0,4},{4,0},{8,12},{12,8},{16,20},{20,16},{24,28},{28,24},{1,5},{5... | collective-permute-start | bytes 196616 | tf_op jit(solution)/shard_map/ppermute | solution.py:66
  72.3 4.7 %collective-permute-start.30 = (bf16[32,256]{1,0:T(8,128)(2,1)S(1)}, bf16[32,256]{1,0:T(8,128)(2,1)S(1)}, u32[]{:S(2)}, u32[]{:S(2)}) collective-permute-start(bf16[32,256]{1,0:T(8,128)(2,1)S(1)} %get-tuple-element.165), channel_id=1, source_target_pairs={{0,3},{1,2},{2,1},{3,0},{4,7},{5,6},{6,5},{7,4},{8,11},{9,10},{10,... | collective-permute-start | bytes 49160 | tf_op jit(solution)/shard_map/ppermute | solution.py:66
  74.6 3.7 %collective-permute-start.31 = (bf16[32,256]{1,0:T(8,128)(2,1)S(1)}, bf16[32,256]{1,0:T(8,128)(2,1)S(1)}, u32[]{:S(2)}, u32[]{:S(2)}) collective-permute-start(bf16[32,256]{1,0:T(8,128)(2,1)S(1)} %get-tuple-element.164), channel_id=1, source_target_pairs={{0,2},{1,3},{2,0},{3,1},{4,6},{5,7},{6,4},{7,5},{8,10},{9,11},{10,... | collective-permute-start | bytes 49160 | tf_op jit(solution)/shard_map/ppermute | solution.py:66
  74.8 3.7 %collective-permute-start.32 = (bf16[32,256]{1,0:T(8,128)(2,1)S(1)}, bf16[32,256]{1,0:T(8,128)(2,1)S(1)}, u32[]{:S(2)}, u32[]{:S(2)}) collective-permute-start(bf16[32,256]{1,0:T(8,128)(2,1)S(1)} %get-tuple-element.163), channel_id=1, source_target_pairs={{0,1},{1,0},{2,3},{3,2},{4,5},{5,4},{6,7},{7,6},{8,9},{9,8},{10,11... | collective-permute-start | bytes 49160 | tf_op jit(solution)/shard_map/ppermute | solution.py:66
